TPU v7x, 32 devices: a whole 2x2x4 slice. The times are simulated.
32 devices in a mesh: lon: 8 (over y, x, core), lat: 4 (over z).
Axes of the slice: x: 2, y: 2, z: 4, core: 2. Of those that a mesh axis runs over, the one named last changes fastest.
Arguments:
- state: float32 [16, 256, 1024], P(None, 'lat', 'lon'), may hold values from -6 to 6
- land_mask: int32 [256, 1024], P('lat', 'lon'), may hold values from 0 to 1, as said below
- kernel_one: bfloat16 [3, 3, 16, 16], replicated, may hold values from -0.5 to 0.5
- bias_one: float32 [16], replicated, may hold values from -3 to 3
- kernel_two: bfloat16 [3, 3, 16, 16], replicated, may hold values from -0.5 to 0.5
- bias_two: float32 [16], replicated, may hold values from -3 to 3
- kernel_three: bfloat16 [3, 3, 8, 16], replicated, may hold values from -0.5 to 0.5
- bias_three: float32 [8], replicated, may hold values from -3 to 3
Outputs:
- updated: float32 [16, 256, 1024], P(None, 'lat', 'lon')
Inputs may be any that keep to these rules, and one draw needn't show every extreme that they name: `land_mask`: 1 marks an ocean cell and 0 land; whole tiles of 64 x 128 cells may be land.
All inputs are finite; a program needn't handle non-finite values.
Results may differ from a plain program's by a relative error of at most 0.0003.
Values sent between devices are 32-bit elements; how exact they have to be, the bound alone decides.
No kernel may reach another device: no remote copies, remote signals or barrier semaphores. Data moves between devices by JAX's collectives and lax.ppermute only.
A program may use at most 128 MiB of HBM per device.

v0:
```python
import jax
import jax.numpy as jnp
from jax import lax
from jax.sharding import PartitionSpec as P


def padded_2(x, sides, width, wrap):
    for axis, dim in sides:
        size, length = (lax.axis_size(axis), x.shape[dim])
        up = [(i, (i + 1) % size) for i in range(size if wrap else size - 1)]
        down = [(j, i) for i, j in up]
        last = lax.slice_in_dim(x, length - width, length, axis=dim)
        leading = lax.slice_in_dim(x, 0, width, axis=dim)
        before = lax.ppermute(last, axis, up)
        after = lax.ppermute(leading, axis, down)
        x = jnp.concatenate([before, x, after], axis=dim)
    return x


def conv(x, kernel, bias):
    rows = x.shape[1] - 2
    cols = x.shape[2] - 2
    total = jnp.zeros((kernel.shape[2], rows, cols), jnp.float32) + bias[:, None, None]
    for a in range(3):
        for c in range(3):
            total = total + jnp.einsum(
                "ok,khw->ohw",
                kernel[a, c],
                x[:, a : a + rows, c : c + cols],
                preferred_element_type=jnp.float32,
            )
    return total


def fold_rows(state, wide):
    channels = state.shape[0]
    height = state.shape[1]
    flipped = wide[:, height - 3 :, :][:, ::-1, ::-1]
    count = lax.axis_size("lon")
    flat = flipped.reshape(count, flipped.size // count)
    mixed = lax.all_to_all(flat, "lon", split_axis=0, concat_axis=0, tiled=True)
    back = lax.all_to_all(mixed[::-1], "lon", split_axis=0, concat_axis=0, tiled=True)
    rows = back.reshape(flipped.shape)
    sign = jnp.where(jnp.arange(channels) < channels // 2, -1.0, 1.0).astype(jnp.float32)
    return rows * sign[:, None, None]


def step_tile(
    padded, state, ocean, kernel_one, bias_one, kernel_two, bias_two, kernel_three, bias_three
):
    channels = state.shape[0]
    levels = channels // 4
    layer_in = padded.astype(jnp.bfloat16)
    hidden_one = jax.nn.silu(conv(layer_in, kernel_one, bias_one)).astype(jnp.bfloat16)
    hidden_two = jax.nn.silu(conv(hidden_one, kernel_two, bias_two)).astype(jnp.bfloat16)
    forcing = conv(hidden_two, kernel_three, bias_three)
    centre = padded[:, 3:-3, 3:-3]
    east = padded[:, 3:-3, 4:-2]
    west = padded[:, 3:-3, 2:-4]
    north = padded[:, 4:-2, 3:-3]
    south_cells = padded[:, 2:-4, 3:-3]
    speed_u = jnp.tile(centre[0:levels], (4, 1, 1))
    speed_v = jnp.tile(centre[levels : 2 * levels], (4, 1, 1))
    tendency = -0.5 * (speed_u * (east - west) + speed_v * (north - south_cells))
    tendency = tendency + 0.2 * (east + west + north + south_cells - 4.0 * centre)
    extra = jnp.concatenate(
        [forcing, jnp.zeros((channels - forcing.shape[0],) + forcing.shape[1:], jnp.float32)],
        axis=0,
    )
    tendency = tendency + extra
    return state + 0.1 * ocean[None, :, :] * tendency


def shards(state, land_mask, kernel_one, bias_one, kernel_two, bias_two, kernel_three, bias_three):
    height = state.shape[1]
    at_top = lax.axis_index("lat") == lax.axis_size("lat") - 1
    widened = padded_2(state, (("lon", 2),), 3, True)
    tall = padded_2(widened, (("lat", 1),), 3, False)
    rows = fold_rows(state, widened)
    padded = jnp.concatenate(
        [tall[:, : height + 3], jnp.where(at_top, rows, tall[:, height + 3 :])], axis=1
    )
    ocean = land_mask.astype(jnp.float32)
    return step_tile(
        padded, state, ocean, kernel_one, bias_one, kernel_two, bias_two, kernel_three, bias_three
    )


def solution(mesh):
    return jax.shard_map(
        shards,
        mesh=mesh,
        in_specs=(P(None, "lat", "lon"), P("lat", "lon"), P(), P(), P(), P(), P(), P()),
        out_specs=P(None, "lat", "lon"),
        check_vma=False,
    )
```

profile of v0, /device:TPU:16, one launch (start us, length us, event | category | flops | bytes accessed | tf_op | source)
XLA Modules:
  0.0 90.5 jit_solution(7939866144419664401)
XLA Ops:
  0.0 1.3 %copy.137 = f32[16,64,128]{2,0,1:T(8,128)S(1)} copy(f32[16,64,128]{2,1,0:T(8,128)} %param.8) | data formatting | bytes 1048576 | tf_op args[0]
  1.6 1.9 %collective-permute-start = (f32[16,64,3]{2,0,1:T(8,128)S(1)}, f32[16,64,3]{2,0,1:T(8,128)S(1)}, u32[]{:S(2)}, u32[]{:S(2)}) collective-permute-start(f32[16,64,3]{2,0,1:T(8,128)S(1)} %get-tuple-element.32), channel_id=1, source_target_pairs={{4,0},{8,4},{12,8},{16,12},{20,16},{24,20},{28,24},{0,28},{5,1},{9... | collective-permute-start | bytes 36872 | tf_op jit(solution)/shard_map/ppermute | solution.py:15
  3.5 11.4 %collective-permute-done = f32[16,64,3]{2,0,1:T(8,128)S(1)} collective-permute-done((f32[16,64,3]{2,0,1:T(8,128)S(1)}, f32[16,64,3]{2,0,1:T(8,128)S(1)}, u32[]{:S(2)}, u32[]{:S(2)}) %collective-permute-start) | collective-permute-done | bytes 12320 | tf_op jit(solution)/shard_map/ppermute | solution.py:15
  14.9 1.9 %collective-permute-done.1 = f32[16,64,3]{2,0,1:T(8,128)S(1)} collective-permute-done((f32[16,64,3]{2,0,1:T(8,128)S(1)}, f32[16,64,3]{2,0,1:T(8,128)S(1)}, u32[]{:S(2)}, u32[]{:S(2)}) %collective-permute-start.1) | collective-permute-done | bytes 12320 | tf_op jit(solution)/shard_map/ppermute | solution.py:14
  16.8 0.5 fusion.67
  17.9 0.7 all_to_all.19
  18.7 3.3 %all-to-all-start = ((f32[8,1,804]{2,1,0:T(1,128)}), f32[8,1,804]{2,1,0:T(1,128)S(1)}, u32[]{:S(2)}, u32[]{:S(2)}) async-start(f32[8,1,804]{2,1,0:T(1,128)} %all_to_all.19), calls=%async_computation | async-start | bytes 57344 | tf_op jit(solution)/shard_map/all_to_all | solution.py:41
  22.0 0.6 convert_multiply_fusion
  22.6 3.5 %collective-permute-start.3 = (f32[16,3,134]{2,0,1:T(8,128)S(1)}, f32[16,3,134]{2,0,1:T(8,128)S(1)}, u32[]{:S(2)}, u32[]{:S(2)}) collective-permute-start(f32[16,3,134]{2,0,1:T(8,128)S(1)} %get-tuple-element.9), channel_id=1, source_target_pairs={{0,1},{1,2},{2,3},{4,5},{5,6},{6,7},{8,9},{9,10},{10,11},{12,13},{... | collective-permute-start | bytes 77192 | tf_op jit(solution)/shard_map/ppermute | solution.py:14
  26.1 2.4 %collective-permute-start.2 = (f32[16,3,134]{2,0,1:T(8,128)S(1)}, f32[16,3,134]{2,0,1:T(8,128)S(1)}, u32[]{:S(2)}, u32[]{:S(2)}) collective-permute-start(f32[16,3,134]{2,0,1:T(8,128)S(1)} %get-tuple-element.10), channel_id=1, source_target_pairs={{1,0},{2,1},{3,2},{5,4},{6,5},{7,6},{9,8},{10,9},{11,10},{13,12},{... | collective-permute-start | bytes 77192 | tf_op jit(solution)/shard_map/ppermute | solution.py:15
  28.7 0.6 copy.116
  29.3 4.1 %all-to-all-start.1 = ((f32[8,1,804]{2,1,0:T(1,128)}), f32[8,1,804]{2,1,0:T(1,128)S(1)}, u32[]{:S(2)}, u32[]{:S(2)}) async-start(f32[8,1,804]{2,1,0:T(1,128)} %copy.116), calls=%async_computation.1 | async-start | bytes 57344 | tf_op jit(solution)/shard_map/all_to_all | solution.py:42
  33.5 0.7 copy.112
  34.3 4.0 %all-to-all-done.1 = f32[8,1,804]{2,1,0:T(1,128)S(1)} async-done(((f32[8,1,804]{2,1,0:T(1,128)}), f32[8,1,804]{2,1,0:T(1,128)S(1)}, u32[]{:S(2)}, u32[]{:S(2)}) %all-to-all-start.1) | async-done | bytes 25760 | tf_op jit(solution)/shard_map/all_to_all | solution.py:42
  38.5 0.7 fusion.68
  39.3 2.4 %fusion.71 = (bf16[16,68,132]{2,0,1:T(8,128)(2,1)S(1)}, bf16[16,68,132]{2,0,1:T(8,128)(2,1)S(1)}, bf16[16,68,132]{2,0,1:T(8,128)(2,1)S(1)}, bf16[16,68,132]{2,0,...) fusion(bf16[16,70,134]{2,0,1:T(8,128)(2,1)S(1)} %pad_maximum_fu, ...), kind=kLoop, calls=%fused_computation.114 | loop fusion | bytes 5170176 | tf_op jit(solution)/shard_map/slice | solution.py:29
  41.7 2.8 %copy.119 = bf16[16,68,132]{1,0,2:T(8,128)(2,1)} copy(bf16[16,68,132]{2,0,1:T(8,128)(2,1)} %get-tuple-element.19) | data formatting | bytes 574464 | tf_op jit(solution)/shard_map/slice | solution.py:29
  44.5 2.8 %copy.120 = bf16[16,68,132]{1,0,2:T(8,128)(2,1)} copy(bf16[16,68,132]{2,0,1:T(8,128)(2,1)} %get-tuple-element.18) | data formatting | bytes 574464 | tf_op jit(solution)/shard_map/slice | solution.py:29
  47.3 2.8 %copy.121 = bf16[16,68,132]{1,0,2:T(8,128)(2,1)} copy(bf16[16,68,132]{2,0,1:T(8,128)(2,1)} %get-tuple-element.17) | data formatting | bytes 574464 | tf_op jit(solution)/shard_map/slice | solution.py:29
  50.1 2.8 %copy.122 = bf16[16,68,132]{1,0,2:T(8,128)(2,1)} copy(bf16[16,68,132]{2,0,1:T(8,128)(2,1)} %get-tuple-element.16) | data formatting | bytes 574464 | tf_op jit(solution)/shard_map/slice | solution.py:29
  52.9 1.7 %copy.123 = bf16[16,68,132]{1,0,2:T(8,128)(2,1)} copy(bf16[16,68,132]{2,0,1:T(8,128)(2,1)S(1)} %get-tuple-element.15) | data formatting | bytes 574464 | tf_op jit(solution)/shard_map/slice | solution.py:29
  54.7 1.7 %copy.124 = bf16[16,68,132]{1,0,2:T(8,128)(2,1)} copy(bf16[16,68,132]{2,0,1:T(8,128)(2,1)S(1)} %get-tuple-element.14) | data formatting | bytes 574464 | tf_op jit(solution)/shard_map/slice | solution.py:29
  56.4 1.0 %copy.125 = bf16[16,68,132]{1,0,2:T(8,128)(2,1)S(1)} copy(bf16[16,68,132]{2,0,1:T(8,128)(2,1)S(1)} %get-tuple-element.13) | data formatting | bytes 574464 | tf_op jit(solution)/shard_map/slice | solution.py:29
  57.4 1.0 %copy.126 = bf16[16,68,132]{1,0,2:T(8,128)(2,1)S(1)} copy(bf16[16,68,132]{2,0,1:T(8,128)(2,1)S(1)} %get-tuple-element.12) | data formatting | bytes 574464 | tf_op jit(solution)/shard_map/slice | solution.py:29
  58.4 1.0 %copy.127 = bf16[16,68,132]{1,0,2:T(8,128)(2,1)S(1)} copy(bf16[16,68,132]{2,0,1:T(8,128)(2,1)S(1)} %get-tuple-element.11) | data formatting | bytes 574464 | tf_op jit(solution)/shard_map/slice | solution.py:29
  59.7 0.8 copy-done.5
  60.8 0.8 copy-done.4
  61.8 0.8 copy-done.3
  62.9 0.8 copy-done.2
  63.9 0.8 copy-done.1
  65.6 0.6 multiply_convert_fusion
  69.0 0.5 multiply_convert_fusion.1
  69.5 2.2 %fusion.72 = (bf16[16,64,128]{1,0,2:T(8,128)(2,1)S(1)}, bf16[16,64,128]{1,0,2:T(8,128)(2,1)S(1)}, bf16[16,64,128]{1,0,2:T(8,128)(2,1)S(1)}, bf16[16,64,128]{1,0,...) fusion(bf16[16,66,130]{1,0,2:T(8,128)(2,1)S(1)} %multiply_conve, ...), kind=kLoop, calls=%fused_computation.115 | loop fusion | bytes 4718592 | tf_op jit(solution)/shard_map/slice | solution.py:29
  71.7 2.3 %copy.128 = bf16[16,64,128]{2,0,1:T(8,128)(2,1)} copy(bf16[16,64,128]{1,0,2:T(8,128)(2,1)} %get-tuple-element.28) | data formatting | bytes 524288 | tf_op jit(solution)/shard_map/slice | solution.py:29
  74.0 2.3 %copy.129 = bf16[16,64,128]{2,0,1:T(8,128)(2,1)} copy(bf16[16,64,128]{1,0,2:T(8,128)(2,1)} %get-tuple-element.27) | data formatting | bytes 524288 | tf_op jit(solution)/shard_map/slice | solution.py:29
  76.3 2.3 %copy.130 = bf16[16,64,128]{2,0,1:T(8,128)(2,1)} copy(bf16[16,64,128]{1,0,2:T(8,128)(2,1)} %get-tuple-element.26) | data formatting | bytes 524288 | tf_op jit(solution)/shard_map/slice | solution.py:29
  78.6 2.3 %copy.131 = bf16[16,64,128]{2,0,1:T(8,128)(2,1)} copy(bf16[16,64,128]{1,0,2:T(8,128)(2,1)} %get-tuple-element.25) | data formatting | bytes 524288 | tf_op jit(solution)/shard_map/slice | solution.py:29
  80.9 0.6 copy.132
  81.5 0.6 copy.133
  82.1 0.6 copy.134
  82.7 0.6 copy.135
  83.3 0.6 copy.136
  83.9 0.9 convolution_add_fusion.26
  84.8 0.8 convolution_add_fusion.25
  85.7 0.8 convolution_add_fusion.24
  87.7 0.4 copy-done.15
  88.6 0.9 multiply_add_fusion
  89.5 1.0 %copy.138 = f32[16,64,128]{2,1,0:T(8,128)} copy(f32[16,64,128]{2,0,1:T(8,128)S(1)} %multiply_add_fusion) | data formatting | bytes 1048576 | tf_op jit(solution)/shard_map/add | solution.py:71
  (90 shorter events, 8.0 us)
Async XLA Ops:
  1.4 2.2 %copy-start.10 = (f32[16,64,128]{2,1,0:T(8,128)S(1)}, f32[16,64,128]{2,1,0:T(8,128)}, u32[]{:S(2)}) copy-start(f32[16,64,128]{2,1,0:T(8,128)} %param.8) | copy-start | bytes 1572868
  1.6 13.4 %collective-permute-start = (f32[16,64,3]{2,0,1:T(8,128)S(1)}, f32[16,64,3]{2,0,1:T(8,128)S(1)}, u32[]{:S(2)}, u32[]{:S(2)}) collective-permute-start(f32[16,64,3]{2,0,1:T(8,128)S(1)} %get-tuple-element.32), channel_id=1, source_target_pairs={{4,0},{8,4},{12,8},{16,12},{20,16},{24,20},{28,24},{0,28},{5,1},{9... | collective-permute-start | bytes 36872 | tf_op jit(solution)/shard_map/ppermute | solution.py:15
  3.5 13.3 %collective-permute-start.1 = (f32[16,64,3]{2,0,1:T(8,128)S(1)}, f32[16,64,3]{2,0,1:T(8,128)S(1)}, u32[]{:S(2)}, u32[]{:S(2)}) collective-permute-start(f32[16,64,3]{2,0,1:T(8,128)S(1)} %get-tuple-element.31), channel_id=1, source_target_pairs={{0,4},{4,8},{8,12},{12,16},{16,20},{20,24},{24,28},{28,0},{1,5},{5... | collective-permute-start | bytes 36872 | tf_op jit(solution)/shard_map/ppermute | solution.py:14
  3.5 18.5 %copy-start.20 = (s32[64,128]{1,0:T(8,128)S(1)}, s32[64,128]{1,0:T(8,128)}, u32[]{:S(2)}) copy-start(s32[64,128]{1,0:T(8,128)} %param.9) | copy-start | bytes 98308
  14.9 2.4 %copy-start.6 = (f32[16,64,3]{2,0,1:T(8,128)}, f32[16,64,3]{2,0,1:T(8,128)S(1)}, u32[]{:S(2)}) copy-start(f32[16,64,3]{2,0,1:T(8,128)S(1)} %collective-permute-done) | copy-start | bytes 36868
  16.8 0.8 copy-start.8
  18.7 9.8 %all-to-all-start = ((f32[8,1,804]{2,1,0:T(1,128)}), f32[8,1,804]{2,1,0:T(1,128)S(1)}, u32[]{:S(2)}, u32[]{:S(2)}) async-start(f32[8,1,804]{2,1,0:T(1,128)} %all_to_all.19), calls=%async_computation | async-start | bytes 57344 | tf_op jit(solution)/shard_map/all_to_all | solution.py:41
  22.6 11.6 %collective-permute-start.3 = (f32[16,3,134]{2,0,1:T(8,128)S(1)}, f32[16,3,134]{2,0,1:T(8,128)S(1)}, u32[]{:S(2)}, u32[]{:S(2)}) collective-permute-start(f32[16,3,134]{2,0,1:T(8,128)S(1)} %get-tuple-element.9), channel_id=1, source_target_pairs={{0,1},{1,2},{2,3},{4,5},{5,6},{6,7},{8,9},{9,10},{10,11},{12,13},{... | collective-permute-start | bytes 77192 | tf_op jit(solution)/shard_map/ppermute | solution.py:14
  26.1 12.3 %collective-permute-start.2 = (f32[16,3,134]{2,0,1:T(8,128)S(1)}, f32[16,3,134]{2,0,1:T(8,128)S(1)}, u32[]{:S(2)}, u32[]{:S(2)}) collective-permute-start(f32[16,3,134]{2,0,1:T(8,128)S(1)} %get-tuple-element.10), channel_id=1, source_target_pairs={{1,0},{2,1},{3,2},{5,4},{6,5},{7,6},{9,8},{10,9},{11,10},{13,12},{... | collective-permute-start | bytes 77192 | tf_op jit(solution)/shard_map/ppermute | solution.py:15
  29.3 8.9 %all-to-all-start.1 = ((f32[8,1,804]{2,1,0:T(1,128)}), f32[8,1,804]{2,1,0:T(1,128)S(1)}, u32[]{:S(2)}, u32[]{:S(2)}) async-start(f32[8,1,804]{2,1,0:T(1,128)} %copy.116), calls=%async_computation.1 | async-start | bytes 57344 | tf_op jit(solution)/shard_map/all_to_all | solution.py:42
  34.3 4.9 %copy-start.16 = (f32[16,3,134]{2,0,1:T(8,128)}, f32[16,3,134]{2,0,1:T(8,128)S(1)}, u32[]{:S(2)}) copy-start(f32[16,3,134]{2,0,1:T(8,128)S(1)} %collective-permute-done.3) | copy-start | bytes 77188
  57.4 2.0 %copy-start = (bf16[16,68,132]{1,0,2:T(8,128)(2,1)S(1)}, bf16[16,68,132]{1,0,2:T(8,128)(2,1)}, u32[]{:S(2)}) copy-start(bf16[16,68,132]{1,0,2:T(8,128)(2,1)} %copy.119) | copy-start | bytes 861700
  57.4 2.0 %copy-start.21 = (bf16[3,3,16,16]{3,2,1,0:T(8,128)(2,1)S(1)}, bf16[3,3,16,16]{3,2,1,0:T(8,128)(2,1)}, u32[]{:S(2)}) copy-start(bf16[3,3,16,16]{3,2,1,0:T(8,128)(2,1)} %param.10) | copy-start | bytes 13828
  57.4 2.0 %copy-start.24 = (f32[16]{0:T(128)S(1)}, f32[16]{0:T(128)}, u32[]{:S(2)}) copy-start(f32[16]{0:T(128)} %param.11) | copy-start | bytes 196
  59.4 1.0 %copy-start.5 = (bf16[16,68,132]{1,0,2:T(8,128)(2,1)S(1)}, bf16[16,68,132]{1,0,2:T(8,128)(2,1)}, u32[]{:S(2)}) copy-start(bf16[16,68,132]{1,0,2:T(8,128)(2,1)} %copy.120) | copy-start | bytes 861700
  60.5 1.0 %copy-start.4 = (bf16[16,68,132]{1,0,2:T(8,128)(2,1)S(1)}, bf16[16,68,132]{1,0,2:T(8,128)(2,1)}, u32[]{:S(2)}) copy-start(bf16[16,68,132]{1,0,2:T(8,128)(2,1)} %copy.121) | copy-start | bytes 861700
  61.5 1.0 %copy-start.3 = (bf16[16,68,132]{1,0,2:T(8,128)(2,1)S(1)}, bf16[16,68,132]{1,0,2:T(8,128)(2,1)}, u32[]{:S(2)}) copy-start(bf16[16,68,132]{1,0,2:T(8,128)(2,1)} %copy.122) | copy-start | bytes 861700
  62.6 1.0 %copy-start.2 = (bf16[16,68,132]{1,0,2:T(8,128)(2,1)S(1)}, bf16[16,68,132]{1,0,2:T(8,128)(2,1)}, u32[]{:S(2)}) copy-start(bf16[16,68,132]{1,0,2:T(8,128)(2,1)} %copy.123) | copy-start | bytes 861700
  63.6 1.0 %copy-start.1 = (bf16[16,68,132]{1,0,2:T(8,128)(2,1)S(1)}, bf16[16,68,132]{1,0,2:T(8,128)(2,1)}, u32[]{:S(2)}) copy-start(bf16[16,68,132]{1,0,2:T(8,128)(2,1)} %copy.124) | copy-start | bytes 861700
  65.5 0.8 copy-start.22
  65.6 0.8 copy-start.25
  82.0 1.8 %copy-start.14 = (bf16[16,64,128]{2,0,1:T(8,128)(2,1)S(1)}, bf16[16,64,128]{2,0,1:T(8,128)(2,1)}, u32[]{:S(2)}) copy-start(bf16[16,64,128]{2,0,1:T(8,128)(2,1)} %copy.128) | copy-start | bytes 786436
  82.1 1.8 %copy-start.26 = (f32[8]{0:T(128)S(1)}, f32[8]{0:T(128)}, u32[]{:S(2)}) copy-start(f32[8]{0:T(128)} %param.15) | copy-start | bytes 100
  82.7 2.2 %copy-start.13 = (bf16[16,64,128]{2,0,1:T(8,128)(2,1)S(1)}, bf16[16,64,128]{2,0,1:T(8,128)(2,1)}, u32[]{:S(2)}) copy-start(bf16[16,64,128]{2,0,1:T(8,128)(2,1)} %copy.129) | copy-start | bytes 786436
  83.3 2.4 %copy-start.12 = (bf16[16,64,128]{2,0,1:T(8,128)(2,1)S(1)}, bf16[16,64,128]{2,0,1:T(8,128)(2,1)}, u32[]{:S(2)}) copy-start(bf16[16,64,128]{2,0,1:T(8,128)(2,1)} %copy.130) | copy-start | bytes 786436
  83.9 2.7 %copy-start.11 = (bf16[16,64,128]{2,0,1:T(8,128)(2,1)S(1)}, bf16[16,64,128]{2,0,1:T(8,128)(2,1)}, u32[]{:S(2)}) copy-start(bf16[16,64,128]{2,0,1:T(8,128)(2,1)} %copy.131) | copy-start | bytes 786436
  83.9 2.7 %copy-start.23 = (bf16[3,3,8,16]{3,2,1,0:T(8,128)(2,1)S(1)}, bf16[3,3,8,16]{3,2,1,0:T(8,128)(2,1)}, u32[]{:S(2)}) copy-start(bf16[3,3,8,16]{3,2,1,0:T(8,128)(2,1)} %param.14) | copy-start | bytes 6916
  87.2 0.9 %copy-start.15 = (f32[4,64,128]{2,0,1:T(4,128)S(1)}, f32[4,64,128]{2,0,1:T(4,128)}, u32[]{:S(2)}) copy-start(f32[4,64,128]{2,0,1:T(4,128)} %copy.112) | copy-start | bytes 393220
  87.4 1.1 %copy-start.7 = (f32[16,64,3]{2,0,1:T(8,128)S(1)}, f32[16,64,3]{2,0,1:T(8,128)}, u32[]{:S(2)}) copy-start(f32[16,64,3]{2,0,1:T(8,128)} %copy-done.6) | copy-start | bytes 36868
  87.4 1.2 %copy-start.9 = (f32[16,64,3]{2,0,1:T(8,128)S(1)}, f32[16,64,3]{2,0,1:T(8,128)}, u32[]{:S(2)}) copy-start(f32[16,64,3]{2,0,1:T(8,128)} %copy-done.8) | copy-start | bytes 36868
  87.4 1.2 %copy-start.17 = (f32[16,3,134]{2,0,1:T(8,128)S(1)}, f32[16,3,134]{2,0,1:T(8,128)}, u32[]{:S(2)}) copy-start(f32[16,3,134]{2,0,1:T(8,128)} %copy-done.16) | copy-start | bytes 77188
  87.4 1.2 %copy-start.18 = (f32[16,3,134]{2,0,1:T(8,128)S(1)}, f32[16,3,134]{2,0,1:T(8,128)}, u32[]{:S(2)}) copy-start(f32[16,3,134]{2,0,1:T(8,128)} %get-tuple-element.8) | copy-start | bytes 77188
  87.4 1.2 %copy-start.19 = (f32[64,128]{1,0:T(8,128)S(1)}, f32[64,128]{1,0:T(8,128)}, u32[]{:S(2)}) copy-start(f32[64,128]{1,0:T(8,128)} %convert_multiply_fusion) | copy-start | bytes 98308
where the time goes:
time: 92 us; the launch traced here: 90.5 us
  local copies, waits for them, and re-layouts  45 us (49%)
  waiting for transfers between devices  17.3 us (19%)
  starting transfers between devices  15.2 us (17%)
  matrix products  9.5 us (10%)
  other arithmetic  2.85 us (3%)
    slice x20, local copies, waits for them, and re-layouts, conv(): x[:, a:a + rows, c:c + cols]  34.4 us
    ppermute x2, waiting for transfers between devices, padded_2(): after = lax.ppermute(leading, axis, down)  11.4 us
    dot_general x27, matrix products, conv(): jnp.einsum('ok,khw->ohw', kernel[a, c], x[:, a:a + rows, c:c + cols], pre...  9.5 us
    unnamed x58, local copies, waits for them, and re-layouts  6.78 us
    ppermute x2, starting transfers between devices, padded_2(): after = lax.ppermute(leading, axis, down)  4.29 us
    all_to_all x1, starting transfers between devices, fold_rows(): lax.all_to_all(mixed[::-1], 'lon', split_axis=0, concat_axis=0, tiled=True)  4.12 us
    all_to_all x1, waiting for transfers between devices, fold_rows(): lax.all_to_all(mixed[::-1], 'lon', split_axis=0, concat_axis=0, tiled=True)  3.96 us
    ppermute x2, starting transfers between devices, padded_2(): before = lax.ppermute(last, axis, up)  3.48 us
  transfers between devices with their start and end apart: 6, of which 3 were waited for; matrix products, arithmetic and copies ran while one was open for 3% of the time, Pallas kernels for 0%

commit v1 on v0

v1 whole, which is shorter than its diff:
```python
import functools

import jax
import jax.numpy as jnp
from jax import lax
from jax.experimental import pallas as pl
from jax.experimental.pallas import tpu as pltpu
from jax.sharding import PartitionSpec as P

F32 = jnp.float32
BF16 = jnp.bfloat16

ROWS = 64
PITCH = 72
BLOCK = 8
DEPTH = 512
SPAN = (BLOCK + 2) * 16
VMEM = pl.BlockSpec(memory_space=pltpu.VMEM)
HBM = pl.BlockSpec(memory_space=pltpu.HBM)
LIMIT = 40 * 2**20


def lanes():
    return lax.broadcasted_iota(jnp.int32, (8, 128), 1)


def turn(x, by):
    if isinstance(by, int):
        by = by % 128
        if by == 0:
            return x
    return pltpu.roll(x, by, x.ndim - 1)


def silu(v):
    half = 0.5 * v
    return half + half * jnp.tanh(half)


def dot(weights, x):
    return jnp.dot(weights, x, preferred_element_type=F32)


def even_place(axis):
    return lax.rem(lax.axis_index(axis), 2) == 0


def sides(inner, outer):
    even = even_place("lon")
    return (
        [jnp.where(even, inner[i], outer[i]) for i in range(4)],
        [jnp.where(even, outer[i], inner[i]) for i in range(4)],
    )


def tendency(q, north, south, east, west):
    sub = lax.broadcasted_iota(jnp.int32, (8, 128), 0)
    swapped = pltpu.roll(q[0], 4, 0)
    u = jnp.where(sub < 4, q[0], swapped)
    v = jnp.where(sub < 4, swapped, q[0])
    result = []
    for e, w, n, s, x in zip(east, west, north, south, q):
        total = -0.5 * (u * (e - w) + v * (n - s))
        result.append(total + 0.2 * (e + w + n + s - 4.0 * x))
    return result


def beside(e, e_at, w, w_at):
    return jnp.where(lanes() < 64, turn(e, -e_at), turn(w, 125 - w_at))


def turn_wide(x, c):
    return pltpu.roll(x, (1 - c) % 256, 1) if c != 1 else x


def spread(rows, width):
    blank = jnp.zeros((16, 2 * width), BF16)
    result = []
    for c in range(3):
        for row in rows:
            parts = [turn_wide(row[:, at : at + 256], c)[:, 0:width] for at in (0, 256)]
            result.append(jnp.concatenate(parts, axis=1))
        result.extend([blank] * ((BLOCK + 2 if c < 2 else BLOCK + 4) - len(rows)))
    return jnp.concatenate(result, axis=0)


def prepare_kernel(state_ref, *refs):
    others, refs = refs[0:7], refs[7:]
    rows_ref, strip_ref, outer_ref, inner_ref, *held, cells_ref, sems = refs
    fetches = []
    for at in range(0, 16, 2):
        span = pl.ds(at, 2)
        target = cells_ref.at[span, pl.ds(0, ROWS), :]
        fetches.append(pltpu.make_async_copy(state_ref.at[span], target, sems.at[len(fetches)]))
    for source, target in zip(others, held):
        fetches.append(pltpu.make_async_copy(source, target, sems.at[len(fetches)]))
    for fetch in fetches:
        fetch.start()

    flat = cells_ref.reshape(16 * PITCH, 128)
    group = lanes() // 16
    part = (lanes() % 16) // 4
    even = even_place("lon")
    shifts = [
        [jnp.where(even, (4 * s - a) % 128, (4 * s - b) % 128) for s in range(4)]
        for a, b in ((6, 3), (3, 6))
    ]
    for fetch in fetches[0:8]:
        fetch.wait()
    for half in range(2):
        strip = [jnp.zeros((8, 128), F32)] * 8
        for b in range(8):
            for r in range(8):
                x = flat[pl.ds(8 * PITCH * half + 8 * b + r, 8, stride=PITCH), :]
                rows_ref[8 * b + r, half] = x
                strip[r] = jnp.where(group == b, turn(x, 6 + 16 * b), strip[r])
        for r in range(8):
            strip_ref[r, half] = strip[r]
        for target, shift in zip((outer_ref, inner_ref), shifts):
            for q in range(2):
                value = jnp.zeros((8, 128), F32)
                for s in range(4):
                    value = jnp.where(part == s, turn(strip[4 * q + s], shift[s]), value)
                target[2 * q + half] = value
    for fetch in fetches[8:]:
        fetch.wait()


def prepare(state, others):
    block = jax.ShapeDtypeStruct
    arrays = [pltpu.with_memory_space_constraint(x, pltpu.HBM) for x in (state, *others)]
    return pl.pallas_call(
        prepare_kernel,
        out_shape=[
            block((ROWS, 2, 8, 128), F32),
            block((8, 2, 8, 128), F32),
            block((4, 8, 128), F32),
            block((4, 8, 128), F32),
            *[block(x.shape, x.dtype) for x in others],
        ],
        in_specs=[HBM] * 8,
        out_specs=[VMEM] * 11,
        scratch_shapes=[pltpu.VMEM((16, PITCH, 128), F32), pltpu.SemaphoreType.DMA((15,))],
        compiler_params=pltpu.CompilerParams(vmem_limit_bytes=LIMIT),
        cost_estimate=pl.CostEstimate(flops=400000, bytes_accessed=1200000, transcendentals=0),
        name="rows_edges",
    )(*arrays)


def corners_kernel(size, rows_ref, outer_ref, inner_ref, north_ref, first_ref, second_ref):
    lat = lax.axis_index("lat")
    even = lax.rem(lat, 2) == 0
    for t in range(3):
        for half in range(2):
            at = 2 * t + half
            low = rows_ref[t, half]
            first_ref[at] = jnp.where(even, north_ref[at], low)
            second_ref[at] = jnp.where(even, low, north_ref[at])
    top = lat == size - 1
    col = lanes()
    part = col // 16
    straight = even_place("lon")
    mirrored = straight != top
    index = jnp.where(top, 112 + 4 * (3 - col // 4 % 4) + 2 - col % 4, 112 + col % 16)
    low = high = jnp.zeros((8, 128), F32)
    for i in range(4):
        half = i // 2
        pair = (inner_ref, outer_ref) if i % 2 == 0 else (outer_ref, inner_ref)
        x = jnp.where(straight, pair[0][half], pair[1][half])
        low = jnp.where(part == i, turn(x, 16 * i), low)
        x = jnp.where(mirrored, pair[0][2 + half], pair[1][2 + half])
        high = jnp.where(part == i, jnp.take_along_axis(x, index, axis=1), high)
    high = jnp.where(top & (col < 32), -high, high)
    first_ref[6] = jnp.where(even, high, low)
    second_ref[6] = jnp.where(even, low, high)


def corners(size, rows, inner, outer, north):
    return pl.pallas_call(
        functools.partial(corners_kernel, size),
        out_shape=[jax.ShapeDtypeStruct((7, 8, 128), F32)] * 2,
        in_specs=[VMEM] * 4,
        out_specs=[VMEM] * 2,
        compiler_params=pltpu.CompilerParams(vmem_limit_bytes=LIMIT),
        cost_estimate=pl.CostEstimate(flops=1000, bytes_accessed=100000, transcendentals=0),
        name="add_corners",
    )(rows, outer, inner, north)


def band(kernel_ref, wide_ref, target_ref):
    n = kernel_ref.shape[2]
    wide_ref[...] = jnp.zeros_like(wide_ref)
    tiles = [None] * (DEPTH // 128)
    for c in range(3):
        for a in range(3):
            wide_ref[3 * c + a, :, 0:16] = kernel_ref[a, c].astype(wide_ref.dtype)
            tile, off = divmod(SPAN * c + 16 * a, 128)
            x = turn(wide_ref[3 * c + a], off)
            tiles[tile] = x if tiles[tile] is None else tiles[tile] + x
    blank = jnp.zeros((n, 128), wide_ref.dtype)
    first = jnp.concatenate([blank if x is None else x for x in tiles], axis=1)
    rows = [first] + [pltpu.roll(first, 16 * r, 1) for r in range(1, BLOCK)]
    for r in range(0, BLOCK, 16 // n):
        target_ref[n * r : n * r + 16, :] = jnp.concatenate(rows[r : r + 16 // n], axis=0).astype(BF16)


def band_compact(wide_ref, target_ref, slots, outs):
    n = wide_ref.shape[1]
    tiles = [jnp.zeros((n, 128), wide_ref.dtype)] * (target_ref.shape[1] // 128)
    for c in range(3):
        for a in range(3):
            tile, off = divmod(16 * slots * c + 16 * a, 128)
            tiles[tile] = tiles[tile] + turn(wide_ref[3 * c + a], off)
    first = jnp.concatenate(tiles, axis=1)
    rows = [pltpu.roll(first, 16 * r, 1) if r else first for r in range(outs)]
    rows = rows + [jnp.zeros_like(first)] * (target_ref.shape[0] // n - outs)
    for r in range(0, len(rows), 16 // n):
        target_ref[n * r : n * r + 16, :] = jnp.concatenate(rows[r : r + 16 // n], axis=0).astype(BF16)


def main_kernel(
    size, rows_ref, mask_ref, k_one_ref, k_two_ref, k_three_ref, b_one_ref, b_two_ref, b_three_ref,
    out_ref, north_ref, ocean_ref, one_ref, two_ref, three_ref,
    late_one_ref, late_two_ref, late_three_ref, bias_ref,
    wide_ref, narrow_ref, first_ref, second_ref, third_ref,
):
    top = lax.axis_index("lat") == size - 1
    col = lanes()
    for t in range(3):
        for half in range(2):
            folded = jnp.take_along_axis(rows_ref[ROWS - 1 - t, half], 127 - col, axis=1)
            folded = -folded if half == 0 else folded
            north_ref[2 * t + half] = jnp.where(top, folded, rows_ref[ROWS - 3 + t, half])
    ocean = jnp.zeros((8, 128), F32)
    for b in range(8):
        x = 0.1 * mask_ref[8 * b : 8 * b + 8, :].astype(F32)
        ocean = jnp.where(col // 16 == b, turn(x, 6 + 16 * b), ocean)
    ocean_ref[...] = ocean

    biases = []
    at = 0
    for ref in (b_one_ref, b_two_ref, b_three_ref):
        n = ref.shape[1]
        same = lax.broadcasted_iota(jnp.int32, (n, n), 0) == lax.broadcasted_iota(jnp.int32, (n, n), 1)
        column = jnp.sum(jnp.where(same, ref[...], 0.0), axis=1, keepdims=True)
        biases.append(jnp.broadcast_to(column, (n, 128)))
        bias_ref[at : at + n, :] = biases[-1]
        at += n
    band(k_one_ref, wide_ref.at[0], one_ref)
    band(k_two_ref, wide_ref.at[1], two_ref)
    band(k_three_ref, narrow_ref, three_ref)
    band_compact(wide_ref.at[0], late_one_ref, 5, 3)
    band_compact(wide_ref.at[1], late_two_ref, 7, 5)
    band_compact(narrow_ref, late_three_ref, 5, 3)
    for ref in (first_ref, second_ref, third_ref):
        for c in range(3):
            for row in (0, ROWS + 1, ROWS + 2, ROWS + 3):
                ref[c, row] = jnp.zeros((16, 128), BF16)

    for row in range(ROWS):
        x = jnp.concatenate([rows_ref[row, 0], rows_ref[row, 1]], axis=0).astype(BF16)
        for c in range(3):
            first_ref[c, row + 1] = turn(x, 1 - c)

    def layer(source, weights, at):
        parts = []
        for start in (at, at + ROWS // 2):
            for c in range(3):
                count = BLOCK + 2 if c < 2 else BLOCK + 4
                parts.append(source[c, start : start + count].reshape(16 * count, 128))
        x = jnp.concatenate(
            [jnp.concatenate(parts[0:3], axis=0), jnp.concatenate(parts[3:6], axis=0)], axis=1
        )
        return dot(weights[...], x)

    for source, weights, bias, target in (
        (first_ref, one_ref, biases[0], second_ref),
        (second_ref, two_ref, biases[1], third_ref),
    ):
        bias = jnp.concatenate([bias, bias], axis=1)
        for at in range(0, ROWS // 2, BLOCK):
            total = layer(source, weights, at).reshape(BLOCK, 16, 256)
            value = silu(total + bias[None]).astype(BF16).reshape(16 * BLOCK, 256)
            for part in range(2):
                start = at + ROWS // 2 * part + 1
                x = value[:, 128 * part : 128 * part + 128]
                for c in range(3):
                    target[c, start : start + BLOCK] = turn(x, 1 - c).reshape(BLOCK, 16, 128)

    bias = jnp.concatenate([biases[2], biases[2]], axis=1)
    for at in range(0, ROWS // 2, BLOCK):
        forcing = layer(third_ref, three_ref, at).reshape(BLOCK, 8, 256) + bias[None]
        for part in range(2):
            for r in range(BLOCK):
                row = at + ROWS // 2 * part + r
                near = [min(max(row + d, 0), ROWS - 1) for d in (0, 1, -1)]
                q, north, south = [[rows_ref[i, half] for half in range(2)] for i in near]
                east = [turn(x, -1) for x in q]
                west = [turn(x, 1) for x in q]
                new = tendency(q, north, south, east, west)
                new[0] = new[0] + forcing[r, :, 128 * part : 128 * part + 128]
                ocean = 0.1 * mask_ref[row : row + 1, :].astype(F32)
                for half in range(2):
                    out_ref[row, half] = q[half] + ocean * new[half]


def main_pass(size, rows, mask, parameters):
    taps = pltpu.VMEM((3, ROWS + 4, 16, 128), BF16)
    block = jax.ShapeDtypeStruct
    return pl.pallas_call(
        functools.partial(main_kernel, size),
        out_shape=[
            block(rows.shape, F32),
            block((6, 8, 128), F32),
            block((8, 128), F32),
            *[block((n, DEPTH), BF16) for n in (128, 128, 64)],
            *[block(shape, BF16) for shape in ((48, 256), (80, 384), (32, 256))],
            block((40, 128), F32),
        ],
        in_specs=[VMEM] * 8,
        out_specs=[VMEM] * 10,
        scratch_shapes=[
            pltpu.VMEM((2, 9, 16, 128), BF16),
            pltpu.VMEM((9, 8, 128), F32),
            *[taps] * 3,
        ],
        compiler_params=pltpu.CompilerParams(vmem_limit_bytes=LIMIT),
        cost_estimate=pl.CostEstimate(
            flops=150000000, bytes_accessed=1500000, transcendentals=300000
        ),
        name="main_pass",
    )(rows, mask, *parameters)


def taps(rows, count):
    blank = jnp.zeros_like(rows[0])
    result = []
    for c in range(3):
        for row in rows:
            width = row.shape[1] // 128
            parts = [turn(row[:, 128 * i : 128 * i + 128], 1 - c) for i in range(width)]
            result.append(jnp.concatenate(parts, axis=1) if width > 1 else parts[0])
        result.extend([blank] * ((BLOCK + 2 if c < 2 else BLOCK + 4) - len(rows)))
    return jnp.concatenate(result, axis=0)


def strip_kernel(
    rows_ref, strip_ref, outer_ref, inner_ref, main_ref, ocean_ref, one_ref, two_ref, three_ref,
    bias_ref, cells_ref, low_ref, high_ref, side_ref, pre_ref, hidden_ref,
):
    east, west = sides(inner_ref, outer_ref)
    col = lanes()
    at = col % 16
    cells = []
    for r in range(8):
        pair = [[], []]
        for half in range(2):
            block = 2 * (r // 4) + half
            own = strip_ref[r, half]
            pair[0].append(jnp.where(at < 6, own, turn(east[block], 6 - 4 * (r % 4))))
            pair[1].append(jnp.where(at < 3, turn(west[block], -4 * (r % 4)), turn(own, -3)))
        cells.append(pair)

    def moved(pair, by):
        return [[turn(x, by) for x in part] for part in pair]

    cells = [moved(x, 16) for x in cells[5:8]] + cells + [moved(x, -16) for x in cells[0:3]]
    rows = []
    for pair in cells:
        parts = [jnp.concatenate(part, axis=0) for part in pair]
        rows.append(jnp.concatenate(parts, axis=1).astype(BF16))

    for weights, bias_at in ((one_ref, 0), (two_ref, 16)):
        count = len(rows) - 2 - BLOCK
        bias = jnp.concatenate([bias_ref[bias_at : bias_at + 16, :]] * 2, axis=1)
        low = dot(weights[...], taps(rows[0:10], 256)).reshape(BLOCK, 16, 256)
        high = dot(weights[0 : 16 * count, :], taps(rows[BLOCK:], 256)).reshape(count, 16, 256)
        low = silu(low + bias[None]).astype(BF16)
        high = silu(high + bias[None]).astype(BF16)
        rows = [low[i] for i in range(BLOCK)] + [high[i] for i in range(count)]
    forcing = dot(three_ref[...], taps(rows, 256)).reshape(BLOCK, 8, 256)
    forcing = forcing + jnp.concatenate([bias_ref[32:40, :]] * 2, axis=1)[None]

    both = []
    for r in range(8):
        new = []
        for part in range(2):
            q, north, south = [cells[i][part] for i in (r + 3, r + 4, r + 2)]
            value = tendency(
                q, north, south, [turn(x, -1) for x in q], [turn(x, 1) for x in q]
            )
            value[0] = value[0] + forcing[r, :, 128 * part : 128 * part + 128]
            new.append(value)
        ocean = ocean_ref[r : r + 1, :]
        value = [jnp.where(at < 6, new[0][half], turn(new[1][half], 3)) for half in range(2)]
        both.append([strip_ref[r, half] + ocean * value[half] for half in range(2)])

    edge = (col < 3) | (col >= 125)
    for b in range(8):
        ref, start = (low_ref, 0) if b == 0 else (high_ref, 0) if b == 7 else (cells_ref, 8 * b - 8)
        pitch = ref.shape[1]
        flat = ref.reshape(16 * pitch, 128)
        for r in range(8):
            for half in range(2):
                value = turn(both[r][half], -(16 * b + 6))
                value = jnp.where(edge, value, main_ref[8 * b + r, half])
                flat[pl.ds(8 * pitch * half + start + r, 8, stride=pitch), :] = value


    def own(row):
        start = 16 * (row // 8) + 4 * (row % 4)
        block = 2 * (row % 8 // 4)
        return [beside(east[block + h], start, west[block + h], start) for h in range(2)]

    own_rows = []
    for row in list(range(6)) + list(range(ROWS - 6, ROWS)):
        side = own(row)
        at = row if row < 3 else row - ROWS + 6
        if row < 3 or row >= ROWS - 3:
            for half in range(2):
                side_ref[at, half] = side[half]
        parts = [
            jnp.concatenate([rows_ref[row, 0], rows_ref[row, 1]], axis=0),
            jnp.concatenate(side, axis=0),
        ]
        own_rows.append(jnp.concatenate(parts, axis=1).astype(BF16))
    blank = jnp.zeros((16, 256), BF16)
    low = [blank] * 3 + own_rows[0:6]
    high = own_rows[6:12] + [blank] * 3
    rows = [jnp.concatenate(pair, axis=1) for pair in zip(low, high)]
    total = dot(one_ref[0:112, :], spread(rows, 256)).reshape(7, 16, 512)
    total = total + jnp.concatenate([bias_ref[0:16, :]] * 4, axis=1)[None]
    for r in range(3):
        pre_ref[r] = jnp.concatenate([total[r, :, 0:256], total[4 + r, :, 256:512]], axis=1)
    for r in range(4):
        for strip, x in enumerate((total[3 + r, :, 0:256], total[r, :, 256:512])):
            value = silu(x).astype(BF16)
            for c in range(3):
                hidden_ref[strip, c, r] = turn_wide(value, c)


def strip_pass(rows, strip, inner, outer, main, ocean, weights, bias):
    block = jax.ShapeDtypeStruct
    return pl.pallas_call(
        strip_kernel,
        out_shape=[
            block((16, ROWS - 8, 128), F32),
            *[block((16, 8, 128), F32)] * 2,
            block((6, 2, 8, 128), F32),
            block((3, 16, 512), F32),
            block((2, 3, 4, 16, 256), BF16),
        ],
        in_specs=[VMEM] * 10,
        out_specs=[VMEM] * 6,
        compiler_params=pltpu.CompilerParams(vmem_limit_bytes=LIMIT),
        cost_estimate=pl.CostEstimate(
            flops=150000000, bytes_accessed=2000000, transcendentals=100000
        ),
        name="strip_pass",
    )(rows, strip, outer, inner, main, ocean, *weights, bias)


def border_kernel(
    rows_ref, mask_ref, first_ref, second_ref, side_ref, pre_ref, hidden_ref, one_ref, two_ref,
    three_ref, bias_ref, cells_ref, low_in_ref, high_in_ref, out_ref, low_ref, high_ref, sems,
):
    lat = lax.axis_index("lat")
    even = lax.rem(lat, 2) == 0
    span = pl.ds(8, ROWS - 16)
    source = cells_ref.at[:, pl.ds(0, ROWS - 16), :]
    stores = [pltpu.make_async_copy(source, out_ref.at[:, span, :], sems.at[0])]
    stores[0].start()

    south, north = [], []
    low, high = [], []
    for t in range(3):
        blocks = [[], [], [], []]
        for half in range(2):
            at = 2 * t + half
            corner = jnp.where(even, second_ref[6], first_ref[6])
            x = jnp.where(even, second_ref[at], first_ref[at])
            y = beside(corner, 32 * half + 4 + 4 * t, corner, 32 * half + 20 + 4 * t)
            blocks[0].append(jnp.where(lat == 0, 0.0, x))
            blocks[1].append(jnp.where(lat == 0, 0.0, y))
            corner = jnp.where(even, first_ref[6], second_ref[6])
            blocks[2].append(jnp.where(even, first_ref[at], second_ref[at]))
            blocks[3].append(beside(corner, 32 * half + 4 * t, corner, 32 * half + 16 + 4 * t))
        south.append(blocks[0])
        north.append(blocks[2])
        wide = [jnp.concatenate(x, axis=0) for x in blocks]
        low.append(jnp.concatenate(wide[0:2], axis=1).astype(BF16))
        high.append(jnp.concatenate(wide[2:4], axis=1).astype(BF16))

    blank = jnp.zeros((16, 256), BF16)
    operand = []
    for c in range(3):
        lows = [turn_wide(x, c) for x in low] + [blank] * 2
        highs = [blank] * 2 + [turn_wide(x, c) for x in high]
        operand.extend(jnp.concatenate(pair, axis=1) for pair in zip(lows, highs))
    operand.append(jnp.zeros((16, 512), BF16))
    total = dot(one_ref[...], jnp.concatenate(operand, axis=0)).reshape(3, 16, 512)
    late = silu(total + pre_ref[...]).astype(BF16)

    operand = []
    for c in range(3):
        lows = [turn_wide(late[r, :, 0:256], c) for r in range(3)]
        lows = lows + [hidden_ref[0, c, r] for r in range(4)]
        highs = [hidden_ref[1, c, r] for r in range(4)]
        highs = highs + [turn_wide(late[r, :, 256:512], c) for r in range(3)]
        operand.extend(jnp.concatenate(pair, axis=1) for pair in zip(lows, highs))
    operand.extend([jnp.zeros((16, 512), BF16)] * 3)
    total = dot(two_ref[...], jnp.concatenate(operand, axis=0)).reshape(5, 16, 512)
    value = silu(total + jnp.concatenate([bias_ref[16:32, :]] * 4, axis=1)[None]).astype(BF16)
    operand = []
    for c in range(3):
        for r in range(5):
            parts = [turn_wide(value[r, :, at : at + 256], c)[:, 0:128] for at in (0, 256)]
            operand.append(jnp.concatenate(parts, axis=1))
    operand.append(jnp.zeros((16, 256), BF16))
    total = dot(three_ref[...], jnp.concatenate(operand, axis=0)).reshape(4, 8, 256)
    total = total + jnp.concatenate([bias_ref[32:40, :]] * 2, axis=1)[None]

    col = lanes()
    own = {row: [rows_ref[row, half] for half in range(2)] for row in (0, 1, 2, 3, 60, 61, 62, 63)}
    own[-1], own[ROWS] = south[2], north[0]
    for strip in range(2):
        ref, at = ((low_ref, 0), (high_ref, ROWS - 8))[strip]
        flat = ref.reshape(128, 128)
        for t in range(3):
            row = t if strip == 0 else ROWS - 3 + t
            q = own[row]
            side = [side_ref[3 * strip + t, half] for half in range(2)]
            ocean = 0.1 * mask_ref[row : row + 1, :].astype(F32)
            e = [turn(jnp.where(col == 0, y, x), -1) for x, y in zip(q, side)]
            w = [turn(jnp.where(col == 127, y, x), 1) for x, y in zip(q, side)]
            new = tendency(q, own[row + 1], own[row - 1], e, w)
            new[0] = new[0] + total[t, :, 128 * strip : 128 * strip + 128]
            for half in range(2):
                flat[pl.ds(64 * half + row - at, 8, stride=8), :] = q[half] + ocean * new[half]
        store = pltpu.make_async_copy(ref, out_ref.at[:, pl.ds(at, 8), :], sems.at[1 + strip])
        store.start()
        stores.append(store)
    for store in stores:
        store.wait()


def border_pass(rows, mask, first, second, side, pre, hidden, late, bias, cells, low, high):
    block = jax.ShapeDtypeStruct
    out, _, _ = pl.pallas_call(
        border_kernel,
        out_shape=[block((16, ROWS, 128), F32), block(low.shape, F32), block(high.shape, F32)],
        in_specs=[VMEM] * 14,
        out_specs=[HBM, VMEM, VMEM],
        scratch_shapes=[pltpu.SemaphoreType.DMA((3,))],
        input_output_aliases={12: 1, 13: 2},
        compiler_params=pltpu.CompilerParams(vmem_limit_bytes=LIMIT),
        cost_estimate=pl.CostEstimate(flops=60000000, bytes_accessed=1000000, transcendentals=60000),
        name="border_pass",
    )(rows, mask, first, second, side, pre, hidden, *late, bias, cells, low, high)
    return out


def shards(state, land_mask, kernel_one, bias_one, kernel_two, bias_two, kernel_three, bias_three):
    lon, lat = (lax.axis_size("lon"), lax.axis_size("lat"))
    biases = [x.reshape(1, x.shape[0]) for x in (bias_one, bias_two, bias_three)]
    rows, strip, outer, inner, mask, *parameters = prepare(
        state, (land_mask, kernel_one, kernel_two, kernel_three, *biases)
    )

    inner = lax.ppermute(inner, "lon", [(i, i + 1 - 2 * (i % 2)) for i in range(lon)])
    outer = lax.ppermute(outer, "lon", [(i, (i + 1 if i % 2 else i - 1) % lon) for i in range(lon)])
    main, north, ocean, *weights, bias = main_pass(lat, rows, mask, parameters)
    weights, late = weights[0:3], weights[3:6]

    def pairs(parity):
        result = []
        for i in range(lon):
            for j in range(parity, lat - 1, 2):
                result += [(i * lat + j, i * lat + j + 1), (i * lat + j + 1, i * lat + j)]
            if parity == 1:
                result.append((i * lat, (i + 1 - 2 * (i % 2)) * lat))
            if (lat - 1) % 2 == parity:
                result.append((i * lat + lat - 1, (lon - 1 - i) * lat + lat - 1))
        return result

    first, second = corners(lat, rows, inner, outer, north)
    first = lax.ppermute(first, ("lon", "lat"), pairs(0))
    second = lax.ppermute(second, ("lon", "lat"), pairs(1))
    cells, low, high, *own = strip_pass(
        rows, strip, inner, outer, main, ocean, weights, bias
    )
    return border_pass(rows, mask, first, second, *own, late, bias, cells, low, high)


def solution(mesh):
    return jax.shard_map(
        shards,
        mesh=mesh,
        in_specs=(P(None, "lat", "lon"), P("lat", "lon"), P(), P(), P(), P(), P(), P()),
        out_specs=P(None, "lat", "lon"),
        check_vma=False,
    )
```

time: 92 us -> 13 us (0.14); the launches traced: 90.5 us -> 12.8 us
  local copies, waits for them, and re-layouts: 45 us -> 0 us
  waiting for transfers between devices: 17.3 us -> 2.63 us
  starting transfers between devices: 15.2 us -> 3.54 us
  matrix products: 9.5 us -> 0 us
  Pallas kernels: 0 us -> 6.61 us
  other arithmetic: 2.85 us -> 0 us
    slice x25 -> x0, local copies, waits for them, and re-layouts: 35.4 us -> none  [the longest x20 34.4 us: conv(): x[:, a:a + rows, c:c + cols]]
    ppermute x4, waiting for transfers between devices: 13.3 us -> 2.63 us  [the longest x1 1.58 us: shards(): second = lax.ppermute(second, ('lon', 'lat'), pairs(1))]
    dot_general x27 -> x0, matrix products: 9.5 us -> none  [conv(): jnp.einsum('ok,khw->ohw', kernel[a, c], x[:, a:a + rows, c:c + cols], pre...]
    all_to_all x2 -> x0, starting transfers between devices: 7.46 us -> none  [the longest x1 4.12 us: fold_rows(): lax.all_to_all(mixed[::-1], 'lon', split_axis=0, concat_axis=0, tiled=True)]
    unnamed x58 -> x0, local copies, waits for them, and re-layouts: 6.78 us -> none
    pallas_call x0 -> x5, Pallas kernels: none -> 6.61 us  [the longest x1 1.8 us: strip_pass(): pl.pallas_call(strip_kernel, out_shape=[block((16, ROWS - 8, 128), F32),...]
    ppermute x4, starting transfers between devices: 7.77 us -> 3.54 us  [the longest x1 1.95 us: shards(): lax.ppermute(outer, 'lon', [(i, (i + 1 if i % 2 else i - 1) % lon) for i...]
    all_to_all x2 -> x0, waiting for transfers between devices: 3.97 us -> none  [the longest x1 3.96 us: fold_rows(): lax.all_to_all(mixed[::-1], 'lon', split_axis=0, concat_axis=0, tiled=True)]
  transfers between devices with their start and end apart: 6 -> 4, of which waited for: 3 -> 3; matrix products, arithmetic and copies ran while one was open for 3% -> 0% of each run, Pallas kernels for 0% -> 27%
where the time goes in v1:
time: 13 us; the launch traced here: 12.8 us
  Pallas kernels  6.61 us (51%)
  starting transfers between devices  3.54 us (27%)
  waiting for transfers between devices  2.63 us (20%)
    ppermute x1, starting transfers between devices, shards(): lax.ppermute(outer, 'lon', [(i, (i + 1 if i % 2 else i - 1) % lon) for i...  1.95 us
    pallas_call x1, Pallas kernels, strip_pass(): pl.pallas_call(strip_kernel, out_shape=[block((16, ROWS - 8, 128), F32),...  1.8 us
    pallas_call x1, Pallas kernels, main_pass(): pl.pallas_call(functools.partial(main_kernel, size), out_shape=[block(row...  1.67 us
    ppermute x1, starting transfers between devices, shards(): first = lax.ppermute(first, ('lon', 'lat'), pairs(0))  1.58 us
    ppermute x1, waiting for transfers between devices, shards(): second = lax.ppermute(second, ('lon', 'lat'), pairs(1))  1.58 us
    pallas_call x1, Pallas kernels, prepare(): pl.pallas_call(prepare_kernel, out_shape=[block((ROWS, 2, 8, 128), F32),...  1.56 us
    pallas_call x1, Pallas kernels, border_pass(): pl.pallas_call(border_kernel, out_shape=[block((16, ROWS, 128), F32), blo...  1.49 us
    ppermute x1, waiting for transfers between devices, shards(): lax.ppermute(outer, 'lon', [(i, (i + 1 if i % 2 else i - 1) % lon) for i...  0.57 us
  transfers between devices with their start and end apart: 4, of which 3 were waited for; matrix products, arithmetic and copies ran while one was open for 0% of the time, Pallas kernels for 27%

profile of v1, /device:TPU:16, one launch (start us, length us, event | category | flops | bytes accessed | tf_op | source)
XLA Modules:
  0.0 12.8 jit_solution(11087278687281108411)
XLA Ops:
  0.0 1.6 %rows_edges.1 = (f32[64,2,8,128]{3,2,1,0:T(8,128)S(1)}, f32[8,2,8,128]{3,2,1,0:T(8,128)S(1)}, f32[4,8,128]{2,1,0:T(8,128)S(1)}, f32[4,8,128]{2,1,0:T(8,128)S(1)}...) custom-call(f32[16,64,128]{2,1,0:T(8,128)} %state_ref.1, ...), custom_call_target="tpu_custom_call" | custom-call | flops 400000 | bytes 1200000 | tf_op jit(solution)/shard_map/rows_edges/pallas_call | solution.py:132
  1.6 2.0 %collective-permute-start = (f32[4,8,128]{2,1,0:T(8,128)S(1)}, f32[4,8,128]{2,1,0:T(8,128)S(1)}, u32[]{:S(2)}, u32[]{:S(2)}) collective-permute-start(f32[4,8,128]{2,1,0:T(8,128)S(1)} %get-tuple-element.37), channel_id=1, source_target_pairs={{0,28},{4,8},{8,4},{12,16},{16,12},{20,24},{24,20},{28,0},{1,29},{... | collective-permute-start | bytes 49160 | tf_op jit(solution)/shard_map/ppermute | solution.py:571
  3.5 0.0 collective-permute-start.1
  3.5 1.7 %main_pass.1 = (f32[64,2,8,128]{3,2,1,0:T(8,128)S(1)}, f32[6,8,128]{2,1,0:T(8,128)S(1)}, f32[8,128]{1,0:T(8,128)S(1)}, bf16[128,512]{1,0:T(8,128)(2,1)S(1)}, bf1...) custom-call(f32[64,2,8,128]{3,2,1,0:T(8,128)S(1)} %get-tuple-element, ...), custom_call_target="tpu_custom_call" | custom-call | flops 150000000 | bytes 1500000 | tf_op jit(solution)/shard_map/main_pass/pallas_call | solution.py:310
  5.2 0.6 %collective-permute-done.outer_ref = f32[4,8,128]{2,1,0:T(8,128)S(1)} collective-permute-done((f32[4,8,128]{2,1,0:T(8,128)S(1)}, f32[4,8,128]{2,1,0:T(8,128)S(1)}, u32[]{:S(2)}, u32[]{:S(2)}) %collective-permute-start) | collective-permute-done | bytes 16416 | tf_op jit(solution)/shard_map/ppermute | solution.py:571
  5.8 0.0 collective-permute-done.1.inner_ref
  5.8 0.1 add_corners.1
  5.9 1.6 %collective-permute-start.2 = (f32[7,8,128]{2,1,0:T(8,128)S(1)}, f32[7,8,128]{2,1,0:T(8,128)S(1)}, u32[]{:S(2)}, u32[]{:S(2)}) collective-permute-start(f32[7,8,128]{2,1,0:T(8,128)S(1)} %get-tuple-element.46), channel_id=1, source_target_pairs={{0,1},{1,0},{2,3},{3,2},{4,5},{5,4},{6,7},{7,6},{8,9},{9,8},{10,11... | collective-permute-start | bytes 86024 | tf_op jit(solution)/shard_map/ppermute | solution.py:587
  7.5 0.0 collective-permute-start.3
  7.5 1.8 %strip_pass.1 = (f32[16,56,128]{2,1,0:T(8,128)S(1)}, f32[16,8,128]{2,1,0:T(8,128)S(1)}, f32[16,8,128]{2,1,0:T(8,128)S(1)}, f32[6,2,8,128]{3,2,1,0:T(8,128)S(1)},...) custom-call(f32[64,2,8,128]{3,2,1,0:T(8,128)S(1)} %get-tuple-element.35.rows_ref, ...), custom_call_target="tpu_custom_call" | custom-call | flops 150000000 | bytes 2000000 | tf_op jit(solution)/shard_map/strip_pass/pallas_call | solution.py:444
  9.3 0.5 %collective-permute-done.2.first_ref = f32[7,8,128]{2,1,0:T(8,128)S(1)} collective-permute-done((f32[7,8,128]{2,1,0:T(8,128)S(1)}, f32[7,8,128]{2,1,0:T(8,128)S(1)}, u32[]{:S(2)}, u32[]{:S(2)}) %collective-permute-start.2) | collective-permute-done | bytes 28704 | tf_op jit(solution)/shard_map/ppermute | solution.py:587
  9.7 1.6 %collective-permute-done.3.second_ref = f32[7,8,128]{2,1,0:T(8,128)S(1)} collective-permute-done((f32[7,8,128]{2,1,0:T(8,128)S(1)}, f32[7,8,128]{2,1,0:T(8,128)S(1)}, u32[]{:S(2)}, u32[]{:S(2)}) %collective-permute-start.3) | collective-permute-done | bytes 28704 | tf_op jit(solution)/shard_map/ppermute | solution.py:588
  11.3 1.5 %border_pass.1 = (f32[16,64,128]{2,1,0:T(8,128)}, f32[16,8,128]{2,1,0:T(8,128)S(1)}, f32[16,8,128]{2,1,0:T(8,128)S(1)}) custom-call(f32[64,2,8,128]{3,2,1,0:T(8,128)S(1)} %get-tuple-element.35.rows_ref, s32[64,128]{1,0:T(8,128)S(1)} %get-tuple-element.36.mask_ref, ...), custom_call_target="tpu_custom_call", output_to_operand_aliasing={{1}: (12, {}), {2}: (13, {})} | custom-call | flops 60000000 | bytes 1000000 | tf_op jit(solution)/shard_map/border_pass/pallas_call | solution.py:549
Async XLA Ops:
  1.6 4.2 %collective-permute-start = (f32[4,8,128]{2,1,0:T(8,128)S(1)}, f32[4,8,128]{2,1,0:T(8,128)S(1)}, u32[]{:S(2)}, u32[]{:S(2)}) collective-permute-start(f32[4,8,128]{2,1,0:T(8,128)S(1)} %get-tuple-element.37), channel_id=1, source_target_pairs={{0,28},{4,8},{8,4},{12,16},{16,12},{20,24},{24,20},{28,0},{1,29},{... | collective-permute-start | bytes 49160 | tf_op jit(solution)/shard_map/ppermute | solution.py:571
  3.5 2.3 %collective-permute-start.1 = (f32[4,8,128]{2,1,0:T(8,128)S(1)}, f32[4,8,128]{2,1,0:T(8,128)S(1)}, u32[]{:S(2)}, u32[]{:S(2)}) collective-permute-start(f32[4,8,128]{2,1,0:T(8,128)S(1)} %get-tuple-element.38), channel_id=1, source_target_pairs={{0,4},{4,0},{8,12},{12,8},{16,20},{20,16},{24,28},{28,24},{1,5},{5... | collective-permute-start | bytes 49160 | tf_op jit(solution)/shard_map/ppermute | solution.py:570
  5.9 3.9 %collective-permute-start.2 = (f32[7,8,128]{2,1,0:T(8,128)S(1)}, f32[7,8,128]{2,1,0:T(8,128)S(1)}, u32[]{:S(2)}, u32[]{:S(2)}) collective-permute-start(f32[7,8,128]{2,1,0:T(8,128)S(1)} %get-tuple-element.46), channel_id=1, source_target_pairs={{0,1},{1,0},{2,3},{3,2},{4,5},{5,4},{6,7},{7,6},{8,9},{9,8},{10,11... | collective-permute-start | bytes 86024 | tf_op jit(solution)/shard_map/ppermute | solution.py:587
  7.5 3.9 %collective-permute-start.3 = (f32[7,8,128]{2,1,0:T(8,128)S(1)}, f32[7,8,128]{2,1,0:T(8,128)S(1)}, u32[]{:S(2)}, u32[]{:S(2)}) collective-permute-start(f32[7,8,128]{2,1,0:T(8,128)S(1)} %get-tuple-element.47), channel_id=1, source_target_pairs={{1,2},{2,1},{0,4},{3,31},{5,6},{6,5},{4,0},{7,27},{9,10},{10,9},{8... | collective-permute-start | bytes 86024 | tf_op jit(solution)/shard_map/ppermute | solution.py:588

commit v2 on v1

--- a/solution.py
+++ b/solution.py
@@ -84,19 +84,65 @@
     return jnp.concatenate(result, axis=0)
 
 
-def prepare_kernel(state_ref, *refs):
-    others, refs = refs[0:7], refs[7:]
-    rows_ref, strip_ref, outer_ref, inner_ref, *held, cells_ref, sems = refs
-    fetches = []
-    for at in range(0, 16, 2):
-        span = pl.ds(at, 2)
-        target = cells_ref.at[span, pl.ds(0, ROWS), :]
-        fetches.append(pltpu.make_async_copy(state_ref.at[span], target, sems.at[len(fetches)]))
-    for source, target in zip(others, held):
-        fetches.append(pltpu.make_async_copy(source, target, sems.at[len(fetches)]))
+def small_kernel(
+    state_ref, b_one_ref, b_two_ref, b_three_ref,
+    cells_ref, outer_ref, inner_ref, h_one_ref, h_two_ref, h_three_ref, sems,
+):
+    pairs = []
+    for at, count in ((0, 8), (ROWS - 8, 8), (8, ROWS - 16)):
+        piece = (slice(None), pl.ds(at, count), slice(None))
+        pairs.append((state_ref.at[piece], cells_ref.at[piece]))
+    pairs += [(b_one_ref, h_one_ref), (b_two_ref, h_two_ref), (b_three_ref, h_three_ref)]
+    fetches = [
+        pltpu.make_async_copy(source, target, sems.at[i]) for i, (source, target) in enumerate(pairs)
+    ]
     for fetch in fetches:
         fetch.start()
-
+    even = even_place("lon")
+    for fetch in fetches[0:2]:
+        fetch.wait()
+
+    flat = cells_ref.reshape(16 * PITCH, 128)
+    part = lanes() // 4
+    outer = inner = jnp.zeros((8, 128), F32)
+    for high in range(2):
+        for half in range(2):
+            for s in range(3):
+                row = s + (ROWS - 3) * high
+                x = flat[pl.ds(8 * PITCH * half + row, 8, stride=PITCH), :]
+                at = 64 * high + 32 * half + 4 * s
+                first, last = at, (at - 125) % 128
+                by = jnp.where(even, first, last)
+                outer = jnp.where(part == at // 4, turn(x, by), outer)
+                by = jnp.where(even, last, first)
+                inner = jnp.where(part == at // 4, turn(x, by), inner)
+    outer_ref[...] = outer
+    inner_ref[...] = inner
+    for fetch in fetches[2:]:
+        fetch.wait()
+
+
+def small_edges(state, biases):
+    block = jax.ShapeDtypeStruct
+    arrays = [pltpu.with_memory_space_constraint(x, pltpu.HBM) for x in (state, *biases)]
+    return pl.pallas_call(
+        small_kernel,
+        out_shape=[
+            block((16, PITCH, 128), F32),
+            block((8, 128), F32),
+            block((8, 128), F32),
+            *[block(x.shape, F32) for x in biases],
+        ],
+        in_specs=[HBM] * 4,
+        out_specs=[VMEM] * 6,
+        scratch_shapes=[pltpu.SemaphoreType.DMA((6,))],
+        compiler_params=pltpu.CompilerParams(vmem_limit_bytes=LIMIT),
+        cost_estimate=pl.CostEstimate(flops=20000, bytes_accessed=1000000, transcendentals=0),
+        name="small_edges",
+    )(*arrays)
+
+
+def rows_kernel(size, cells_ref, rows_ref, strip_ref, outer_ref, inner_ref, north_ref):
     flat = cells_ref.reshape(16 * PITCH, 128)
     group = lanes() // 16
     part = (lanes() % 16) // 4
@@ -105,8 +151,6 @@
         [jnp.where(even, (4 * s - a) % 128, (4 * s - b) % 128) for s in range(4)]
         for a, b in ((6, 3), (3, 6))
     ]
-    for fetch in fetches[0:8]:
-        fetch.wait()
     for half in range(2):
         strip = [jnp.zeros((8, 128), F32)] * 8
         for b in range(8):
@@ -122,32 +166,38 @@
                 for s in range(4):
                     value = jnp.where(part == s, turn(strip[4 * q + s], shift[s]), value)
                 target[2 * q + half] = value
-    for fetch in fetches[8:]:
-        fetch.wait()
-
-
-def prepare(state, others):
+
+    top = lax.axis_index("lat") == size - 1
+    order = jnp.where(top, 127 - lanes(), lanes())
+    for t in range(3):
+        for half in range(2):
+            row = jnp.where(top, ROWS - 1 - t, ROWS - 3 + t)
+            x = jnp.take_along_axis(
+                flat[pl.ds(8 * PITCH * half + row, 8, stride=PITCH), :], order, axis=1
+            )
+            north_ref[2 * t + half] = jnp.where(top, -x, x) if half == 0 else x
+
+
+def rows_edges(size, cells):
     block = jax.ShapeDtypeStruct
-    arrays = [pltpu.with_memory_space_constraint(x, pltpu.HBM) for x in (state, *others)]
     return pl.pallas_call(
-        prepare_kernel,
+        functools.partial(rows_kernel, size),
         out_shape=[
             block((ROWS, 2, 8, 128), F32),
             block((8, 2, 8, 128), F32),
             block((4, 8, 128), F32),
             block((4, 8, 128), F32),
-            *[block(x.shape, x.dtype) for x in others],
+            block((6, 8, 128), F32),
         ],
-        in_specs=[HBM] * 8,
-        out_specs=[VMEM] * 11,
-        scratch_shapes=[pltpu.VMEM((16, PITCH, 128), F32), pltpu.SemaphoreType.DMA((15,))],
+        in_specs=[VMEM],
+        out_specs=[VMEM] * 5,
         compiler_params=pltpu.CompilerParams(vmem_limit_bytes=LIMIT),
         cost_estimate=pl.CostEstimate(flops=400000, bytes_accessed=1200000, transcendentals=0),
         name="rows_edges",
-    )(*arrays)
-
-
-def corners_kernel(size, rows_ref, outer_ref, inner_ref, north_ref, first_ref, second_ref):
+    )(cells)
+
+
+def corners_kernel(size, rows_ref, outer_ref, inner_ref, north_ref, _, first_ref, second_ref):
     lat = lax.axis_index("lat")
     even = lax.rem(lat, 2) == 0
     for t in range(3):
@@ -158,33 +208,33 @@
             second_ref[at] = jnp.where(even, low, north_ref[at])
     top = lat == size - 1
     col = lanes()
-    part = col // 16
+    side = col // 16 % 2
     straight = even_place("lon")
     mirrored = straight != top
-    index = jnp.where(top, 112 + 4 * (3 - col // 4 % 4) + 2 - col % 4, 112 + col % 16)
-    low = high = jnp.zeros((8, 128), F32)
-    for i in range(4):
-        half = i // 2
-        pair = (inner_ref, outer_ref) if i % 2 == 0 else (outer_ref, inner_ref)
-        x = jnp.where(straight, pair[0][half], pair[1][half])
-        low = jnp.where(part == i, turn(x, 16 * i), low)
-        x = jnp.where(mirrored, pair[0][2 + half], pair[1][2 + half])
-        high = jnp.where(part == i, jnp.take_along_axis(x, index, axis=1), high)
+    s, j = col // 4 % 4, col % 4
+    index = 64 + 32 * (col // 32 % 2) + jnp.where(top, 4 * (2 - s) + 2 - j, 4 * s + j)
+    inner, outer = inner_ref[...], outer_ref[...]
+    low = jnp.where(side == 0, jnp.where(straight, inner, outer), turn(jnp.where(straight, outer, inner), 16))
+    high = [
+        jnp.take_along_axis(jnp.where(mirrored, *pair), index, axis=1)
+        for pair in ((inner, outer), (outer, inner))
+    ]
+    high = jnp.where(side == 0, *high)
     high = jnp.where(top & (col < 32), -high, high)
     first_ref[6] = jnp.where(even, high, low)
     second_ref[6] = jnp.where(even, low, high)
 
 
-def corners(size, rows, inner, outer, north):
+def corners(size, rows, inner, outer, north, main):
     return pl.pallas_call(
         functools.partial(corners_kernel, size),
         out_shape=[jax.ShapeDtypeStruct((7, 8, 128), F32)] * 2,
-        in_specs=[VMEM] * 4,
+        in_specs=[VMEM] * 4 + [pl.BlockSpec(memory_space=pl.ANY)],
         out_specs=[VMEM] * 2,
         compiler_params=pltpu.CompilerParams(vmem_limit_bytes=LIMIT),
         cost_estimate=pl.CostEstimate(flops=1000, bytes_accessed=100000, transcendentals=0),
         name="add_corners",
-    )(rows, outer, inner, north)
+    )(rows, outer, inner, north, main)
 
 
 def band(kernel_ref, wide_ref, target_ref):
@@ -218,19 +268,41 @@
         target_ref[n * r : n * r + 16, :] = jnp.concatenate(rows[r : r + 16 // n], axis=0).astype(BF16)
 
 
-def main_kernel(
-    size, rows_ref, mask_ref, k_one_ref, k_two_ref, k_three_ref, b_one_ref, b_two_ref, b_three_ref,
-    out_ref, north_ref, ocean_ref, one_ref, two_ref, three_ref,
-    late_one_ref, late_two_ref, late_three_ref, bias_ref,
-    wide_ref, narrow_ref, first_ref, second_ref, third_ref,
-):
-    top = lax.axis_index("lat") == size - 1
+def layer(source, weights, at):
+    halves = []
+    for start in (at, at + ROWS // 2):
+        parts = []
+        for c in range(3):
+            count = BLOCK + 2 if c < 2 else BLOCK + 4
+            parts.append(source[c, start : start + count].reshape(16 * count, 128))
+        halves.append(jnp.concatenate(parts, axis=0))
+    return dot(weights[...], jnp.concatenate(halves, axis=1))
+
+
+def clear_ends(ref):
+    for c in range(3):
+        for row in (0, ROWS + 1, ROWS + 2, ROWS + 3):
+            ref[c, row] = jnp.zeros((16, 128), BF16)
+
+
+def hidden(source, weights, bias, target):
+    clear_ends(target)
+    bias = jnp.concatenate([bias, bias], axis=1)
+    for at in range(0, ROWS // 2, BLOCK):
+        total = layer(source, weights, at).reshape(BLOCK, 16, 256)
+        value = silu(total + bias[None]).astype(BF16).reshape(16 * BLOCK, 256)
+        for part in range(2):
+            start = at + ROWS // 2 * part + 1
+            x = value[:, 128 * part : 128 * part + 128]
+            for c in range(3):
+                target[c, start : start + BLOCK] = turn(x, 1 - c).reshape(BLOCK, 16, 128)
+
+
+def main_first(rows_ref, mask_ref, parameters, held, wide_ref, narrow_ref, first_ref):
+    k_one_ref, k_two_ref, k_three_ref, b_one_ref, b_two_ref, b_three_ref = parameters
+    second_ref, ocean_ref, one_ref, two_ref, three_ref = held[0:5]
+    late_one_ref, late_two_ref, late_three_ref, bias_ref, _ = held[5:10]
     col = lanes()
-    for t in range(3):
-        for half in range(2):
-            folded = jnp.take_along_axis(rows_ref[ROWS - 1 - t, half], 127 - col, axis=1)
-            folded = -folded if half == 0 else folded
-            north_ref[2 * t + half] = jnp.where(top, folded, rows_ref[ROWS - 3 + t, half])
     ocean = jnp.zeros((8, 128), F32)
     for b in range(8):
         x = 0.1 * mask_ref[8 * b : 8 * b + 8, :].astype(F32)
@@ -252,42 +324,19 @@
     band_compact(wide_ref.at[0], late_one_ref, 5, 3)
     band_compact(wide_ref.at[1], late_two_ref, 7, 5)
     band_compact(narrow_ref, late_three_ref, 5, 3)
-    for ref in (first_ref, second_ref, third_ref):
-        for c in range(3):
-            for row in (0, ROWS + 1, ROWS + 2, ROWS + 3):
-                ref[c, row] = jnp.zeros((16, 128), BF16)
-
+
+    clear_ends(first_ref)
     for row in range(ROWS):
         x = jnp.concatenate([rows_ref[row, 0], rows_ref[row, 1]], axis=0).astype(BF16)
         for c in range(3):
             first_ref[c, row + 1] = turn(x, 1 - c)
-
-    def layer(source, weights, at):
-        parts = []
-        for start in (at, at + ROWS // 2):
-            for c in range(3):
-                count = BLOCK + 2 if c < 2 else BLOCK + 4
-                parts.append(source[c, start : start + count].reshape(16 * count, 128))
-        x = jnp.concatenate(
-            [jnp.concatenate(parts[0:3], axis=0), jnp.concatenate(parts[3:6], axis=0)], axis=1
-        )
-        return dot(weights[...], x)
-
-    for source, weights, bias, target in (
-        (first_ref, one_ref, biases[0], second_ref),
-        (second_ref, two_ref, biases[1], third_ref),
-    ):
-        bias = jnp.concatenate([bias, bias], axis=1)
-        for at in range(0, ROWS // 2, BLOCK):
-            total = layer(source, weights, at).reshape(BLOCK, 16, 256)
-            value = silu(total + bias[None]).astype(BF16).reshape(16 * BLOCK, 256)
-            for part in range(2):
-                start = at + ROWS // 2 * part + 1
-                x = value[:, 128 * part : 128 * part + 128]
-                for c in range(3):
-                    target[c, start : start + BLOCK] = turn(x, 1 - c).reshape(BLOCK, 16, 128)
-
-    bias = jnp.concatenate([biases[2], biases[2]], axis=1)
+    hidden(first_ref, one_ref, biases[0], second_ref)
+
+
+def main_rest(rows_ref, mask_ref, held, third_ref):
+    second_ref, _, _, two_ref, three_ref, _, _, _, bias_ref, out_ref = held
+    hidden(second_ref, two_ref, bias_ref[16:32, :], third_ref)
+    bias = jnp.concatenate([bias_ref[32:40, :]] * 2, axis=1)
     for at in range(0, ROWS // 2, BLOCK):
         forcing = layer(third_ref, three_ref, at).reshape(BLOCK, 8, 256) + bias[None]
         for part in range(2):
@@ -304,32 +353,58 @@
                     out_ref[row, half] = q[half] + ocean * new[half]
 
 
-def main_pass(size, rows, mask, parameters):
-    taps = pltpu.VMEM((3, ROWS + 4, 16, 128), BF16)
-    block = jax.ShapeDtypeStruct
+TAPS = (3, ROWS + 4, 16, 128)
+HELD = [
+    jax.ShapeDtypeStruct(shape, kind)
+    for shape, kind in (
+        (TAPS, BF16),
+        ((8, 128), F32),
+        ((128, DEPTH), BF16),
+        ((128, DEPTH), BF16),
+        ((64, DEPTH), BF16),
+        ((48, 256), BF16),
+        ((80, 384), BF16),
+        ((32, 256), BF16),
+        ((40, 128), F32),
+        ((ROWS, 2, 8, 128), F32),
+    )
+]
+
+
+def main_kernel(early, *refs):
+    rows_ref, mask_ref, *parameters = refs[0:8]
+    *held, wide_ref, narrow_ref, first_ref, third_ref = refs[8 if early else 19 :]
+    lat = lax.axis_index("lat")
+
+    @pl.when(lat <= 1 if early else lat > 1)
+    def _():
+        main_first(rows_ref, mask_ref, parameters, held, wide_ref, narrow_ref, first_ref)
+
+    @pl.when(lat == 0 if early else lat > 0)
+    def _():
+        main_rest(rows_ref, mask_ref, held, third_ref)
+
+
+def main_pass(rows, mask, parameters, held=(), message=()):
+    early = len(held) == 0
     return pl.pallas_call(
-        functools.partial(main_kernel, size),
-        out_shape=[
-            block(rows.shape, F32),
-            block((6, 8, 128), F32),
-            block((8, 128), F32),
-            *[block((n, DEPTH), BF16) for n in (128, 128, 64)],
-            *[block(shape, BF16) for shape in ((48, 256), (80, 384), (32, 256))],
-            block((40, 128), F32),
-        ],
-        in_specs=[VMEM] * 8,
+        functools.partial(main_kernel, early),
+        out_shape=HELD,
+        in_specs=[VMEM] * (8 + len(held)) + [pl.BlockSpec(memory_space=pl.ANY)] * len(message),
         out_specs=[VMEM] * 10,
         scratch_shapes=[
             pltpu.VMEM((2, 9, 16, 128), BF16),
             pltpu.VMEM((9, 8, 128), F32),
-            *[taps] * 3,
+            pltpu.VMEM(TAPS, BF16),
+            pltpu.VMEM(TAPS, BF16),
         ],
+        input_output_aliases={8 + i: i for i in range(len(held))},
         compiler_params=pltpu.CompilerParams(vmem_limit_bytes=LIMIT),
         cost_estimate=pl.CostEstimate(
-            flops=150000000, bytes_accessed=1500000, transcendentals=300000
+            flops=80000000, bytes_accessed=1500000, transcendentals=150000
         ),
-        name="main_pass",
-    )(rows, mask, *parameters)
+        name="main_early" if early else "main_late",
+    )(rows, mask, *parameters, *held, *message)
 
 
 def taps(rows, count):
@@ -479,7 +554,7 @@
             at = 2 * t + half
             corner = jnp.where(even, second_ref[6], first_ref[6])
             x = jnp.where(even, second_ref[at], first_ref[at])
-            y = beside(corner, 32 * half + 4 + 4 * t, corner, 32 * half + 20 + 4 * t)
+            y = beside(corner, 32 * half + 4 * t, corner, 32 * half + 16 + 4 * t)
             blocks[0].append(jnp.where(lat == 0, 0.0, x))
             blocks[1].append(jnp.where(lat == 0, 0.0, y))
             corner = jnp.where(even, first_ref[6], second_ref[6])
@@ -563,14 +638,17 @@
 def shards(state, land_mask, kernel_one, bias_one, kernel_two, bias_two, kernel_three, bias_three):
     lon, lat = (lax.axis_size("lon"), lax.axis_size("lat"))
     biases = [x.reshape(1, x.shape[0]) for x in (bias_one, bias_two, bias_three)]
-    rows, strip, outer, inner, mask, *parameters = prepare(
-        state, (land_mask, kernel_one, kernel_two, kernel_three, *biases)
-    )
-
-    inner = lax.ppermute(inner, "lon", [(i, i + 1 - 2 * (i % 2)) for i in range(lon)])
-    outer = lax.ppermute(outer, "lon", [(i, (i + 1 if i % 2 else i - 1) % lon) for i in range(lon)])
-    main, north, ocean, *weights, bias = main_pass(lat, rows, mask, parameters)
-    weights, late = weights[0:3], weights[3:6]
+    cells, outer, inner, *biases = small_edges(state, biases)
+
+    near = [(i, i + 1 - 2 * (i % 2)) for i in range(lon)]
+    far = [(i, (i + 1 if i % 2 else i - 1) % lon) for i in range(lon)]
+    inner = lax.ppermute(inner, "lon", near)
+    outer = lax.ppermute(outer, "lon", far)
+    rows, strip, all_outer, all_inner, north = rows_edges(lat, cells)
+    all_inner = lax.ppermute(all_inner, "lon", near)
+    all_outer = lax.ppermute(all_outer, "lon", far)
+    parameters = (kernel_one, kernel_two, kernel_three, *biases)
+    held = main_pass(rows, land_mask, parameters)
 
     def pairs(parity):
         result = []
@@ -583,13 +661,16 @@
                 result.append((i * lat + lat - 1, (lon - 1 - i) * lat + lat - 1))
         return result
 
-    first, second = corners(lat, rows, inner, outer, north)
+    first, second = corners(lat, rows, inner, outer, north, held[0])
+    held = main_pass(rows, land_mask, parameters, held, (second,))
+    _, ocean, *weights, bias, main = held
+    weights, late = weights[0:3], weights[3:6]
     first = lax.ppermute(first, ("lon", "lat"), pairs(0))
     second = lax.ppermute(second, ("lon", "lat"), pairs(1))
     cells, low, high, *own = strip_pass(
-        rows, strip, inner, outer, main, ocean, weights, bias
+        rows, strip, all_inner, all_outer, main, ocean, weights, bias
     )
-    return border_pass(rows, mask, first, second, *own, late, bias, cells, low, high)
+    return border_pass(rows, land_mask, first, second, *own, late, bias, cells, low, high)
 
 
 def solution(mesh):

time: 13 us -> 13.8 us (1.062)
  the two profiles are of different devices: /device:TPU:16 before, /device:TPU:0 now
where the time goes in v2:
time: 13.8 us; the launch traced here: 13.7 us
  Pallas kernels  6.75 us (49%)
  starting transfers between devices  5.52 us (40%)
  waiting for transfers between devices  1.34 us (10%)
    ppermute x1, starting transfers between devices, shards(): outer = lax.ppermute(outer, 'lon', far)  3.4 us
    pallas_call x2, Pallas kernels, main_pass(): pl.pallas_call(functools.partial(main_kernel, early), out_shape=HELD, in_...  1.87 us
    pallas_call x1, Pallas kernels, strip_pass(): pl.pallas_call(strip_kernel, out_shape=[block((16, ROWS - 8, 128), F32),...  1.8 us
    pallas_call x1, Pallas kernels, border_pass(): pl.pallas_call(border_kernel, out_shape=[block((16, ROWS, 128), F32), blo...  1.5 us
    ppermute x1, waiting for transfers between devices, shards(): first = lax.ppermute(first, ('lon', 'lat'), pairs(0))  1.19 us
    pallas_call x1, Pallas kernels, small_edges(): pl.pallas_call(small_kernel, out_shape=[block((16, PITCH, 128), F32), blo...  1.13 us
    ppermute x1, starting transfers between devices, shards(): all_outer = lax.ppermute(all_outer, 'lon', far)  0.8 us
    ppermute x1, starting transfers between devices, shards(): first = lax.ppermute(first, ('lon', 'lat'), pairs(0))  0.74 us
  transfers between devices with their start and end apart: 6, of which 2 were waited for; matrix products, arithmetic and copies ran while one was open for 0% of the time, Pallas kernels for 30%

profile of v2, /device:TPU:0, one launch (start us, length us, event | category | flops | bytes accessed | tf_op | source)
XLA Modules:
  0.0 13.7 jit_solution(15443663620406397101)
XLA Ops:
  0.0 1.1 %small_edges.1 = (f32[16,72,128]{2,1,0:T(8,128)S(1)}, f32[8,128]{1,0:T(8,128)S(1)}, f32[8,128]{1,0:T(8,128)S(1)}, f32[1,16]{1,0:T(1,128)S(1)}, f32[1,16]{1,0:T(1,128)S(1)}, /*index=5*/f32[1,8]{1,0:T(1,128)S(1)}) custom-call(f32[16,64,128]{2,1,0:T(8,128)} %state_ref.1, f32[1,16]{1,0:T(1,128)} %bitcast.3, f32[1,16]{1,0:T(1,128)} %bitcast.4, f32[1,8]{1,0:T(1,128)} %bitcast.5), custom_call_target="tpu_custom_call" | custom-call | flops 20000 | bytes 1000000 | tf_op jit(solution)/shard_map/small_edges/pallas_call | solution.py:128
  1.1 3.4 %collective-permute-start = (f32[8,128]{1,0:T(8,128)S(1)}, f32[8,128]{1,0:T(8,128)S(1)}, u32[]{:S(2)}, u32[]{:S(2)}) collective-permute-start(f32[8,128]{1,0:T(8,128)S(1)} %get-tuple-element.46), channel_id=1, source_target_pairs={{0,28},{4,8},{8,4},{12,16},{16,12},{20,24},{24,20},{28,0},{1,29},{... | collective-permute-start | bytes 12296 | tf_op jit(solution)/shard_map/ppermute | solution.py:646
  4.5 0.0 collective-permute-start.1
  4.5 0.0 copy-start
  4.5 0.0 copy-start.1
  4.5 0.0 copy-start.2
  4.6 0.0 copy-start.3
  4.6 0.4 %rows_edges.1 = (f32[64,2,8,128]{3,2,1,0:T(8,128)S(1)}, f32[8,2,8,128]{3,2,1,0:T(8,128)S(1)}, f32[4,8,128]{2,1,0:T(8,128)S(1)}, f32[4,8,128]{2,1,0:T(8,128)S(1)}, f32[6,8,128]{2,1,0:T(8,128)S(1)}) custom-call(f32[16,72,128]{2,1,0:T(8,128)S(1)} %get-tuple-element.44.cells_ref), custom_call_target="tpu_custom_call" | custom-call | flops 400000 | bytes 1200000 | tf_op jit(solution)/shard_map/rows_edges/pallas_call | solution.py:183
  4.9 0.8 %collective-permute-start.4 = (f32[4,8,128]{2,1,0:T(8,128)S(1)}, f32[4,8,128]{2,1,0:T(8,128)S(1)}, u32[]{:S(2)}, u32[]{:S(2)}) collective-permute-start(f32[4,8,128]{2,1,0:T(8,128)S(1)} %get-tuple-element.56), channel_id=1, source_target_pairs={{0,28},{4,8},{8,4},{12,16},{16,12},{20,24},{24,20},{28,0},{1,29},{... | collective-permute-start | bytes 49160 | tf_op jit(solution)/shard_map/ppermute | solution.py:649
  5.7 0.6 %collective-permute-start.5 = (f32[4,8,128]{2,1,0:T(8,128)S(1)}, f32[4,8,128]{2,1,0:T(8,128)S(1)}, u32[]{:S(2)}, u32[]{:S(2)}) collective-permute-start(f32[4,8,128]{2,1,0:T(8,128)S(1)} %get-tuple-element.57), channel_id=1, source_target_pairs={{0,4},{4,0},{8,12},{12,8},{16,20},{20,16},{24,28},{28,24},{1,5},{5... | collective-permute-start | bytes 49160 | tf_op jit(solution)/shard_map/ppermute | solution.py:648
  6.3 0.0 copy-done
  6.3 0.0 copy-done.1
  6.3 0.0 copy-done.2
  6.3 0.0 copy-done.3
  6.3 1.9 %main_early.1 = (bf16[3,68,16,128]{3,2,1,0:T(8,128)(2,1)S(1)}, f32[8,128]{1,0:T(8,128)S(1)}, bf16[128,512]{1,0:T(8,128)(2,1)S(1)}, bf16[128,512]{1,0:T(8,128)(2,...) custom-call(f32[64,2,8,128]{3,2,1,0:T(8,128)S(1)} %get-tuple-element, ...), custom_call_target="tpu_custom_call" | custom-call | flops 80000000 | bytes 1500000 | tf_op jit(solution)/shard_map/main_early/pallas_call | solution.py:390
  8.2 0.0 collective-permute-done.outer_ref
  8.2 0.0 collective-permute-done.1.inner_ref
  8.2 0.1 add_corners.1
  8.3 0.7 %collective-permute-start.2 = (f32[7,8,128]{2,1,0:T(8,128)S(1)}, f32[7,8,128]{2,1,0:T(8,128)S(1)}, u32[]{:S(2)}, u32[]{:S(2)}) collective-permute-start(f32[7,8,128]{2,1,0:T(8,128)S(1)} %get-tuple-element.53), channel_id=1, source_target_pairs={{0,1},{1,0},{2,3},{3,2},{4,5},{5,4},{6,7},{7,6},{8,9},{9,8},{10,11... | collective-permute-start | bytes 86024 | tf_op jit(solution)/shard_map/ppermute | solution.py:668
  9.1 0.0 collective-permute-start.3
  9.1 0.1 collective-permute-done.4.outer_ref
  9.2 0.0 collective-permute-done.5.inner_ref
  9.2 1.8 %strip_pass.1 = (f32[16,56,128]{2,1,0:T(8,128)S(1)}, f32[16,8,128]{2,1,0:T(8,128)S(1)}, f32[16,8,128]{2,1,0:T(8,128)S(1)}, f32[6,2,8,128]{3,2,1,0:T(8,128)S(1)},...) custom-call(f32[64,2,8,128]{3,2,1,0:T(8,128)S(1)} %get-tuple-element.45.refs_0_.rows_ref, ...), custom_call_target="tpu_custom_call" | custom-call | flops 150000000 | bytes 2000000 | tf_op jit(solution)/shard_map/strip_pass/pallas_call | solution.py:519
  11.0 1.2 %collective-permute-done.2.first_ref = f32[7,8,128]{2,1,0:T(8,128)S(1)} collective-permute-done((f32[7,8,128]{2,1,0:T(8,128)S(1)}, f32[7,8,128]{2,1,0:T(8,128)S(1)}, u32[]{:S(2)}, u32[]{:S(2)}) %collective-permute-start.2) | collective-permute-done | bytes 28704 | tf_op jit(solution)/shard_map/ppermute | solution.py:668
  12.2 0.0 collective-permute-done.3.second_ref
  12.2 1.5 %border_pass.1 = (f32[16,64,128]{2,1,0:T(8,128)}, f32[16,8,128]{2,1,0:T(8,128)S(1)}, f32[16,8,128]{2,1,0:T(8,128)S(1)}) custom-call(f32[64,2,8,128]{3,2,1,0:T(8,128)S(1)} %get-tuple-element.45.refs_0_.rows_ref, s32[64,128]{1,0:T(8,128)S(1)} %copy-done, ...), custom_call_target="tpu_custom_call", output_to_operand_aliasing={{1}: (12, {}), {2}: (13, {})} | custom-call | flops 60000000 | bytes 1000000 | tf_op jit(solution)/shard_map/border_pass/pallas_call | solution.py:624
  (1 shorter events, 0.0 us)
Async XLA Ops:
  1.1 7.1 %collective-permute-start = (f32[8,128]{1,0:T(8,128)S(1)}, f32[8,128]{1,0:T(8,128)S(1)}, u32[]{:S(2)}, u32[]{:S(2)}) collective-permute-start(f32[8,128]{1,0:T(8,128)S(1)} %get-tuple-element.46), channel_id=1, source_target_pairs={{0,28},{4,8},{8,4},{12,16},{16,12},{20,24},{24,20},{28,0},{1,29},{... | collective-permute-start | bytes 12296 | tf_op jit(solution)/shard_map/ppermute | solution.py:646
  4.5 3.7 %collective-permute-start.1 = (f32[8,128]{1,0:T(8,128)S(1)}, f32[8,128]{1,0:T(8,128)S(1)}, u32[]{:S(2)}, u32[]{:S(2)}) collective-permute-start(f32[8,128]{1,0:T(8,128)S(1)} %get-tuple-element.47), channel_id=1, source_target_pairs={{0,4},{4,0},{8,12},{12,8},{16,20},{20,16},{24,28},{28,24},{1,5},{5... | collective-permute-start | bytes 12296 | tf_op jit(solution)/shard_map/ppermute | solution.py:645
  4.5 1.8 %copy-start = (s32[64,128]{1,0:T(8,128)S(1)}, s32[64,128]{1,0:T(8,128)}, u32[]{:S(2)}) copy-start(s32[64,128]{1,0:T(8,128)} %mask_ref.1) | copy-start | bytes 98308
  4.5 1.8 %copy-start.1 = (bf16[3,3,16,16]{3,2,1,0:T(8,128)(2,1)S(1)}, bf16[3,3,16,16]{3,2,1,0:T(8,128)(2,1)}, u32[]{:S(2)}) copy-start(bf16[3,3,16,16]{3,2,1,0:T(8,128)(2,1)} %refs_2_.3) | copy-start | bytes 13828
  4.5 1.8 %copy-start.2 = (bf16[3,3,16,16]{3,2,1,0:T(8,128)(2,1)S(1)}, bf16[3,3,16,16]{3,2,1,0:T(8,128)(2,1)}, u32[]{:S(2)}) copy-start(bf16[3,3,16,16]{3,2,1,0:T(8,128)(2,1)} %refs_3_.3) | copy-start | bytes 13828
  4.6 1.8 %copy-start.3 = (bf16[3,3,8,16]{3,2,1,0:T(8,128)(2,1)S(1)}, bf16[3,3,8,16]{3,2,1,0:T(8,128)(2,1)}, u32[]{:S(2)}) copy-start(bf16[3,3,8,16]{3,2,1,0:T(8,128)(2,1)} %refs_4_.3) | copy-start | bytes 6916
  4.9 4.3 %collective-permute-start.4 = (f32[4,8,128]{2,1,0:T(8,128)S(1)}, f32[4,8,128]{2,1,0:T(8,128)S(1)}, u32[]{:S(2)}, u32[]{:S(2)}) collective-permute-start(f32[4,8,128]{2,1,0:T(8,128)S(1)} %get-tuple-element.56), channel_id=1, source_target_pairs={{0,28},{4,8},{8,4},{12,16},{16,12},{20,24},{24,20},{28,0},{1,29},{... | collective-permute-start | bytes 49160 | tf_op jit(solution)/shard_map/ppermute | solution.py:649
  5.7 3.5 %collective-permute-start.5 = (f32[4,8,128]{2,1,0:T(8,128)S(1)}, f32[4,8,128]{2,1,0:T(8,128)S(1)}, u32[]{:S(2)}, u32[]{:S(2)}) collective-permute-start(f32[4,8,128]{2,1,0:T(8,128)S(1)} %get-tuple-element.57), channel_id=1, source_target_pairs={{0,4},{4,0},{8,12},{12,8},{16,20},{20,16},{24,28},{28,24},{1,5},{5... | collective-permute-start | bytes 49160 | tf_op jit(solution)/shard_map/ppermute | solution.py:648
  8.3 3.9 %collective-permute-start.2 = (f32[7,8,128]{2,1,0:T(8,128)S(1)}, f32[7,8,128]{2,1,0:T(8,128)S(1)}, u32[]{:S(2)}, u32[]{:S(2)}) collective-permute-start(f32[7,8,128]{2,1,0:T(8,128)S(1)} %get-tuple-element.53), channel_id=1, source_target_pairs={{0,1},{1,0},{2,3},{3,2},{4,5},{5,4},{6,7},{7,6},{8,9},{9,8},{10,11... | collective-permute-start | bytes 86024 | tf_op jit(solution)/shard_map/ppermute | solution.py:668
  9.1 3.1 %collective-permute-start.3 = (f32[7,8,128]{2,1,0:T(8,128)S(1)}, f32[7,8,128]{2,1,0:T(8,128)S(1)}, u32[]{:S(2)}, u32[]{:S(2)}) collective-permute-start(f32[7,8,128]{2,1,0:T(8,128)S(1)} %get-tuple-element.54.refs_18_), channel_id=1, source_target_pairs={{1,2},{2,1},{0,4},{3,31},{5,6},{6,5},{4,0},{7,27},{9,10},{10,9},{8... | collective-permute-start | bytes 86024 | tf_op jit(solution)/shard_map/ppermute | solution.py:669

commit v3 on v1

--- a/solution.py
+++ b/solution.py
@@ -30,6 +30,10 @@
         if by == 0:
             return x
     return pltpu.roll(x, by, x.ndim - 1)
+
+
+def load_row(flat, row, half):
+    return flat[pl.ds(8 * PITCH * half + row, 8, stride=PITCH), :]
 
 
 def silu(v):
@@ -84,16 +88,12 @@
     return jnp.concatenate(result, axis=0)
 
 
-def prepare_kernel(state_ref, *refs):
-    others, refs = refs[0:7], refs[7:]
-    rows_ref, strip_ref, outer_ref, inner_ref, *held, cells_ref, sems = refs
+def edges_kernel(state_ref, cells_ref, strip_ref, outer_ref, inner_ref, sems):
     fetches = []
-    for at in range(0, 16, 2):
-        span = pl.ds(at, 2)
+    for half in range(2):
+        span = pl.ds(8 * half, 8)
         target = cells_ref.at[span, pl.ds(0, ROWS), :]
-        fetches.append(pltpu.make_async_copy(state_ref.at[span], target, sems.at[len(fetches)]))
-    for source, target in zip(others, held):
-        fetches.append(pltpu.make_async_copy(source, target, sems.at[len(fetches)]))
+        fetches.append(pltpu.make_async_copy(state_ref.at[span], target, sems.at[half]))
     for fetch in fetches:
         fetch.start()
 
@@ -105,14 +105,13 @@
         [jnp.where(even, (4 * s - a) % 128, (4 * s - b) % 128) for s in range(4)]
         for a, b in ((6, 3), (3, 6))
     ]
-    for fetch in fetches[0:8]:
+    for fetch in fetches:
         fetch.wait()
     for half in range(2):
         strip = [jnp.zeros((8, 128), F32)] * 8
         for b in range(8):
             for r in range(8):
-                x = flat[pl.ds(8 * PITCH * half + 8 * b + r, 8, stride=PITCH), :]
-                rows_ref[8 * b + r, half] = x
+                x = load_row(flat, 8 * b + r, half)
                 strip[r] = jnp.where(group == b, turn(x, 6 + 16 * b), strip[r])
         for r in range(8):
             strip_ref[r, half] = strip[r]
@@ -122,29 +121,25 @@
                 for s in range(4):
                     value = jnp.where(part == s, turn(strip[4 * q + s], shift[s]), value)
                 target[2 * q + half] = value
-    for fetch in fetches[8:]:
-        fetch.wait()
-
-
-def prepare(state, others):
+
+
+def edges(state):
     block = jax.ShapeDtypeStruct
-    arrays = [pltpu.with_memory_space_constraint(x, pltpu.HBM) for x in (state, *others)]
     return pl.pallas_call(
-        prepare_kernel,
+        edges_kernel,
         out_shape=[
-            block((ROWS, 2, 8, 128), F32),
+            block((16, PITCH, 128), F32),
             block((8, 2, 8, 128), F32),
             block((4, 8, 128), F32),
             block((4, 8, 128), F32),
-            *[block(x.shape, x.dtype) for x in others],
         ],
-        in_specs=[HBM] * 8,
-        out_specs=[VMEM] * 11,
-        scratch_shapes=[pltpu.VMEM((16, PITCH, 128), F32), pltpu.SemaphoreType.DMA((15,))],
+        in_specs=[HBM],
+        out_specs=[VMEM] * 4,
+        scratch_shapes=[pltpu.SemaphoreType.DMA((2,))],
         compiler_params=pltpu.CompilerParams(vmem_limit_bytes=LIMIT),
         cost_estimate=pl.CostEstimate(flops=400000, bytes_accessed=1200000, transcendentals=0),
-        name="rows_edges",
-    )(*arrays)
+        name="tile_edges",
+    )(pltpu.with_memory_space_constraint(state, pltpu.HBM))
 
 
 def corners_kernel(size, rows_ref, outer_ref, inner_ref, north_ref, first_ref, second_ref):
@@ -219,33 +214,33 @@
 
 
 def main_kernel(
-    size, rows_ref, mask_ref, k_one_ref, k_two_ref, k_three_ref, b_one_ref, b_two_ref, b_three_ref,
-    out_ref, north_ref, ocean_ref, one_ref, two_ref, three_ref,
+    size, cells_ref, mask_ref, k_one_ref, k_two_ref, k_three_ref, b_one_ref, b_two_ref, b_three_ref,
+    rows_ref, out_ref, north_ref, ocean_ref, one_ref, two_ref, three_ref,
     late_one_ref, late_two_ref, late_three_ref, bias_ref,
-    wide_ref, narrow_ref, first_ref, second_ref, third_ref,
+    wide_ref, narrow_ref, first_ref, second_ref, third_ref, s_one_ref, s_two_ref, s_three_ref, sems,
 ):
+    flat = cells_ref.reshape(16 * PITCH, 128)
+    scalars = (s_one_ref, s_two_ref, s_three_ref)
+    fetches = [
+        pltpu.make_async_copy(source, target, sems.at[i])
+        for i, (source, target) in enumerate(zip((b_one_ref, b_two_ref, b_three_ref), scalars))
+    ]
+    for fetch in fetches:
+        fetch.start()
+
     top = lax.axis_index("lat") == size - 1
     col = lanes()
     for t in range(3):
         for half in range(2):
-            folded = jnp.take_along_axis(rows_ref[ROWS - 1 - t, half], 127 - col, axis=1)
+            folded = jnp.take_along_axis(load_row(flat, ROWS - 1 - t, half), 127 - col, axis=1)
             folded = -folded if half == 0 else folded
-            north_ref[2 * t + half] = jnp.where(top, folded, rows_ref[ROWS - 3 + t, half])
+            north_ref[2 * t + half] = jnp.where(top, folded, load_row(flat, ROWS - 3 + t, half))
     ocean = jnp.zeros((8, 128), F32)
     for b in range(8):
         x = 0.1 * mask_ref[8 * b : 8 * b + 8, :].astype(F32)
         ocean = jnp.where(col // 16 == b, turn(x, 6 + 16 * b), ocean)
     ocean_ref[...] = ocean
 
-    biases = []
-    at = 0
-    for ref in (b_one_ref, b_two_ref, b_three_ref):
-        n = ref.shape[1]
-        same = lax.broadcasted_iota(jnp.int32, (n, n), 0) == lax.broadcasted_iota(jnp.int32, (n, n), 1)
-        column = jnp.sum(jnp.where(same, ref[...], 0.0), axis=1, keepdims=True)
-        biases.append(jnp.broadcast_to(column, (n, 128)))
-        bias_ref[at : at + n, :] = biases[-1]
-        at += n
     band(k_one_ref, wide_ref.at[0], one_ref)
     band(k_two_ref, wide_ref.at[1], two_ref)
     band(k_three_ref, narrow_ref, three_ref)
@@ -258,9 +253,26 @@
                 ref[c, row] = jnp.zeros((16, 128), BF16)
 
     for row in range(ROWS):
-        x = jnp.concatenate([rows_ref[row, 0], rows_ref[row, 1]], axis=0).astype(BF16)
+        x = [load_row(flat, row, half) for half in range(2)]
+        for half in range(2):
+            rows_ref[row, half] = x[half]
+        x = jnp.concatenate(x, axis=0).astype(BF16)
         for c in range(3):
             first_ref[c, row + 1] = turn(x, 1 - c)
+
+    for fetch in fetches:
+        fetch.wait()
+    biases = []
+    at = 0
+    for ref in scalars:
+        n = ref.shape[0]
+        sub = lax.broadcasted_iota(jnp.int32, (n, 128), 0)
+        value = jnp.zeros((n, 128), F32)
+        for o in range(n):
+            value = jnp.where(sub == o, ref[o], value)
+        biases.append(value)
+        bias_ref[at : at + n, :] = value
+        at += n
 
     def layer(source, weights, at):
         parts = []
@@ -304,32 +316,35 @@
                     out_ref[row, half] = q[half] + ocean * new[half]
 
 
-def main_pass(size, rows, mask, parameters):
+def main_pass(size, cells, mask, kernels, biases):
     taps = pltpu.VMEM((3, ROWS + 4, 16, 128), BF16)
     block = jax.ShapeDtypeStruct
     return pl.pallas_call(
         functools.partial(main_kernel, size),
         out_shape=[
-            block(rows.shape, F32),
+            block((ROWS, 2, 8, 128), F32),
+            block((ROWS, 2, 8, 128), F32),
             block((6, 8, 128), F32),
             block((8, 128), F32),
             *[block((n, DEPTH), BF16) for n in (128, 128, 64)],
             *[block(shape, BF16) for shape in ((48, 256), (80, 384), (32, 256))],
             block((40, 128), F32),
         ],
-        in_specs=[VMEM] * 8,
-        out_specs=[VMEM] * 10,
+        in_specs=[VMEM] * 5 + [HBM] * 3,
+        out_specs=[VMEM] * 11,
         scratch_shapes=[
             pltpu.VMEM((2, 9, 16, 128), BF16),
             pltpu.VMEM((9, 8, 128), F32),
             *[taps] * 3,
+            *[pltpu.SMEM(x.shape, F32) for x in biases],
+            pltpu.SemaphoreType.DMA((3,)),
         ],
         compiler_params=pltpu.CompilerParams(vmem_limit_bytes=LIMIT),
         cost_estimate=pl.CostEstimate(
             flops=150000000, bytes_accessed=1500000, transcendentals=300000
         ),
         name="main_pass",
-    )(rows, mask, *parameters)
+    )(cells, mask, *kernels, *[pltpu.with_memory_space_constraint(x, pltpu.HBM) for x in biases])
 
 
 def taps(rows, count):
@@ -562,14 +577,13 @@
 
 def shards(state, land_mask, kernel_one, bias_one, kernel_two, bias_two, kernel_three, bias_three):
     lon, lat = (lax.axis_size("lon"), lax.axis_size("lat"))
-    biases = [x.reshape(1, x.shape[0]) for x in (bias_one, bias_two, bias_three)]
-    rows, strip, outer, inner, mask, *parameters = prepare(
-        state, (land_mask, kernel_one, kernel_two, kernel_three, *biases)
-    )
+    cells, strip, outer, inner = edges(state)
 
     inner = lax.ppermute(inner, "lon", [(i, i + 1 - 2 * (i % 2)) for i in range(lon)])
     outer = lax.ppermute(outer, "lon", [(i, (i + 1 if i % 2 else i - 1) % lon) for i in range(lon)])
-    main, north, ocean, *weights, bias = main_pass(lat, rows, mask, parameters)
+    rows, main, north, ocean, *weights, bias = main_pass(
+        lat, cells, land_mask, (kernel_one, kernel_two, kernel_three), (bias_one, bias_two, bias_three)
+    )
     weights, late = weights[0:3], weights[3:6]
 
     def pairs(parity):
@@ -589,7 +603,7 @@
     cells, low, high, *own = strip_pass(
         rows, strip, inner, outer, main, ocean, weights, bias
     )
-    return border_pass(rows, mask, first, second, *own, late, bias, cells, low, high)
+    return border_pass(rows, land_mask, first, second, *own, late, bias, cells, low, high)
 
 
 def solution(mesh):

time: 13 us -> 13.2 us (1.015)
  Pallas kernels: 6.61 us -> 7.4 us
  waiting for transfers between devices: 2.63 us -> 2.07 us
    pallas_call x2, Pallas kernels: 3.23 us -> 4.01 us  [the longest x1 2.58 us: main_pass(): pl.pallas_call(functools.partial(main_kernel, size), out_shape=[block((RO...]
    ppermute x1, waiting for transfers between devices: 0.57 us -> 0.01 us  [shards(): lax.ppermute(outer, 'lon', [(i, (i + 1 if i % 2 else i - 1) % lon) for i...]
  transfers between devices with their start and end apart: 4 -> 4, of which waited for: 3 -> 2; matrix products, arithmetic and copies ran while one was open for 0% -> 0% of each run, Pallas kernels for 27% -> 33%
where the time goes in v3:
time: 13.2 us; the launch traced here: 13.1 us
  Pallas kernels  7.4 us (56%)
  starting transfers between devices  3.54 us (27%)
  waiting for transfers between devices  2.07 us (16%)
    pallas_call x1, Pallas kernels, main_pass(): pl.pallas_call(functools.partial(main_kernel, size), out_shape=[block((RO...  2.58 us
    ppermute x1, starting transfers between devices, shards(): lax.ppermute(outer, 'lon', [(i, (i + 1 if i % 2 else i - 1) % lon) for i...  1.95 us
    pallas_call x1, Pallas kernels, strip_pass(): pl.pallas_call(strip_kernel, out_shape=[block((16, ROWS - 8, 128), F32),...  1.8 us
    ppermute x1, starting transfers between devices, shards(): first = lax.ppermute(first, ('lon', 'lat'), pairs(0))  1.59 us
    ppermute x1, waiting for transfers between devices, shards(): second = lax.ppermute(second, ('lon', 'lat'), pairs(1))  1.58 us
    pallas_call x1, Pallas kernels, border_pass(): pl.pallas_call(border_kernel, out_shape=[block((16, ROWS, 128), F32), blo...  1.49 us
    pallas_call x1, Pallas kernels, edges(): pl.pallas_call(edges_kernel, out_shape=[block((16, PITCH, 128), F32), blo...  1.43 us
    ppermute x1, waiting for transfers between devices, shards(): first = lax.ppermute(first, ('lon', 'lat'), pairs(0))  0.48 us
  transfers between devices with their start and end apart: 4, of which 2 were waited for; matrix products, arithmetic and copies ran while one was open for 0% of the time, Pallas kernels for 33%

profile of v3, /device:TPU:16, one launch (start us, length us, event | category | flops | bytes accessed | tf_op | source)
XLA Modules:
  0.0 13.1 jit_solution(13311892727835889046)
XLA Ops:
  0.0 0.0 copy-start.1
  0.0 0.0 copy-start.2
  0.0 0.0 copy-start
  0.0 0.0 copy-start.3
  0.0 1.4 %tile_edges.1 = (f32[16,72,128]{2,1,0:T(8,128)S(1)}, f32[8,2,8,128]{3,2,1,0:T(8,128)S(1)}, f32[4,8,128]{2,1,0:T(8,128)S(1)}, f32[4,8,128]{2,1,0:T(8,128)S(1)}) custom-call(f32[16,64,128]{2,1,0:T(8,128)} %state_ref.1), custom_call_target="tpu_custom_call" | custom-call | flops 400000 | bytes 1200000 | tf_op jit(solution)/shard_map/tile_edges/pallas_call | solution.py:128
  1.5 2.0 %collective-permute-start = (f32[4,8,128]{2,1,0:T(8,128)S(1)}, f32[4,8,128]{2,1,0:T(8,128)S(1)}, u32[]{:S(2)}, u32[]{:S(2)}) collective-permute-start(f32[4,8,128]{2,1,0:T(8,128)S(1)} %get-tuple-element.31), channel_id=1, source_target_pairs={{0,28},{4,8},{8,4},{12,16},{16,12},{20,24},{24,20},{28,0},{1,29},{... | collective-permute-start | bytes 49160 | tf_op jit(solution)/shard_map/ppermute | solution.py:583
  3.4 0.0 collective-permute-start.1
  3.4 0.0 copy-done.1
  3.4 0.0 copy-done.2
  3.4 0.0 copy-done
  3.4 0.0 copy-done.3
  3.4 2.6 %main_pass.1 = (f32[64,2,8,128]{3,2,1,0:T(8,128)S(1)}, f32[64,2,8,128]{3,2,1,0:T(8,128)S(1)}, f32[6,8,128]{2,1,0:T(8,128)S(1)}, f32[8,128]{1,0:T(8,128)S(1)}, bf...) custom-call(f32[16,72,128]{2,1,0:T(8,128)S(1)} %get-tuple-element.29, ...), custom_call_target="tpu_custom_call" | custom-call | flops 150000000 | bytes 1500000 | tf_op jit(solution)/shard_map/main_pass/pallas_call | solution.py:322
  6.0 0.0 collective-permute-done.outer_ref
  6.0 0.0 collective-permute-done.1.inner_ref
  6.0 0.1 add_corners.1
  6.1 1.6 %collective-permute-start.2 = (f32[7,8,128]{2,1,0:T(8,128)S(1)}, f32[7,8,128]{2,1,0:T(8,128)S(1)}, u32[]{:S(2)}, u32[]{:S(2)}) collective-permute-start(f32[7,8,128]{2,1,0:T(8,128)S(1)} %get-tuple-element.34), channel_id=1, source_target_pairs={{0,1},{1,0},{2,3},{3,2},{4,5},{5,4},{6,7},{7,6},{8,9},{9,8},{10,11... | collective-permute-start | bytes 86024 | tf_op jit(solution)/shard_map/ppermute | solution.py:601
  7.7 0.0 collective-permute-start.3
  7.7 1.8 %strip_pass.1 = (f32[16,56,128]{2,1,0:T(8,128)S(1)}, f32[16,8,128]{2,1,0:T(8,128)S(1)}, f32[16,8,128]{2,1,0:T(8,128)S(1)}, f32[6,2,8,128]{3,2,1,0:T(8,128)S(1)},...) custom-call(f32[64,2,8,128]{3,2,1,0:T(8,128)S(1)} %get-tuple-element.30.rows_ref, ...), custom_call_target="tpu_custom_call" | custom-call | flops 150000000 | bytes 2000000 | tf_op jit(solution)/shard_map/strip_pass/pallas_call | solution.py:459
  9.5 0.5 %collective-permute-done.2.first_ref = f32[7,8,128]{2,1,0:T(8,128)S(1)} collective-permute-done((f32[7,8,128]{2,1,0:T(8,128)S(1)}, f32[7,8,128]{2,1,0:T(8,128)S(1)}, u32[]{:S(2)}, u32[]{:S(2)}) %collective-permute-start.2) | collective-permute-done | bytes 28704 | tf_op jit(solution)/shard_map/ppermute | solution.py:601
  10.0 1.6 %collective-permute-done.3.second_ref = f32[7,8,128]{2,1,0:T(8,128)S(1)} collective-permute-done((f32[7,8,128]{2,1,0:T(8,128)S(1)}, f32[7,8,128]{2,1,0:T(8,128)S(1)}, u32[]{:S(2)}, u32[]{:S(2)}) %collective-permute-start.3) | collective-permute-done | bytes 28704 | tf_op jit(solution)/shard_map/ppermute | solution.py:602
  11.6 1.5 %border_pass.1 = (f32[16,64,128]{2,1,0:T(8,128)}, f32[16,8,128]{2,1,0:T(8,128)S(1)}, f32[16,8,128]{2,1,0:T(8,128)S(1)}) custom-call(f32[64,2,8,128]{3,2,1,0:T(8,128)S(1)} %get-tuple-element.30.rows_ref, s32[64,128]{1,0:T(8,128)S(1)} %copy-done, f32[7,8,128]{2,1,0:T(8,128)S(1)} %collective-permute-done.2.first_ref, ...), custom_call_target="tpu_custom_call", output_to_operand_aliasing={{1}: (12, {}), {2}: (13, {})} | custom-call | flops 60000000 | bytes 1000000 | tf_op jit(solution)/shard_map/border_pass/pallas_call | solution.py:564
Async XLA Ops:
  0.0 3.4 %copy-start.1 = (bf16[3,3,16,16]{3,2,1,0:T(8,128)(2,1)S(1)}, bf16[3,3,16,16]{3,2,1,0:T(8,128)(2,1)}, u32[]{:S(2)}) copy-start(bf16[3,3,16,16]{3,2,1,0:T(8,128)(2,1)} %k_one_ref.1) | copy-start | bytes 13828
  0.0 3.4 %copy-start.2 = (bf16[3,3,16,16]{3,2,1,0:T(8,128)(2,1)S(1)}, bf16[3,3,16,16]{3,2,1,0:T(8,128)(2,1)}, u32[]{:S(2)}) copy-start(bf16[3,3,16,16]{3,2,1,0:T(8,128)(2,1)} %k_two_ref.1) | copy-start | bytes 13828
  0.0 3.4 %copy-start = (s32[64,128]{1,0:T(8,128)S(1)}, s32[64,128]{1,0:T(8,128)}, u32[]{:S(2)}) copy-start(s32[64,128]{1,0:T(8,128)} %mask_ref.3) | copy-start | bytes 98308
  0.0 3.4 %copy-start.3 = (bf16[3,3,8,16]{3,2,1,0:T(8,128)(2,1)S(1)}, bf16[3,3,8,16]{3,2,1,0:T(8,128)(2,1)}, u32[]{:S(2)}) copy-start(bf16[3,3,8,16]{3,2,1,0:T(8,128)(2,1)} %k_three_ref.1) | copy-start | bytes 6916
  1.5 4.6 %collective-permute-start = (f32[4,8,128]{2,1,0:T(8,128)S(1)}, f32[4,8,128]{2,1,0:T(8,128)S(1)}, u32[]{:S(2)}, u32[]{:S(2)}) collective-permute-start(f32[4,8,128]{2,1,0:T(8,128)S(1)} %get-tuple-element.31), channel_id=1, source_target_pairs={{0,28},{4,8},{8,4},{12,16},{16,12},{20,24},{24,20},{28,0},{1,29},{... | collective-permute-start | bytes 49160 | tf_op jit(solution)/shard_map/ppermute | solution.py:583
  3.4 2.6 %collective-permute-start.1 = (f32[4,8,128]{2,1,0:T(8,128)S(1)}, f32[4,8,128]{2,1,0:T(8,128)S(1)}, u32[]{:S(2)}, u32[]{:S(2)}) collective-permute-start(f32[4,8,128]{2,1,0:T(8,128)S(1)} %get-tuple-element.32), channel_id=1, source_target_pairs={{0,4},{4,0},{8,12},{12,8},{16,20},{20,16},{24,28},{28,24},{1,5},{5... | collective-permute-start | bytes 49160 | tf_op jit(solution)/shard_map/ppermute | solution.py:582
  6.1 3.9 %collective-permute-start.2 = (f32[7,8,128]{2,1,0:T(8,128)S(1)}, f32[7,8,128]{2,1,0:T(8,128)S(1)}, u32[]{:S(2)}, u32[]{:S(2)}) collective-permute-start(f32[7,8,128]{2,1,0:T(8,128)S(1)} %get-tuple-element.34), channel_id=1, source_target_pairs={{0,1},{1,0},{2,3},{3,2},{4,5},{5,4},{6,7},{7,6},{8,9},{9,8},{10,11... | collective-permute-start | bytes 86024 | tf_op jit(solution)/shard_map/ppermute | solution.py:601
  7.7 3.9 %collective-permute-start.3 = (f32[7,8,128]{2,1,0:T(8,128)S(1)}, f32[7,8,128]{2,1,0:T(8,128)S(1)}, u32[]{:S(2)}, u32[]{:S(2)}) collective-permute-start(f32[7,8,128]{2,1,0:T(8,128)S(1)} %get-tuple-element.35), channel_id=1, source_target_pairs={{1,2},{2,1},{0,4},{3,31},{5,6},{6,5},{4,0},{7,27},{9,10},{10,9},{8... | collective-permute-start | bytes 86024 | tf_op jit(solution)/shard_map/ppermute | solution.py:602

commit v4 on v1

--- a/solution.py
+++ b/solution.py
@@ -84,18 +84,20 @@
     return jnp.concatenate(result, axis=0)
 
 
-def prepare_kernel(state_ref, *refs):
-    others, refs = refs[0:7], refs[7:]
-    rows_ref, strip_ref, outer_ref, inner_ref, *held, cells_ref, sems = refs
+def prepare_kernel(
+    state_ref, b_one_ref, b_two_ref, b_three_ref,
+    rows_ref, strip_ref, outer_ref, inner_ref, h_one_ref, h_two_ref, h_three_ref, cells_ref, sems,
+):
     fetches = []
-    for at in range(0, 16, 2):
-        span = pl.ds(at, 2)
+    for half in range(2):
+        span = pl.ds(8 * half, 8)
         target = cells_ref.at[span, pl.ds(0, ROWS), :]
-        fetches.append(pltpu.make_async_copy(state_ref.at[span], target, sems.at[len(fetches)]))
-    for source, target in zip(others, held):
+        fetches.append(pltpu.make_async_copy(state_ref.at[span], target, sems.at[half]))
+    biases = ((b_one_ref, h_one_ref), (b_two_ref, h_two_ref), (b_three_ref, h_three_ref))
+    for source, target in biases:
         fetches.append(pltpu.make_async_copy(source, target, sems.at[len(fetches)]))
-    for fetch in fetches:
-        fetch.start()
+    for i, fetch in enumerate(fetches):
+        fetch.start(priority=i % 2)
 
     flat = cells_ref.reshape(16 * PITCH, 128)
     group = lanes() // 16
@@ -105,7 +107,7 @@
         [jnp.where(even, (4 * s - a) % 128, (4 * s - b) % 128) for s in range(4)]
         for a, b in ((6, 3), (3, 6))
     ]
-    for fetch in fetches[0:8]:
+    for fetch in fetches:
         fetch.wait()
     for half in range(2):
         strip = [jnp.zeros((8, 128), F32)] * 8
@@ -122,13 +124,11 @@
                 for s in range(4):
                     value = jnp.where(part == s, turn(strip[4 * q + s], shift[s]), value)
                 target[2 * q + half] = value
-    for fetch in fetches[8:]:
-        fetch.wait()
-
-
-def prepare(state, others):
+
+
+def prepare(state, biases):
     block = jax.ShapeDtypeStruct
-    arrays = [pltpu.with_memory_space_constraint(x, pltpu.HBM) for x in (state, *others)]
+    arrays = [pltpu.with_memory_space_constraint(x, pltpu.HBM) for x in (state, *biases)]
     return pl.pallas_call(
         prepare_kernel,
         out_shape=[
@@ -136,11 +136,11 @@
             block((8, 2, 8, 128), F32),
             block((4, 8, 128), F32),
             block((4, 8, 128), F32),
-            *[block(x.shape, x.dtype) for x in others],
+            *[block(x.shape, F32) for x in biases],
         ],
-        in_specs=[HBM] * 8,
-        out_specs=[VMEM] * 11,
-        scratch_shapes=[pltpu.VMEM((16, PITCH, 128), F32), pltpu.SemaphoreType.DMA((15,))],
+        in_specs=[HBM] * 4,
+        out_specs=[VMEM] * 7,
+        scratch_shapes=[pltpu.VMEM((16, PITCH, 128), F32), pltpu.SemaphoreType.DMA((5,))],
         compiler_params=pltpu.CompilerParams(vmem_limit_bytes=LIMIT),
         cost_estimate=pl.CostEstimate(flops=400000, bytes_accessed=1200000, transcendentals=0),
         name="rows_edges",
@@ -538,7 +538,7 @@
             for half in range(2):
                 flat[pl.ds(64 * half + row - at, 8, stride=8), :] = q[half] + ocean * new[half]
         store = pltpu.make_async_copy(ref, out_ref.at[:, pl.ds(at, 8), :], sems.at[1 + strip])
-        store.start()
+        store.start(priority=strip)
         stores.append(store)
     for store in stores:
         store.wait()
@@ -563,13 +563,12 @@
 def shards(state, land_mask, kernel_one, bias_one, kernel_two, bias_two, kernel_three, bias_three):
     lon, lat = (lax.axis_size("lon"), lax.axis_size("lat"))
     biases = [x.reshape(1, x.shape[0]) for x in (bias_one, bias_two, bias_three)]
-    rows, strip, outer, inner, mask, *parameters = prepare(
-        state, (land_mask, kernel_one, kernel_two, kernel_three, *biases)
-    )
+    rows, strip, outer, inner, *biases = prepare(state, biases)
+    parameters = (kernel_one, kernel_two, kernel_three, *biases)
 
     inner = lax.ppermute(inner, "lon", [(i, i + 1 - 2 * (i % 2)) for i in range(lon)])
     outer = lax.ppermute(outer, "lon", [(i, (i + 1 if i % 2 else i - 1) % lon) for i in range(lon)])
-    main, north, ocean, *weights, bias = main_pass(lat, rows, mask, parameters)
+    main, north, ocean, *weights, bias = main_pass(lat, rows, land_mask, parameters)
     weights, late = weights[0:3], weights[3:6]
 
     def pairs(parity):
@@ -589,7 +588,7 @@
     cells, low, high, *own = strip_pass(
         rows, strip, inner, outer, main, ocean, weights, bias
     )
-    return border_pass(rows, mask, first, second, *own, late, bias, cells, low, high)
+    return border_pass(rows, land_mask, first, second, *own, late, bias, cells, low, high)
 
 
 def solution(mesh):

time: 13 us -> 12.9 us (level)
  no operation moved by 1% of the time
where the time goes in v4:
time: 12.9 us; the launch traced here: 12.8 us
  Pallas kernels  6.54 us (51%)
  starting transfers between devices  3.54 us (27%)
  waiting for transfers between devices  2.62 us (20%)
    ppermute x1, starting transfers between devices, shards(): lax.ppermute(outer, 'lon', [(i, (i + 1 if i % 2 else i - 1) % lon) for i...  1.95 us
    pallas_call x1, Pallas kernels, strip_pass(): pl.pallas_call(strip_kernel, out_shape=[block((16, ROWS - 8, 128), F32),...  1.8 us
    pallas_call x1, Pallas kernels, main_pass(): pl.pallas_call(functools.partial(main_kernel, size), out_shape=[block(row...  1.66 us
    ppermute x1, starting transfers between devices, shards(): first = lax.ppermute(first, ('lon', 'lat'), pairs(0))  1.58 us
    ppermute x1, waiting for transfers between devices, shards(): second = lax.ppermute(second, ('lon', 'lat'), pairs(1))  1.58 us
    pallas_call x1, Pallas kernels, prepare(): pl.pallas_call(prepare_kernel, out_shape=[block((ROWS, 2, 8, 128), F32),...  1.5 us
    pallas_call x1, Pallas kernels, border_pass(): pl.pallas_call(border_kernel, out_shape=[block((16, ROWS, 128), F32), blo...  1.49 us
    ppermute x1, waiting for transfers between devices, shards(): lax.ppermute(outer, 'lon', [(i, (i + 1 if i % 2 else i - 1) % lon) for i...  0.55 us
  transfers between devices with their start and end apart: 4, of which 3 were waited for; matrix products, arithmetic and copies ran while one was open for 0% of the time, Pallas kernels for 27%

profile of v4, /device:TPU:16, one launch (start us, length us, event | category | flops | bytes accessed | tf_op | source)
XLA Modules:
  0.0 12.8 jit_solution(12210942393779247247)
XLA Ops:
  0.0 0.0 copy-start
  0.0 0.0 copy-start.1
  0.0 0.0 copy-start.2
  0.0 0.0 copy-start.3
  0.0 1.5 %rows_edges.1 = (f32[64,2,8,128]{3,2,1,0:T(8,128)S(1)}, f32[8,2,8,128]{3,2,1,0:T(8,128)S(1)}, f32[4,8,128]{2,1,0:T(8,128)S(1)}, f32[4,8,128]{2,1,0:T(8,128)S(1)}...) custom-call(f32[16,64,128]{2,1,0:T(8,128)} %state_ref.1, f32[1,16]{1,0:T(1,128)} %bitcast.3, ...), custom_call_target="tpu_custom_call" | custom-call | flops 400000 | bytes 1200000 | tf_op jit(solution)/shard_map/rows_edges/pallas_call | solution.py:132
  1.5 2.0 %collective-permute-start = (f32[4,8,128]{2,1,0:T(8,128)S(1)}, f32[4,8,128]{2,1,0:T(8,128)S(1)}, u32[]{:S(2)}, u32[]{:S(2)}) collective-permute-start(f32[4,8,128]{2,1,0:T(8,128)S(1)} %get-tuple-element.32), channel_id=1, source_target_pairs={{0,28},{4,8},{8,4},{12,16},{16,12},{20,24},{24,20},{28,0},{1,29},{... | collective-permute-start | bytes 49160 | tf_op jit(solution)/shard_map/ppermute | solution.py:570
  3.5 0.0 collective-permute-start.1
  3.5 0.0 copy-done
  3.5 0.0 copy-done.1
  3.5 0.0 copy-done.2
  3.5 0.0 copy-done.3
  3.5 1.7 %main_pass.1 = (f32[64,2,8,128]{3,2,1,0:T(8,128)S(1)}, f32[6,8,128]{2,1,0:T(8,128)S(1)}, f32[8,128]{1,0:T(8,128)S(1)}, bf16[128,512]{1,0:T(8,128)(2,1)S(1)}, bf1...) custom-call(f32[64,2,8,128]{3,2,1,0:T(8,128)S(1)} %get-tuple-element, ...), custom_call_target="tpu_custom_call" | custom-call | flops 150000000 | bytes 1500000 | tf_op jit(solution)/shard_map/main_pass/pallas_call | solution.py:310
  5.2 0.6 %collective-permute-done.outer_ref = f32[4,8,128]{2,1,0:T(8,128)S(1)} collective-permute-done((f32[4,8,128]{2,1,0:T(8,128)S(1)}, f32[4,8,128]{2,1,0:T(8,128)S(1)}, u32[]{:S(2)}, u32[]{:S(2)}) %collective-permute-start) | collective-permute-done | bytes 16416 | tf_op jit(solution)/shard_map/ppermute | solution.py:570
  5.7 0.0 collective-permute-done.1.inner_ref
  5.7 0.1 add_corners.1
  5.8 1.6 %collective-permute-start.2 = (f32[7,8,128]{2,1,0:T(8,128)S(1)}, f32[7,8,128]{2,1,0:T(8,128)S(1)}, u32[]{:S(2)}, u32[]{:S(2)}) collective-permute-start(f32[7,8,128]{2,1,0:T(8,128)S(1)} %get-tuple-element.38), channel_id=1, source_target_pairs={{0,1},{1,0},{2,3},{3,2},{4,5},{5,4},{6,7},{7,6},{8,9},{9,8},{10,11... | collective-permute-start | bytes 86024 | tf_op jit(solution)/shard_map/ppermute | solution.py:586
  7.4 0.0 collective-permute-start.3
  7.4 1.8 %strip_pass.1 = (f32[16,56,128]{2,1,0:T(8,128)S(1)}, f32[16,8,128]{2,1,0:T(8,128)S(1)}, f32[16,8,128]{2,1,0:T(8,128)S(1)}, f32[6,2,8,128]{3,2,1,0:T(8,128)S(1)},...) custom-call(f32[64,2,8,128]{3,2,1,0:T(8,128)S(1)} %get-tuple-element.31.rows_ref, ...), custom_call_target="tpu_custom_call" | custom-call | flops 150000000 | bytes 2000000 | tf_op jit(solution)/shard_map/strip_pass/pallas_call | solution.py:444
  9.2 0.5 %collective-permute-done.2.first_ref = f32[7,8,128]{2,1,0:T(8,128)S(1)} collective-permute-done((f32[7,8,128]{2,1,0:T(8,128)S(1)}, f32[7,8,128]{2,1,0:T(8,128)S(1)}, u32[]{:S(2)}, u32[]{:S(2)}) %collective-permute-start.2) | collective-permute-done | bytes 28704 | tf_op jit(solution)/shard_map/ppermute | solution.py:586
  9.7 1.6 %collective-permute-done.3.second_ref = f32[7,8,128]{2,1,0:T(8,128)S(1)} collective-permute-done((f32[7,8,128]{2,1,0:T(8,128)S(1)}, f32[7,8,128]{2,1,0:T(8,128)S(1)}, u32[]{:S(2)}, u32[]{:S(2)}) %collective-permute-start.3) | collective-permute-done | bytes 28704 | tf_op jit(solution)/shard_map/ppermute | solution.py:587
  11.3 1.5 %border_pass.1 = (f32[16,64,128]{2,1,0:T(8,128)}, f32[16,8,128]{2,1,0:T(8,128)S(1)}, f32[16,8,128]{2,1,0:T(8,128)S(1)}) custom-call(f32[64,2,8,128]{3,2,1,0:T(8,128)S(1)} %get-tuple-element.31.rows_ref, s32[64,128]{1,0:T(8,128)S(1)} %copy-done, f32[7,8,128]{2,1,0:T(8,128)S(1)} %collective-permute-done.2.first_ref, ...), custom_call_target="tpu_custom_call", output_to_operand_aliasing={{1}: (12, {}), {2}: (13, {})} | custom-call | flops 60000000 | bytes 1000000 | tf_op jit(solution)/shard_map/border_pass/pallas_call | solution.py:549
Async XLA Ops:
  0.0 3.5 %copy-start = (s32[64,128]{1,0:T(8,128)S(1)}, s32[64,128]{1,0:T(8,128)}, u32[]{:S(2)}) copy-start(s32[64,128]{1,0:T(8,128)} %mask_ref.3) | copy-start | bytes 98308
  0.0 3.5 %copy-start.1 = (bf16[3,3,16,16]{3,2,1,0:T(8,128)(2,1)S(1)}, bf16[3,3,16,16]{3,2,1,0:T(8,128)(2,1)}, u32[]{:S(2)}) copy-start(bf16[3,3,16,16]{3,2,1,0:T(8,128)(2,1)} %k_one_ref.1) | copy-start | bytes 13828
  0.0 3.5 %copy-start.2 = (bf16[3,3,16,16]{3,2,1,0:T(8,128)(2,1)S(1)}, bf16[3,3,16,16]{3,2,1,0:T(8,128)(2,1)}, u32[]{:S(2)}) copy-start(bf16[3,3,16,16]{3,2,1,0:T(8,128)(2,1)} %k_two_ref.1) | copy-start | bytes 13828
  0.0 3.5 %copy-start.3 = (bf16[3,3,8,16]{3,2,1,0:T(8,128)(2,1)S(1)}, bf16[3,3,8,16]{3,2,1,0:T(8,128)(2,1)}, u32[]{:S(2)}) copy-start(bf16[3,3,8,16]{3,2,1,0:T(8,128)(2,1)} %k_three_ref.1) | copy-start | bytes 6916
  1.5 4.2 %collective-permute-start = (f32[4,8,128]{2,1,0:T(8,128)S(1)}, f32[4,8,128]{2,1,0:T(8,128)S(1)}, u32[]{:S(2)}, u32[]{:S(2)}) collective-permute-start(f32[4,8,128]{2,1,0:T(8,128)S(1)} %get-tuple-element.32), channel_id=1, source_target_pairs={{0,28},{4,8},{8,4},{12,16},{16,12},{20,24},{24,20},{28,0},{1,29},{... | collective-permute-start | bytes 49160 | tf_op jit(solution)/shard_map/ppermute | solution.py:570
  3.5 2.3 %collective-permute-start.1 = (f32[4,8,128]{2,1,0:T(8,128)S(1)}, f32[4,8,128]{2,1,0:T(8,128)S(1)}, u32[]{:S(2)}, u32[]{:S(2)}) collective-permute-start(f32[4,8,128]{2,1,0:T(8,128)S(1)} %get-tuple-element.33), channel_id=1, source_target_pairs={{0,4},{4,0},{8,12},{12,8},{16,20},{20,16},{24,28},{28,24},{1,5},{5... | collective-permute-start | bytes 49160 | tf_op jit(solution)/shard_map/ppermute | solution.py:569
  5.8 3.9 %collective-permute-start.2 = (f32[7,8,128]{2,1,0:T(8,128)S(1)}, f32[7,8,128]{2,1,0:T(8,128)S(1)}, u32[]{:S(2)}, u32[]{:S(2)}) collective-permute-start(f32[7,8,128]{2,1,0:T(8,128)S(1)} %get-tuple-element.38), channel_id=1, source_target_pairs={{0,1},{1,0},{2,3},{3,2},{4,5},{5,4},{6,7},{7,6},{8,9},{9,8},{10,11... | collective-permute-start | bytes 86024 | tf_op jit(solution)/shard_map/ppermute | solution.py:586
  7.4 3.9 %collective-permute-start.3 = (f32[7,8,128]{2,1,0:T(8,128)S(1)}, f32[7,8,128]{2,1,0:T(8,128)S(1)}, u32[]{:S(2)}, u32[]{:S(2)}) collective-permute-start(f32[7,8,128]{2,1,0:T(8,128)S(1)} %get-tuple-element.39), channel_id=1, source_target_pairs={{1,2},{2,1},{0,4},{3,31},{5,6},{6,5},{4,0},{7,27},{9,10},{10,9},{8... | collective-permute-start | bytes 86024 | tf_op jit(solution)/shard_map/ppermute | solution.py:587

commit v5 on v4

--- a/solution.py
+++ b/solution.py
@@ -96,8 +96,8 @@
     biases = ((b_one_ref, h_one_ref), (b_two_ref, h_two_ref), (b_three_ref, h_three_ref))
     for source, target in biases:
         fetches.append(pltpu.make_async_copy(source, target, sems.at[len(fetches)]))
-    for i, fetch in enumerate(fetches):
-        fetch.start(priority=i % 2)
+    for fetch in fetches:
+        fetch.start()
 
     flat = cells_ref.reshape(16 * PITCH, 128)
     group = lanes() // 16
@@ -107,7 +107,7 @@
         [jnp.where(even, (4 * s - a) % 128, (4 * s - b) % 128) for s in range(4)]
         for a, b in ((6, 3), (3, 6))
     ]
-    for fetch in fetches:
+    for fetch in fetches[0:2]:
         fetch.wait()
     for half in range(2):
         strip = [jnp.zeros((8, 128), F32)] * 8
@@ -124,6 +124,8 @@
                 for s in range(4):
                     value = jnp.where(part == s, turn(strip[4 * q + s], shift[s]), value)
                 target[2 * q + half] = value
+    for fetch in fetches[2:]:
+        fetch.wait()
 
 
 def prepare(state, biases):
@@ -520,6 +522,8 @@
     total = dot(three_ref[...], jnp.concatenate(operand, axis=0)).reshape(4, 8, 256)
     total = total + jnp.concatenate([bias_ref[32:40, :]] * 2, axis=1)[None]
 
+    low_ref[...] = low_in_ref[...]
+    high_ref[...] = high_in_ref[...]
     col = lanes()
     own = {row: [rows_ref[row, half] for half in range(2)] for row in (0, 1, 2, 3, 60, 61, 62, 63)}
     own[-1], own[ROWS] = south[2], north[0]
@@ -538,26 +542,27 @@
             for half in range(2):
                 flat[pl.ds(64 * half + row - at, 8, stride=8), :] = q[half] + ocean * new[half]
         store = pltpu.make_async_copy(ref, out_ref.at[:, pl.ds(at, 8), :], sems.at[1 + strip])
-        store.start(priority=strip)
+        store.start()
         stores.append(store)
     for store in stores:
         store.wait()
 
 
 def border_pass(rows, mask, first, second, side, pre, hidden, late, bias, cells, low, high):
-    block = jax.ShapeDtypeStruct
-    out, _, _ = pl.pallas_call(
+    return pl.pallas_call(
         border_kernel,
-        out_shape=[block((16, ROWS, 128), F32), block(low.shape, F32), block(high.shape, F32)],
+        out_shape=jax.ShapeDtypeStruct((16, ROWS, 128), F32),
         in_specs=[VMEM] * 14,
-        out_specs=[HBM, VMEM, VMEM],
-        scratch_shapes=[pltpu.SemaphoreType.DMA((3,))],
-        input_output_aliases={12: 1, 13: 2},
+        out_specs=HBM,
+        scratch_shapes=[
+            pltpu.VMEM(low.shape, F32),
+            pltpu.VMEM(high.shape, F32),
+            pltpu.SemaphoreType.DMA((3,)),
+        ],
         compiler_params=pltpu.CompilerParams(vmem_limit_bytes=LIMIT),
         cost_estimate=pl.CostEstimate(flops=60000000, bytes_accessed=1000000, transcendentals=60000),
         name="border_pass",
     )(rows, mask, first, second, side, pre, hidden, *late, bias, cells, low, high)
-    return out
 
 
 def shards(state, land_mask, kernel_one, bias_one, kernel_two, bias_two, kernel_three, bias_three):

time: 12.9 us -> 12.9 us (level)
  no operation moved by 1% of the time
where the time goes in v5:
time: 12.9 us; the launch traced here: 12.8 us
  Pallas kernels  6.55 us (51%)
  starting transfers between devices  3.54 us (27%)
  waiting for transfers between devices  2.61 us (20%)
    ppermute x1, starting transfers between devices, shards(): lax.ppermute(outer, 'lon', [(i, (i + 1 if i % 2 else i - 1) % lon) for i...  1.95 us
    pallas_call x1, Pallas kernels, strip_pass(): pl.pallas_call(strip_kernel, out_shape=[block((16, ROWS - 8, 128), F32),...  1.8 us
    pallas_call x1, Pallas kernels, main_pass(): pl.pallas_call(functools.partial(main_kernel, size), out_shape=[block(row...  1.66 us
    ppermute x1, starting transfers between devices, shards(): first = lax.ppermute(first, ('lon', 'lat'), pairs(0))  1.58 us
    ppermute x1, waiting for transfers between devices, shards(): second = lax.ppermute(second, ('lon', 'lat'), pairs(1))  1.58 us
    pallas_call x1, Pallas kernels, border_pass(): pl.pallas_call(border_kernel, out_shape=jax.ShapeDtypeStruct((16, ROWS, 1...  1.53 us
    pallas_call x1, Pallas kernels, prepare(): pl.pallas_call(prepare_kernel, out_shape=[block((ROWS, 2, 8, 128), F32),...  1.46 us
    ppermute x1, waiting for transfers between devices, shards(): lax.ppermute(outer, 'lon', [(i, (i + 1 if i % 2 else i - 1) % lon) for i...  0.55 us
  transfers between devices with their start and end apart: 4, of which 3 were waited for; matrix products, arithmetic and copies ran while one was open for 0% of the time, Pallas kernels for 27%

profile of v5, /device:TPU:16, one launch (start us, length us, event | category | flops | bytes accessed | tf_op | source)
XLA Modules:
  0.0 12.8 jit_solution(18419643842013126427)
XLA Ops:
  0.0 0.0 copy-start
  0.0 0.0 copy-start.1
  0.0 0.0 copy-start.2
  0.0 0.0 copy-start.3
  0.0 1.5 %rows_edges.1 = (f32[64,2,8,128]{3,2,1,0:T(8,128)S(1)}, f32[8,2,8,128]{3,2,1,0:T(8,128)S(1)}, f32[4,8,128]{2,1,0:T(8,128)S(1)}, f32[4,8,128]{2,1,0:T(8,128)S(1)}...) custom-call(f32[16,64,128]{2,1,0:T(8,128)} %state_ref.1, f32[1,16]{1,0:T(1,128)} %bitcast.3, ...), custom_call_target="tpu_custom_call" | custom-call | flops 400000 | bytes 1200000 | tf_op jit(solution)/shard_map/rows_edges/pallas_call | solution.py:134
  1.5 2.0 %collective-permute-start = (f32[4,8,128]{2,1,0:T(8,128)S(1)}, f32[4,8,128]{2,1,0:T(8,128)S(1)}, u32[]{:S(2)}, u32[]{:S(2)}) collective-permute-start(f32[4,8,128]{2,1,0:T(8,128)S(1)} %get-tuple-element.31), channel_id=1, source_target_pairs={{0,28},{4,8},{8,4},{12,16},{16,12},{20,24},{24,20},{28,0},{1,29},{... | collective-permute-start | bytes 49160 | tf_op jit(solution)/shard_map/ppermute | solution.py:575
  3.4 0.0 collective-permute-start.1
  3.4 0.0 copy-done
  3.5 0.0 copy-done.1
  3.5 0.0 copy-done.2
  3.5 0.0 copy-done.3
  3.5 1.7 %main_pass.1 = (f32[64,2,8,128]{3,2,1,0:T(8,128)S(1)}, f32[6,8,128]{2,1,0:T(8,128)S(1)}, f32[8,128]{1,0:T(8,128)S(1)}, bf16[128,512]{1,0:T(8,128)(2,1)S(1)}, bf1...) custom-call(f32[64,2,8,128]{3,2,1,0:T(8,128)S(1)} %get-tuple-element, ...), custom_call_target="tpu_custom_call" | custom-call | flops 150000000 | bytes 1500000 | tf_op jit(solution)/shard_map/main_pass/pallas_call | solution.py:312
  5.1 0.6 %collective-permute-done.outer_ref = f32[4,8,128]{2,1,0:T(8,128)S(1)} collective-permute-done((f32[4,8,128]{2,1,0:T(8,128)S(1)}, f32[4,8,128]{2,1,0:T(8,128)S(1)}, u32[]{:S(2)}, u32[]{:S(2)}) %collective-permute-start) | collective-permute-done | bytes 16416 | tf_op jit(solution)/shard_map/ppermute | solution.py:575
  5.7 0.0 collective-permute-done.1.inner_ref
  5.7 0.1 add_corners.1
  5.8 1.6 %collective-permute-start.2 = (f32[7,8,128]{2,1,0:T(8,128)S(1)}, f32[7,8,128]{2,1,0:T(8,128)S(1)}, u32[]{:S(2)}, u32[]{:S(2)}) collective-permute-start(f32[7,8,128]{2,1,0:T(8,128)S(1)} %get-tuple-element.37), channel_id=1, source_target_pairs={{0,1},{1,0},{2,3},{3,2},{4,5},{5,4},{6,7},{7,6},{8,9},{9,8},{10,11... | collective-permute-start | bytes 86024 | tf_op jit(solution)/shard_map/ppermute | solution.py:591
  7.4 0.0 collective-permute-start.3
  7.4 1.8 %strip_pass.1 = (f32[16,56,128]{2,1,0:T(8,128)S(1)}, f32[16,8,128]{2,1,0:T(8,128)S(1)}, f32[16,8,128]{2,1,0:T(8,128)S(1)}, f32[6,2,8,128]{3,2,1,0:T(8,128)S(1)},...) custom-call(f32[64,2,8,128]{3,2,1,0:T(8,128)S(1)} %get-tuple-element.30.rows_ref, ...), custom_call_target="tpu_custom_call" | custom-call | flops 150000000 | bytes 2000000 | tf_op jit(solution)/shard_map/strip_pass/pallas_call | solution.py:446
  9.2 0.5 %collective-permute-done.2.first_ref = f32[7,8,128]{2,1,0:T(8,128)S(1)} collective-permute-done((f32[7,8,128]{2,1,0:T(8,128)S(1)}, f32[7,8,128]{2,1,0:T(8,128)S(1)}, u32[]{:S(2)}, u32[]{:S(2)}) %collective-permute-start.2) | collective-permute-done | bytes 28704 | tf_op jit(solution)/shard_map/ppermute | solution.py:591
  9.7 1.6 %collective-permute-done.3.second_ref = f32[7,8,128]{2,1,0:T(8,128)S(1)} collective-permute-done((f32[7,8,128]{2,1,0:T(8,128)S(1)}, f32[7,8,128]{2,1,0:T(8,128)S(1)}, u32[]{:S(2)}, u32[]{:S(2)}) %collective-permute-start.3) | collective-permute-done | bytes 28704 | tf_op jit(solution)/shard_map/ppermute | solution.py:592
  11.2 1.5 %border_pass.1 = f32[16,64,128]{2,1,0:T(8,128)} custom-call(f32[64,2,8,128]{3,2,1,0:T(8,128)S(1)} %get-tuple-element.30.rows_ref, s32[64,128]{1,0:T(8,128)S(1)} %copy-done, f32[7,8,128]{2,1,0:T(8,128)S(1)} %collective-permute-done.2.first_ref, f32[7,8,128]{2,1,0:T(8,128)S(1)} %collective-permute-done.3.second_ref, ...), custom_call_target="tpu_custom_call" | custom-call | flops 60000000 | bytes 1000000 | tf_op jit(solution)/shard_map/border_pass/pallas_call | solution.py:552
Async XLA Ops:
  0.0 3.4 %copy-start = (s32[64,128]{1,0:T(8,128)S(1)}, s32[64,128]{1,0:T(8,128)}, u32[]{:S(2)}) copy-start(s32[64,128]{1,0:T(8,128)} %mask_ref.3) | copy-start | bytes 98308
  0.0 3.4 %copy-start.1 = (bf16[3,3,16,16]{3,2,1,0:T(8,128)(2,1)S(1)}, bf16[3,3,16,16]{3,2,1,0:T(8,128)(2,1)}, u32[]{:S(2)}) copy-start(bf16[3,3,16,16]{3,2,1,0:T(8,128)(2,1)} %k_one_ref.1) | copy-start | bytes 13828
  0.0 3.5 %copy-start.2 = (bf16[3,3,16,16]{3,2,1,0:T(8,128)(2,1)S(1)}, bf16[3,3,16,16]{3,2,1,0:T(8,128)(2,1)}, u32[]{:S(2)}) copy-start(bf16[3,3,16,16]{3,2,1,0:T(8,128)(2,1)} %k_two_ref.1) | copy-start | bytes 13828
  0.0 3.5 %copy-start.3 = (bf16[3,3,8,16]{3,2,1,0:T(8,128)(2,1)S(1)}, bf16[3,3,8,16]{3,2,1,0:T(8,128)(2,1)}, u32[]{:S(2)}) copy-start(bf16[3,3,8,16]{3,2,1,0:T(8,128)(2,1)} %k_three_ref.1) | copy-start | bytes 6916
  1.5 4.2 %collective-permute-start = (f32[4,8,128]{2,1,0:T(8,128)S(1)}, f32[4,8,128]{2,1,0:T(8,128)S(1)}, u32[]{:S(2)}, u32[]{:S(2)}) collective-permute-start(f32[4,8,128]{2,1,0:T(8,128)S(1)} %get-tuple-element.31), channel_id=1, source_target_pairs={{0,28},{4,8},{8,4},{12,16},{16,12},{20,24},{24,20},{28,0},{1,29},{... | collective-permute-start | bytes 49160 | tf_op jit(solution)/shard_map/ppermute | solution.py:575
  3.4 2.3 %collective-permute-start.1 = (f32[4,8,128]{2,1,0:T(8,128)S(1)}, f32[4,8,128]{2,1,0:T(8,128)S(1)}, u32[]{:S(2)}, u32[]{:S(2)}) collective-permute-start(f32[4,8,128]{2,1,0:T(8,128)S(1)} %get-tuple-element.32), channel_id=1, source_target_pairs={{0,4},{4,0},{8,12},{12,8},{16,20},{20,16},{24,28},{28,24},{1,5},{5... | collective-permute-start | bytes 49160 | tf_op jit(solution)/shard_map/ppermute | solution.py:574
  5.8 3.9 %collective-permute-start.2 = (f32[7,8,128]{2,1,0:T(8,128)S(1)}, f32[7,8,128]{2,1,0:T(8,128)S(1)}, u32[]{:S(2)}, u32[]{:S(2)}) collective-permute-start(f32[7,8,128]{2,1,0:T(8,128)S(1)} %get-tuple-element.37), channel_id=1, source_target_pairs={{0,1},{1,0},{2,3},{3,2},{4,5},{5,4},{6,7},{7,6},{8,9},{9,8},{10,11... | collective-permute-start | bytes 86024 | tf_op jit(solution)/shard_map/ppermute | solution.py:591
  7.4 3.9 %collective-permute-start.3 = (f32[7,8,128]{2,1,0:T(8,128)S(1)}, f32[7,8,128]{2,1,0:T(8,128)S(1)}, u32[]{:S(2)}, u32[]{:S(2)}) collective-permute-start(f32[7,8,128]{2,1,0:T(8,128)S(1)} %get-tuple-element.38), channel_id=1, source_target_pairs={{1,2},{2,1},{0,4},{3,31},{5,6},{6,5},{4,0},{7,27},{9,10},{10,9},{8... | collective-permute-start | bytes 86024 | tf_op jit(solution)/shard_map/ppermute | solution.py:592

commit v6 on v5

--- a/solution.py
+++ b/solution.py
@@ -252,7 +252,7 @@
     band(k_two_ref, wide_ref.at[1], two_ref)
     band(k_three_ref, narrow_ref, three_ref)
     band_compact(wide_ref.at[0], late_one_ref, 5, 3)
-    band_compact(wide_ref.at[1], late_two_ref, 7, 5)
+    band_compact(wide_ref.at[1], late_two_ref, 5, 3)
     band_compact(narrow_ref, late_three_ref, 5, 3)
     for ref in (first_ref, second_ref, third_ref):
         for c in range(3):
@@ -316,7 +316,7 @@
             block((6, 8, 128), F32),
             block((8, 128), F32),
             *[block((n, DEPTH), BF16) for n in (128, 128, 64)],
-            *[block(shape, BF16) for shape in ((48, 256), (80, 384), (32, 256))],
+            *[block(shape, BF16) for shape in ((48, 256), (48, 256), (32, 256))],
             block((40, 128), F32),
         ],
         in_specs=[VMEM] * 8,
@@ -348,7 +348,7 @@
 
 def strip_kernel(
     rows_ref, strip_ref, outer_ref, inner_ref, main_ref, ocean_ref, one_ref, two_ref, three_ref,
-    bias_ref, cells_ref, low_ref, high_ref, side_ref, pre_ref, hidden_ref,
+    bias_ref, cells_ref, low_ref, high_ref, side_ref, pre_one_ref, pre_two_ref, pre_three_ref,
 ):
     east, west = sides(inner_ref, outer_ref)
     col = lanes()
@@ -363,6 +363,40 @@
             pair[1].append(jnp.where(at < 3, turn(west[block], -4 * (r % 4)), turn(own, -3)))
         cells.append(pair)
 
+    def own(row):
+        start = 16 * (row // 8) + 4 * (row % 4)
+        block = 2 * (row % 8 // 4)
+        return [beside(east[block + h], start, west[block + h], start) for h in range(2)]
+
+    low, high = [], []
+    for row in list(range(6)) + list(range(ROWS - 6, ROWS)):
+        side = own(row)
+        slot = row if row < 3 else row - ROWS + 6
+        if row < 3 or row >= ROWS - 3:
+            for half in range(2):
+                side_ref[slot, half] = side[half]
+        parts = [
+            jnp.concatenate([rows_ref[row, 0], rows_ref[row, 1]], axis=0),
+            jnp.concatenate(side, axis=0),
+        ]
+        (low if row < 6 else high).append(jnp.concatenate(parts, axis=1).astype(BF16))
+    blank = jnp.zeros((16, 256), BF16)
+    for weights, count, bias_at, pre_ref, width in (
+        (one_ref, 7, 0, pre_one_ref, 256),
+        (two_ref, 5, 16, pre_two_ref, 256),
+        (three_ref, 3, 32, pre_three_ref, 128),
+    ):
+        rows = zip([blank] * 3 + low, high + [blank] * 3)
+        operand = spread([jnp.concatenate(pair, axis=1) for pair in rows], width)
+        n = weights.shape[0] // BLOCK
+        total = dot(weights[0 : (count + count % 2) * n, :], operand).reshape(-1, n, 2 * width)
+        total = total + jnp.concatenate([bias_ref[bias_at : bias_at + n, :]] * (width // 64), axis=1)[None]
+        for r in range(3):
+            parts = [total[r, :, 0:width], total[count - 3 + r, :, width : 2 * width]]
+            pre_ref[r] = jnp.concatenate(parts, axis=1)
+        low = [silu(total[r, :, 0:width]).astype(BF16) for r in range(3, count)]
+        high = [silu(total[r, :, width : 2 * width]).astype(BF16) for r in range(count - 3)]
+
     def moved(pair, by):
         return [[turn(x, by) for x in part] for part in pair]
 
@@ -409,38 +443,6 @@
                 flat[pl.ds(8 * pitch * half + start + r, 8, stride=pitch), :] = value
 
 
-    def own(row):
-        start = 16 * (row // 8) + 4 * (row % 4)
-        block = 2 * (row % 8 // 4)
-        return [beside(east[block + h], start, west[block + h], start) for h in range(2)]
-
-    own_rows = []
-    for row in list(range(6)) + list(range(ROWS - 6, ROWS)):
-        side = own(row)
-        at = row if row < 3 else row - ROWS + 6
-        if row < 3 or row >= ROWS - 3:
-            for half in range(2):
-                side_ref[at, half] = side[half]
-        parts = [
-            jnp.concatenate([rows_ref[row, 0], rows_ref[row, 1]], axis=0),
-            jnp.concatenate(side, axis=0),
-        ]
-        own_rows.append(jnp.concatenate(parts, axis=1).astype(BF16))
-    blank = jnp.zeros((16, 256), BF16)
-    low = [blank] * 3 + own_rows[0:6]
-    high = own_rows[6:12] + [blank] * 3
-    rows = [jnp.concatenate(pair, axis=1) for pair in zip(low, high)]
-    total = dot(one_ref[0:112, :], spread(rows, 256)).reshape(7, 16, 512)
-    total = total + jnp.concatenate([bias_ref[0:16, :]] * 4, axis=1)[None]
-    for r in range(3):
-        pre_ref[r] = jnp.concatenate([total[r, :, 0:256], total[4 + r, :, 256:512]], axis=1)
-    for r in range(4):
-        for strip, x in enumerate((total[3 + r, :, 0:256], total[r, :, 256:512])):
-            value = silu(x).astype(BF16)
-            for c in range(3):
-                hidden_ref[strip, c, r] = turn_wide(value, c)
-
-
 def strip_pass(rows, strip, inner, outer, main, ocean, weights, bias):
     block = jax.ShapeDtypeStruct
     return pl.pallas_call(
@@ -449,11 +451,10 @@
             block((16, ROWS - 8, 128), F32),
             *[block((16, 8, 128), F32)] * 2,
             block((6, 2, 8, 128), F32),
-            block((3, 16, 512), F32),
-            block((2, 3, 4, 16, 256), BF16),
+            *[block(shape, F32) for shape in ((3, 16, 512), (3, 16, 512), (3, 8, 256))],
         ],
         in_specs=[VMEM] * 10,
-        out_specs=[VMEM] * 6,
+        out_specs=[VMEM] * 7,
         compiler_params=pltpu.CompilerParams(vmem_limit_bytes=LIMIT),
         cost_estimate=pl.CostEstimate(
             flops=150000000, bytes_accessed=2000000, transcendentals=100000
@@ -463,8 +464,8 @@
 
 
 def border_kernel(
-    rows_ref, mask_ref, first_ref, second_ref, side_ref, pre_ref, hidden_ref, one_ref, two_ref,
-    three_ref, bias_ref, cells_ref, low_in_ref, high_in_ref, out_ref, low_ref, high_ref, sems,
+    rows_ref, mask_ref, first_ref, second_ref, side_ref, pre_one_ref, pre_two_ref, pre_three_ref,
+    one_ref, two_ref, three_ref, cells_ref, low_in_ref, high_in_ref, out_ref, low_ref, high_ref, sems,
 ):
     lat = lax.axis_index("lat")
     even = lax.rem(lat, 2) == 0
@@ -493,37 +494,26 @@
         low.append(jnp.concatenate(wide[0:2], axis=1).astype(BF16))
         high.append(jnp.concatenate(wide[2:4], axis=1).astype(BF16))
 
-    blank = jnp.zeros((16, 256), BF16)
-    operand = []
-    for c in range(3):
-        lows = [turn_wide(x, c) for x in low] + [blank] * 2
-        highs = [blank] * 2 + [turn_wide(x, c) for x in high]
-        operand.extend(jnp.concatenate(pair, axis=1) for pair in zip(lows, highs))
-    operand.append(jnp.zeros((16, 512), BF16))
-    total = dot(one_ref[...], jnp.concatenate(operand, axis=0)).reshape(3, 16, 512)
-    late = silu(total + pre_ref[...]).astype(BF16)
-
-    operand = []
-    for c in range(3):
-        lows = [turn_wide(late[r, :, 0:256], c) for r in range(3)]
-        lows = lows + [hidden_ref[0, c, r] for r in range(4)]
-        highs = [hidden_ref[1, c, r] for r in range(4)]
-        highs = highs + [turn_wide(late[r, :, 256:512], c) for r in range(3)]
-        operand.extend(jnp.concatenate(pair, axis=1) for pair in zip(lows, highs))
-    operand.extend([jnp.zeros((16, 512), BF16)] * 3)
-    total = dot(two_ref[...], jnp.concatenate(operand, axis=0)).reshape(5, 16, 512)
-    value = silu(total + jnp.concatenate([bias_ref[16:32, :]] * 4, axis=1)[None]).astype(BF16)
-    operand = []
-    for c in range(3):
-        for r in range(5):
-            parts = [turn_wide(value[r, :, at : at + 256], c)[:, 0:128] for at in (0, 256)]
-            operand.append(jnp.concatenate(parts, axis=1))
-    operand.append(jnp.zeros((16, 256), BF16))
-    total = dot(three_ref[...], jnp.concatenate(operand, axis=0)).reshape(4, 8, 256)
-    total = total + jnp.concatenate([bias_ref[32:40, :]] * 2, axis=1)[None]
-
+    def late(weights, low, high, width):
+        blank = jnp.zeros((16, width), BF16)
+        operand = []
+        for c in range(3):
+            lows = [turn_wide(x, c)[:, 0:width] for x in low] + [blank] * 2
+            highs = [blank] * 2 + [turn_wide(x, c)[:, 0:width] for x in high]
+            operand.extend(jnp.concatenate(pair, axis=1) for pair in zip(lows, highs))
+        operand.append(jnp.zeros((16, 2 * width), BF16))
+        return dot(weights[...], jnp.concatenate(operand, axis=0))
+
+    total = late(one_ref, low, high, 256)
     low_ref[...] = low_in_ref[...]
     high_ref[...] = high_in_ref[...]
+    for pre_ref, weights, width in ((pre_one_ref, two_ref, 256), (pre_two_ref, three_ref, 128)):
+        value = silu(total.reshape(3, 16, 512) + pre_ref[...]).astype(BF16)
+        low = [value[r, :, 0:256] for r in range(3)]
+        high = [value[r, :, 256:512] for r in range(3)]
+        total = late(weights, low, high, width)
+    total = total.reshape(4, 8, 256)[0:3] + pre_three_ref[...]
+
     col = lanes()
     own = {row: [rows_ref[row, half] for half in range(2)] for row in (0, 1, 2, 3, 60, 61, 62, 63)}
     own[-1], own[ROWS] = south[2], north[0]
@@ -548,7 +538,7 @@
         store.wait()
 
 
-def border_pass(rows, mask, first, second, side, pre, hidden, late, bias, cells, low, high):
+def border_pass(rows, mask, first, second, side, pre, late, cells, low, high):
     return pl.pallas_call(
         border_kernel,
         out_shape=jax.ShapeDtypeStruct((16, ROWS, 128), F32),
@@ -562,7 +552,7 @@
         compiler_params=pltpu.CompilerParams(vmem_limit_bytes=LIMIT),
         cost_estimate=pl.CostEstimate(flops=60000000, bytes_accessed=1000000, transcendentals=60000),
         name="border_pass",
-    )(rows, mask, first, second, side, pre, hidden, *late, bias, cells, low, high)
+    )(rows, mask, first, second, side, *pre, *late, cells, low, high)
 
 
 def shards(state, land_mask, kernel_one, bias_one, kernel_two, bias_two, kernel_three, bias_three):
@@ -590,10 +580,10 @@
     first, second = corners(lat, rows, inner, outer, north)
     first = lax.ppermute(first, ("lon", "lat"), pairs(0))
     second = lax.ppermute(second, ("lon", "lat"), pairs(1))
-    cells, low, high, *own = strip_pass(
+    cells, low, high, side, *pre = strip_pass(
         rows, strip, inner, outer, main, ocean, weights, bias
     )
-    return border_pass(rows, land_mask, first, second, *own, late, bias, cells, low, high)
+    return border_pass(rows, land_mask, first, second, side, pre, late, cells, low, high)
 
 
 def solution(mesh):

time: 12.9 us -> 12.8 us (level)
  waiting for transfers between devices: 2.61 us -> 2.21 us
  Pallas kernels: 6.55 us -> 6.87 us
    ppermute x1, waiting for transfers between devices: 0.49 us -> 0.04 us  [shards(): first = lax.ppermute(first, ('lon', 'lat'), pairs(0))]
    pallas_call x1, Pallas kernels: 1.8 us -> 2.24 us  [strip_pass(): pl.pallas_call(strip_kernel, out_shape=[block((16, ROWS - 8, 128), F32),...]
  transfers between devices with their start and end apart: 4 -> 4, of which waited for: 3 -> 2; matrix products, arithmetic and copies ran while one was open for 0% -> 0% of each run, Pallas kernels for 27% -> 30%
where the time goes in v6:
time: 12.8 us; the launch traced here: 12.7 us
  Pallas kernels  6.87 us (54%)
  starting transfers between devices  3.54 us (28%)
  waiting for transfers between devices  2.21 us (17%)
    pallas_call x1, Pallas kernels, strip_pass(): pl.pallas_call(strip_kernel, out_shape=[block((16, ROWS - 8, 128), F32),...  2.24 us
    ppermute x1, starting transfers between devices, shards(): lax.ppermute(outer, 'lon', [(i, (i + 1 if i % 2 else i - 1) % lon) for i...  1.95 us
    pallas_call x1, Pallas kernels, main_pass(): pl.pallas_call(functools.partial(main_kernel, size), out_shape=[block(row...  1.62 us
    ppermute x1, starting transfers between devices, shards(): first = lax.ppermute(first, ('lon', 'lat'), pairs(0))  1.58 us
    ppermute x1, waiting for transfers between devices, shards(): second = lax.ppermute(second, ('lon', 'lat'), pairs(1))  1.58 us
    pallas_call x1, Pallas kernels, prepare(): pl.pallas_call(prepare_kernel, out_shape=[block((ROWS, 2, 8, 128), F32),...  1.46 us
    pallas_call x1, Pallas kernels, border_pass(): pl.pallas_call(border_kernel, out_shape=jax.ShapeDtypeStruct((16, ROWS, 1...  1.45 us
    ppermute x1, waiting for transfers between devices, shards(): lax.ppermute(outer, 'lon', [(i, (i + 1 if i % 2 else i - 1) % lon) for i...  0.59 us
  transfers between devices with their start and end apart: 4, of which 2 were waited for; matrix products, arithmetic and copies ran while one was open for 0% of the time, Pallas kernels for 30%

profile of v6, /device:TPU:16, one launch (start us, length us, event | category | flops | bytes accessed | tf_op | source)
XLA Modules:
  0.0 12.7 jit_solution(14959321844733258481)
XLA Ops:
  0.0 0.0 copy-start
  0.0 0.0 copy-start.1
  0.0 0.0 copy-start.2
  0.0 0.0 copy-start.3
  0.0 1.5 %rows_edges.1 = (f32[64,2,8,128]{3,2,1,0:T(8,128)S(1)}, f32[8,2,8,128]{3,2,1,0:T(8,128)S(1)}, f32[4,8,128]{2,1,0:T(8,128)S(1)}, f32[4,8,128]{2,1,0:T(8,128)S(1)}...) custom-call(f32[16,64,128]{2,1,0:T(8,128)} %state_ref.1, f32[1,16]{1,0:T(1,128)} %bitcast.3, ...), custom_call_target="tpu_custom_call" | custom-call | flops 400000 | bytes 1200000 | tf_op jit(solution)/shard_map/rows_edges/pallas_call | solution.py:134
  1.5 2.0 %collective-permute-start = (f32[4,8,128]{2,1,0:T(8,128)S(1)}, f32[4,8,128]{2,1,0:T(8,128)S(1)}, u32[]{:S(2)}, u32[]{:S(2)}) collective-permute-start(f32[4,8,128]{2,1,0:T(8,128)S(1)} %get-tuple-element.32), channel_id=1, source_target_pairs={{0,28},{4,8},{8,4},{12,16},{16,12},{20,24},{24,20},{28,0},{1,29},{... | collective-permute-start | bytes 49160 | tf_op jit(solution)/shard_map/ppermute | solution.py:565
  3.4 0.0 collective-permute-start.1
  3.4 0.0 copy-done
  3.5 0.0 copy-done.1
  3.5 0.0 copy-done.2
  3.5 0.0 copy-done.3
  3.5 1.6 %main_pass.1 = (f32[64,2,8,128]{3,2,1,0:T(8,128)S(1)}, f32[6,8,128]{2,1,0:T(8,128)S(1)}, f32[8,128]{1,0:T(8,128)S(1)}, bf16[128,512]{1,0:T(8,128)(2,1)S(1)}, bf1...) custom-call(f32[64,2,8,128]{3,2,1,0:T(8,128)S(1)} %get-tuple-element, ...), custom_call_target="tpu_custom_call" | custom-call | flops 150000000 | bytes 1500000 | tf_op jit(solution)/shard_map/main_pass/pallas_call | solution.py:312
  5.1 0.6 %collective-permute-done.outer_ref = f32[4,8,128]{2,1,0:T(8,128)S(1)} collective-permute-done((f32[4,8,128]{2,1,0:T(8,128)S(1)}, f32[4,8,128]{2,1,0:T(8,128)S(1)}, u32[]{:S(2)}, u32[]{:S(2)}) %collective-permute-start) | collective-permute-done | bytes 16416 | tf_op jit(solution)/shard_map/ppermute | solution.py:565
  5.7 0.0 collective-permute-done.1.inner_ref
  5.7 0.1 add_corners.1
  5.8 1.6 %collective-permute-start.2 = (f32[7,8,128]{2,1,0:T(8,128)S(1)}, f32[7,8,128]{2,1,0:T(8,128)S(1)}, u32[]{:S(2)}, u32[]{:S(2)}) collective-permute-start(f32[7,8,128]{2,1,0:T(8,128)S(1)} %get-tuple-element.38), channel_id=1, source_target_pairs={{0,1},{1,0},{2,3},{3,2},{4,5},{5,4},{6,7},{7,6},{8,9},{9,8},{10,11... | collective-permute-start | bytes 86024 | tf_op jit(solution)/shard_map/ppermute | solution.py:581
  7.4 0.0 collective-permute-start.3
  7.4 2.2 %strip_pass.1 = (f32[16,56,128]{2,1,0:T(8,128)S(1)}, f32[16,8,128]{2,1,0:T(8,128)S(1)}, f32[16,8,128]{2,1,0:T(8,128)S(1)}, f32[6,2,8,128]{3,2,1,0:T(8,128)S(1)},...) custom-call(f32[64,2,8,128]{3,2,1,0:T(8,128)S(1)} %get-tuple-element.31.rows_ref, ...), custom_call_target="tpu_custom_call" | custom-call | flops 150000000 | bytes 2000000 | tf_op jit(solution)/shard_map/strip_pass/pallas_call | solution.py:448
  9.6 0.0 collective-permute-done.2.first_ref
  9.7 1.6 %collective-permute-done.3.second_ref = f32[7,8,128]{2,1,0:T(8,128)S(1)} collective-permute-done((f32[7,8,128]{2,1,0:T(8,128)S(1)}, f32[7,8,128]{2,1,0:T(8,128)S(1)}, u32[]{:S(2)}, u32[]{:S(2)}) %collective-permute-start.3) | collective-permute-done | bytes 28704 | tf_op jit(solution)/shard_map/ppermute | solution.py:582
  11.2 1.4 %border_pass.1 = f32[16,64,128]{2,1,0:T(8,128)} custom-call(f32[64,2,8,128]{3,2,1,0:T(8,128)S(1)} %get-tuple-element.31.rows_ref, s32[64,128]{1,0:T(8,128)S(1)} %copy-done, f32[7,8,128]{2,1,0:T(8,128)S(1)} %collective-permute-done.2.first_ref, f32[7,8,128]{2,1,0:T(8,128)S(1)} %collective-permute-done.3.second_ref, ...), custom_call_target="tpu_custom_call" | custom-call | flops 60000000 | bytes 1000000 | tf_op jit(solution)/shard_map/border_pass/pallas_call | solution.py:542
Async XLA Ops:
  0.0 3.4 %copy-start = (s32[64,128]{1,0:T(8,128)S(1)}, s32[64,128]{1,0:T(8,128)}, u32[]{:S(2)}) copy-start(s32[64,128]{1,0:T(8,128)} %mask_ref.3) | copy-start | bytes 98308
  0.0 3.4 %copy-start.1 = (bf16[3,3,16,16]{3,2,1,0:T(8,128)(2,1)S(1)}, bf16[3,3,16,16]{3,2,1,0:T(8,128)(2,1)}, u32[]{:S(2)}) copy-start(bf16[3,3,16,16]{3,2,1,0:T(8,128)(2,1)} %k_one_ref.1) | copy-start | bytes 13828
  0.0 3.5 %copy-start.2 = (bf16[3,3,16,16]{3,2,1,0:T(8,128)(2,1)S(1)}, bf16[3,3,16,16]{3,2,1,0:T(8,128)(2,1)}, u32[]{:S(2)}) copy-start(bf16[3,3,16,16]{3,2,1,0:T(8,128)(2,1)} %k_two_ref.1) | copy-start | bytes 13828
  0.0 3.5 %copy-start.3 = (bf16[3,3,8,16]{3,2,1,0:T(8,128)(2,1)S(1)}, bf16[3,3,8,16]{3,2,1,0:T(8,128)(2,1)}, u32[]{:S(2)}) copy-start(bf16[3,3,8,16]{3,2,1,0:T(8,128)(2,1)} %k_three_ref.1) | copy-start | bytes 6916
  1.5 4.2 %collective-permute-start = (f32[4,8,128]{2,1,0:T(8,128)S(1)}, f32[4,8,128]{2,1,0:T(8,128)S(1)}, u32[]{:S(2)}, u32[]{:S(2)}) collective-permute-start(f32[4,8,128]{2,1,0:T(8,128)S(1)} %get-tuple-element.32), channel_id=1, source_target_pairs={{0,28},{4,8},{8,4},{12,16},{16,12},{20,24},{24,20},{28,0},{1,29},{... | collective-permute-start | bytes 49160 | tf_op jit(solution)/shard_map/ppermute | solution.py:565
  3.4 2.3 %collective-permute-start.1 = (f32[4,8,128]{2,1,0:T(8,128)S(1)}, f32[4,8,128]{2,1,0:T(8,128)S(1)}, u32[]{:S(2)}, u32[]{:S(2)}) collective-permute-start(f32[4,8,128]{2,1,0:T(8,128)S(1)} %get-tuple-element.33), channel_id=1, source_target_pairs={{0,4},{4,0},{8,12},{12,8},{16,20},{20,16},{24,28},{28,24},{1,5},{5... | collective-permute-start | bytes 49160 | tf_op jit(solution)/shard_map/ppermute | solution.py:564
  5.8 3.9 %collective-permute-start.2 = (f32[7,8,128]{2,1,0:T(8,128)S(1)}, f32[7,8,128]{2,1,0:T(8,128)S(1)}, u32[]{:S(2)}, u32[]{:S(2)}) collective-permute-start(f32[7,8,128]{2,1,0:T(8,128)S(1)} %get-tuple-element.38), channel_id=1, source_target_pairs={{0,1},{1,0},{2,3},{3,2},{4,5},{5,4},{6,7},{7,6},{8,9},{9,8},{10,11... | collective-permute-start | bytes 86024 | tf_op jit(solution)/shard_map/ppermute | solution.py:581
  7.4 3.9 %collective-permute-start.3 = (f32[7,8,128]{2,1,0:T(8,128)S(1)}, f32[7,8,128]{2,1,0:T(8,128)S(1)}, u32[]{:S(2)}, u32[]{:S(2)}) collective-permute-start(f32[7,8,128]{2,1,0:T(8,128)S(1)} %get-tuple-element.39), channel_id=1, source_target_pairs={{1,2},{2,1},{0,4},{3,31},{5,6},{6,5},{4,0},{7,27},{9,10},{10,9},{8... | collective-permute-start | bytes 86024 | tf_op jit(solution)/shard_map/ppermute | solution.py:582

commit v7 on v6

--- a/solution.py
+++ b/solution.py
@@ -280,8 +280,11 @@
         (second_ref, two_ref, biases[1], third_ref),
     ):
         bias = jnp.concatenate([bias, bias], axis=1)
+        ahead = layer(source, weights, 0)
         for at in range(0, ROWS // 2, BLOCK):
-            total = layer(source, weights, at).reshape(BLOCK, 16, 256)
+            total = ahead.reshape(BLOCK, 16, 256)
+            if at + BLOCK < ROWS // 2:
+                ahead = layer(source, weights, at + BLOCK)
             value = silu(total + bias[None]).astype(BF16).reshape(16 * BLOCK, 256)
             for part in range(2):
                 start = at + ROWS // 2 * part + 1
@@ -290,8 +293,11 @@
                     target[c, start : start + BLOCK] = turn(x, 1 - c).reshape(BLOCK, 16, 128)
 
     bias = jnp.concatenate([biases[2], biases[2]], axis=1)
+    ahead = layer(third_ref, three_ref, 0)
     for at in range(0, ROWS // 2, BLOCK):
-        forcing = layer(third_ref, three_ref, at).reshape(BLOCK, 8, 256) + bias[None]
+        forcing = ahead.reshape(BLOCK, 8, 256) + bias[None]
+        if at + BLOCK < ROWS // 2:
+            ahead = layer(third_ref, three_ref, at + BLOCK)
         for part in range(2):
             for r in range(BLOCK):
                 row = at + ROWS // 2 * part + r
@@ -380,42 +386,42 @@
             jnp.concatenate(side, axis=0),
         ]
         (low if row < 6 else high).append(jnp.concatenate(parts, axis=1).astype(BF16))
+    def moved(pair, by):
+        return [[turn(x, by) for x in part] for part in pair]
+
+    cells = [moved(x, 16) for x in cells[5:8]] + cells + [moved(x, -16) for x in cells[0:3]]
+    rows = []
+    for pair in cells:
+        parts = [jnp.concatenate(part, axis=0) for part in pair]
+        rows.append(jnp.concatenate(parts, axis=1).astype(BF16))
+
     blank = jnp.zeros((16, 256), BF16)
     for weights, count, bias_at, pre_ref, width in (
         (one_ref, 7, 0, pre_one_ref, 256),
         (two_ref, 5, 16, pre_two_ref, 256),
         (three_ref, 3, 32, pre_three_ref, 128),
     ):
-        rows = zip([blank] * 3 + low, high + [blank] * 3)
-        operand = spread([jnp.concatenate(pair, axis=1) for pair in rows], width)
         n = weights.shape[0] // BLOCK
+        more = len(rows) - 2 - BLOCK
+        first = dot(weights[...], taps(rows[0:10], 256)).reshape(BLOCK, n, 256)
+        if more > 0:
+            second = dot(weights[0 : n * more, :], taps(rows[BLOCK:], 256)).reshape(more, n, 256)
+        pairs = zip([blank] * 3 + low, high + [blank] * 3)
+        operand = spread([jnp.concatenate(pair, axis=1) for pair in pairs], width)
         total = dot(weights[0 : (count + count % 2) * n, :], operand).reshape(-1, n, 2 * width)
-        total = total + jnp.concatenate([bias_ref[bias_at : bias_at + n, :]] * (width // 64), axis=1)[None]
+        bias = bias_ref[bias_at : bias_at + n, :]
+        first = first + jnp.concatenate([bias] * 2, axis=1)[None]
+        if more > 0:
+            second = second + jnp.concatenate([bias] * 2, axis=1)[None]
+            rows = [silu(first[i]).astype(BF16) for i in range(BLOCK)]
+            rows = rows + [silu(second[i]).astype(BF16) for i in range(more)]
+        total = total + jnp.concatenate([bias] * (width // 64), axis=1)[None]
         for r in range(3):
             parts = [total[r, :, 0:width], total[count - 3 + r, :, width : 2 * width]]
             pre_ref[r] = jnp.concatenate(parts, axis=1)
         low = [silu(total[r, :, 0:width]).astype(BF16) for r in range(3, count)]
         high = [silu(total[r, :, width : 2 * width]).astype(BF16) for r in range(count - 3)]
-
-    def moved(pair, by):
-        return [[turn(x, by) for x in part] for part in pair]
-
-    cells = [moved(x, 16) for x in cells[5:8]] + cells + [moved(x, -16) for x in cells[0:3]]
-    rows = []
-    for pair in cells:
-        parts = [jnp.concatenate(part, axis=0) for part in pair]
-        rows.append(jnp.concatenate(parts, axis=1).astype(BF16))
-
-    for weights, bias_at in ((one_ref, 0), (two_ref, 16)):
-        count = len(rows) - 2 - BLOCK
-        bias = jnp.concatenate([bias_ref[bias_at : bias_at + 16, :]] * 2, axis=1)
-        low = dot(weights[...], taps(rows[0:10], 256)).reshape(BLOCK, 16, 256)
-        high = dot(weights[0 : 16 * count, :], taps(rows[BLOCK:], 256)).reshape(count, 16, 256)
-        low = silu(low + bias[None]).astype(BF16)
-        high = silu(high + bias[None]).astype(BF16)
-        rows = [low[i] for i in range(BLOCK)] + [high[i] for i in range(count)]
-    forcing = dot(three_ref[...], taps(rows, 256)).reshape(BLOCK, 8, 256)
-    forcing = forcing + jnp.concatenate([bias_ref[32:40, :]] * 2, axis=1)[None]
+    forcing = first
 
     both = []
     for r in range(8):

time: 12.8 us -> 12.8 us (level)
  waiting for transfers between devices: 2.21 us -> 2.68 us
  Pallas kernels: 6.87 us -> 6.4 us
    ppermute x1, waiting for transfers between devices: 0.04 us -> 0.51 us  [shards(): first = lax.ppermute(first, ('lon', 'lat'), pairs(0))]
    pallas_call x1, Pallas kernels: 2.24 us -> 1.77 us  [strip_pass(): pl.pallas_call(strip_kernel, out_shape=[block((16, ROWS - 8, 128), F32),...]
  transfers between devices with their start and end apart: 4 -> 4, of which waited for: 2 -> 3; matrix products, arithmetic and copies ran while one was open for 0% -> 0% of each run, Pallas kernels for 30% -> 27%
where the time goes in v7:
time: 12.8 us; the launch traced here: 12.7 us
  Pallas kernels  6.4 us (50%)
  starting transfers between devices  3.54 us (28%)
  waiting for transfers between devices  2.68 us (21%)
    ppermute x1, starting transfers between devices, shards(): lax.ppermute(outer, 'lon', [(i, (i + 1 if i % 2 else i - 1) % lon) for i...  1.95 us
    pallas_call x1, Pallas kernels, strip_pass(): pl.pallas_call(strip_kernel, out_shape=[block((16, ROWS - 8, 128), F32),...  1.77 us
    pallas_call x1, Pallas kernels, main_pass(): pl.pallas_call(functools.partial(main_kernel, size), out_shape=[block(row...  1.63 us
    ppermute x1, starting transfers between devices, shards(): first = lax.ppermute(first, ('lon', 'lat'), pairs(0))  1.58 us
    ppermute x1, waiting for transfers between devices, shards(): second = lax.ppermute(second, ('lon', 'lat'), pairs(1))  1.58 us
    pallas_call x1, Pallas kernels, prepare(): pl.pallas_call(prepare_kernel, out_shape=[block((ROWS, 2, 8, 128), F32),...  1.46 us
    pallas_call x1, Pallas kernels, border_pass(): pl.pallas_call(border_kernel, out_shape=jax.ShapeDtypeStruct((16, ROWS, 1...  1.45 us
    ppermute x1, waiting for transfers between devices, shards(): lax.ppermute(outer, 'lon', [(i, (i + 1 if i % 2 else i - 1) % lon) for i...  0.58 us
  transfers between devices with their start and end apart: 4, of which 3 were waited for; matrix products, arithmetic and copies ran while one was open for 0% of the time, Pallas kernels for 27%

profile of v7, /device:TPU:16, one launch (start us, length us, event | category | flops | bytes accessed | tf_op | source)
XLA Modules:
  0.0 12.7 jit_solution(1417182530313671015)
XLA Ops:
  0.0 0.0 copy-start
  0.0 0.0 copy-start.1
  0.0 0.0 copy-start.2
  0.0 0.0 copy-start.3
  0.0 1.5 %rows_edges.1 = (f32[64,2,8,128]{3,2,1,0:T(8,128)S(1)}, f32[8,2,8,128]{3,2,1,0:T(8,128)S(1)}, f32[4,8,128]{2,1,0:T(8,128)S(1)}, f32[4,8,128]{2,1,0:T(8,128)S(1)}...) custom-call(f32[16,64,128]{2,1,0:T(8,128)} %state_ref.1, f32[1,16]{1,0:T(1,128)} %bitcast.3, ...), custom_call_target="tpu_custom_call" | custom-call | flops 400000 | bytes 1200000 | tf_op jit(solution)/shard_map/rows_edges/pallas_call | solution.py:134
  1.5 2.0 %collective-permute-start = (f32[4,8,128]{2,1,0:T(8,128)S(1)}, f32[4,8,128]{2,1,0:T(8,128)S(1)}, u32[]{:S(2)}, u32[]{:S(2)}) collective-permute-start(f32[4,8,128]{2,1,0:T(8,128)S(1)} %get-tuple-element.32), channel_id=1, source_target_pairs={{0,28},{4,8},{8,4},{12,16},{16,12},{20,24},{24,20},{28,0},{1,29},{... | collective-permute-start | bytes 49160 | tf_op jit(solution)/shard_map/ppermute | solution.py:571
  3.4 0.0 collective-permute-start.1
  3.4 0.0 copy-done
  3.5 0.0 copy-done.1
  3.5 0.0 copy-done.2
  3.5 0.0 copy-done.3
  3.5 1.6 %main_pass.1 = (f32[64,2,8,128]{3,2,1,0:T(8,128)S(1)}, f32[6,8,128]{2,1,0:T(8,128)S(1)}, f32[8,128]{1,0:T(8,128)S(1)}, bf16[128,512]{1,0:T(8,128)(2,1)S(1)}, bf1...) custom-call(f32[64,2,8,128]{3,2,1,0:T(8,128)S(1)} %get-tuple-element, ...), custom_call_target="tpu_custom_call" | custom-call | flops 150000000 | bytes 1500000 | tf_op jit(solution)/shard_map/main_pass/pallas_call | solution.py:318
  5.1 0.6 %collective-permute-done.outer_ref = f32[4,8,128]{2,1,0:T(8,128)S(1)} collective-permute-done((f32[4,8,128]{2,1,0:T(8,128)S(1)}, f32[4,8,128]{2,1,0:T(8,128)S(1)}, u32[]{:S(2)}, u32[]{:S(2)}) %collective-permute-start) | collective-permute-done | bytes 16416 | tf_op jit(solution)/shard_map/ppermute | solution.py:571
  5.7 0.0 collective-permute-done.1.inner_ref
  5.7 0.1 add_corners.1
  5.8 1.6 %collective-permute-start.2 = (f32[7,8,128]{2,1,0:T(8,128)S(1)}, f32[7,8,128]{2,1,0:T(8,128)S(1)}, u32[]{:S(2)}, u32[]{:S(2)}) collective-permute-start(f32[7,8,128]{2,1,0:T(8,128)S(1)} %get-tuple-element.38), channel_id=1, source_target_pairs={{0,1},{1,0},{2,3},{3,2},{4,5},{5,4},{6,7},{7,6},{8,9},{9,8},{10,11... | collective-permute-start | bytes 86024 | tf_op jit(solution)/shard_map/ppermute | solution.py:587
  7.4 0.0 collective-permute-start.3
  7.4 1.8 %strip_pass.1 = (f32[16,56,128]{2,1,0:T(8,128)S(1)}, f32[16,8,128]{2,1,0:T(8,128)S(1)}, f32[16,8,128]{2,1,0:T(8,128)S(1)}, f32[6,2,8,128]{3,2,1,0:T(8,128)S(1)},...) custom-call(f32[64,2,8,128]{3,2,1,0:T(8,128)S(1)} %get-tuple-element.31.rows_ref, ...), custom_call_target="tpu_custom_call" | custom-call | flops 150000000 | bytes 2000000 | tf_op jit(solution)/shard_map/strip_pass/pallas_call | solution.py:454
  9.2 0.5 %collective-permute-done.2.first_ref = f32[7,8,128]{2,1,0:T(8,128)S(1)} collective-permute-done((f32[7,8,128]{2,1,0:T(8,128)S(1)}, f32[7,8,128]{2,1,0:T(8,128)S(1)}, u32[]{:S(2)}, u32[]{:S(2)}) %collective-permute-start.2) | collective-permute-done | bytes 28704 | tf_op jit(solution)/shard_map/ppermute | solution.py:587
  9.7 1.6 %collective-permute-done.3.second_ref = f32[7,8,128]{2,1,0:T(8,128)S(1)} collective-permute-done((f32[7,8,128]{2,1,0:T(8,128)S(1)}, f32[7,8,128]{2,1,0:T(8,128)S(1)}, u32[]{:S(2)}, u32[]{:S(2)}) %collective-permute-start.3) | collective-permute-done | bytes 28704 | tf_op jit(solution)/shard_map/ppermute | solution.py:588
  11.2 1.4 %border_pass.1 = f32[16,64,128]{2,1,0:T(8,128)} custom-call(f32[64,2,8,128]{3,2,1,0:T(8,128)S(1)} %get-tuple-element.31.rows_ref, s32[64,128]{1,0:T(8,128)S(1)} %copy-done, f32[7,8,128]{2,1,0:T(8,128)S(1)} %collective-permute-done.2.first_ref, f32[7,8,128]{2,1,0:T(8,128)S(1)} %collective-permute-done.3.second_ref, ...), custom_call_target="tpu_custom_call" | custom-call | flops 60000000 | bytes 1000000 | tf_op jit(solution)/shard_map/border_pass/pallas_call | solution.py:548
Async XLA Ops:
  0.0 3.4 %copy-start = (s32[64,128]{1,0:T(8,128)S(1)}, s32[64,128]{1,0:T(8,128)}, u32[]{:S(2)}) copy-start(s32[64,128]{1,0:T(8,128)} %mask_ref.3) | copy-start | bytes 98308
  0.0 3.4 %copy-start.1 = (bf16[3,3,16,16]{3,2,1,0:T(8,128)(2,1)S(1)}, bf16[3,3,16,16]{3,2,1,0:T(8,128)(2,1)}, u32[]{:S(2)}) copy-start(bf16[3,3,16,16]{3,2,1,0:T(8,128)(2,1)} %k_one_ref.1) | copy-start | bytes 13828
  0.0 3.5 %copy-start.2 = (bf16[3,3,16,16]{3,2,1,0:T(8,128)(2,1)S(1)}, bf16[3,3,16,16]{3,2,1,0:T(8,128)(2,1)}, u32[]{:S(2)}) copy-start(bf16[3,3,16,16]{3,2,1,0:T(8,128)(2,1)} %k_two_ref.1) | copy-start | bytes 13828
  0.0 3.5 %copy-start.3 = (bf16[3,3,8,16]{3,2,1,0:T(8,128)(2,1)S(1)}, bf16[3,3,8,16]{3,2,1,0:T(8,128)(2,1)}, u32[]{:S(2)}) copy-start(bf16[3,3,8,16]{3,2,1,0:T(8,128)(2,1)} %k_three_ref.1) | copy-start | bytes 6916
  1.5 4.2 %collective-permute-start = (f32[4,8,128]{2,1,0:T(8,128)S(1)}, f32[4,8,128]{2,1,0:T(8,128)S(1)}, u32[]{:S(2)}, u32[]{:S(2)}) collective-permute-start(f32[4,8,128]{2,1,0:T(8,128)S(1)} %get-tuple-element.32), channel_id=1, source_target_pairs={{0,28},{4,8},{8,4},{12,16},{16,12},{20,24},{24,20},{28,0},{1,29},{... | collective-permute-start | bytes 49160 | tf_op jit(solution)/shard_map/ppermute | solution.py:571
  3.4 2.3 %collective-permute-start.1 = (f32[4,8,128]{2,1,0:T(8,128)S(1)}, f32[4,8,128]{2,1,0:T(8,128)S(1)}, u32[]{:S(2)}, u32[]{:S(2)}) collective-permute-start(f32[4,8,128]{2,1,0:T(8,128)S(1)} %get-tuple-element.33), channel_id=1, source_target_pairs={{0,4},{4,0},{8,12},{12,8},{16,20},{20,16},{24,28},{28,24},{1,5},{5... | collective-permute-start | bytes 49160 | tf_op jit(solution)/shard_map/ppermute | solution.py:570
  5.8 3.9 %collective-permute-start.2 = (f32[7,8,128]{2,1,0:T(8,128)S(1)}, f32[7,8,128]{2,1,0:T(8,128)S(1)}, u32[]{:S(2)}, u32[]{:S(2)}) collective-permute-start(f32[7,8,128]{2,1,0:T(8,128)S(1)} %get-tuple-element.38), channel_id=1, source_target_pairs={{0,1},{1,0},{2,3},{3,2},{4,5},{5,4},{6,7},{7,6},{8,9},{9,8},{10,11... | collective-permute-start | bytes 86024 | tf_op jit(solution)/shard_map/ppermute | solution.py:587
  7.4 3.9 %collective-permute-start.3 = (f32[7,8,128]{2,1,0:T(8,128)S(1)}, f32[7,8,128]{2,1,0:T(8,128)S(1)}, u32[]{:S(2)}, u32[]{:S(2)}) collective-permute-start(f32[7,8,128]{2,1,0:T(8,128)S(1)} %get-tuple-element.39), channel_id=1, source_target_pairs={{1,2},{2,1},{0,4},{3,31},{5,6},{6,5},{4,0},{7,27},{9,10},{10,9},{8... | collective-permute-start | bytes 86024 | tf_op jit(solution)/shard_map/ppermute | solution.py:588

commit v8 on v7

--- a/solution.py
+++ b/solution.py
@@ -109,21 +109,23 @@
     ]
     for fetch in fetches[0:2]:
         fetch.wait()
-    for half in range(2):
-        strip = [jnp.zeros((8, 128), F32)] * 8
-        for b in range(8):
+    strip = [[jnp.zeros((8, 128), F32)] * 8 for half in range(2)]
+    for b in range(8):
+        for half in range(2):
             for r in range(8):
                 x = flat[pl.ds(8 * PITCH * half + 8 * b + r, 8, stride=PITCH), :]
                 rows_ref[8 * b + r, half] = x
-                strip[r] = jnp.where(group == b, turn(x, 6 + 16 * b), strip[r])
-        for r in range(8):
-            strip_ref[r, half] = strip[r]
-        for target, shift in zip((outer_ref, inner_ref), shifts):
-            for q in range(2):
+                strip[half][r] = jnp.where(group == b, turn(x, 6 + 16 * b), strip[half][r])
+    for target, shift in zip((outer_ref, inner_ref), shifts):
+        for q in range(2):
+            for half in range(2):
                 value = jnp.zeros((8, 128), F32)
                 for s in range(4):
-                    value = jnp.where(part == s, turn(strip[4 * q + s], shift[s]), value)
+                    value = jnp.where(part == s, turn(strip[half][4 * q + s], shift[s]), value)
                 target[2 * q + half] = value
+    for half in range(2):
+        for r in range(8):
+            strip_ref[r, half] = strip[half][r]
     for fetch in fetches[2:]:
         fetch.wait()
 
@@ -513,6 +515,19 @@
     total = late(one_ref, low, high, 256)
     low_ref[...] = low_in_ref[...]
     high_ref[...] = high_in_ref[...]
+    col = lanes()
+    own = {row: [rows_ref[row, half] for half in range(2)] for row in (0, 1, 2, 3, 60, 61, 62, 63)}
+    own[-1], own[ROWS] = south[2], north[0]
+    ready = []
+    for at, row in enumerate((0, 1, 2, ROWS - 3, ROWS - 2, ROWS - 1)):
+        q = own[row]
+        side = [side_ref[at, half] for half in range(2)]
+        e = [turn(jnp.where(col == 0, y, x), -1) for x, y in zip(q, side)]
+        w = [turn(jnp.where(col == 127, y, x), 1) for x, y in zip(q, side)]
+        new = tendency(q, own[row + 1], own[row - 1], e, w)
+        ocean = 0.1 * mask_ref[row : row + 1, :].astype(F32)
+        ready.append((q[0] + ocean * new[0], q[1] + ocean * new[1], ocean))
+
     for pre_ref, weights, width in ((pre_one_ref, two_ref, 256), (pre_two_ref, three_ref, 128)):
         value = silu(total.reshape(3, 16, 512) + pre_ref[...]).astype(BF16)
         low = [value[r, :, 0:256] for r in range(3)]
@@ -520,23 +535,16 @@
         total = late(weights, low, high, width)
     total = total.reshape(4, 8, 256)[0:3] + pre_three_ref[...]
 
-    col = lanes()
-    own = {row: [rows_ref[row, half] for half in range(2)] for row in (0, 1, 2, 3, 60, 61, 62, 63)}
-    own[-1], own[ROWS] = south[2], north[0]
     for strip in range(2):
-        ref, at = ((low_ref, 0), (high_ref, ROWS - 8))[strip]
+        ref, at, start = ((low_ref, 0, 0), (high_ref, ROWS - 8, 5))[strip]
         flat = ref.reshape(128, 128)
         for t in range(3):
-            row = t if strip == 0 else ROWS - 3 + t
-            q = own[row]
-            side = [side_ref[3 * strip + t, half] for half in range(2)]
-            ocean = 0.1 * mask_ref[row : row + 1, :].astype(F32)
-            e = [turn(jnp.where(col == 0, y, x), -1) for x, y in zip(q, side)]
-            w = [turn(jnp.where(col == 127, y, x), 1) for x, y in zip(q, side)]
-            new = tendency(q, own[row + 1], own[row - 1], e, w)
-            new[0] = new[0] + total[t, :, 128 * strip : 128 * strip + 128]
+            first, second, ocean = ready[3 * strip + t]
+            forcing = total[t, :, 128 * strip : 128 * strip + 128]
+            new = (first + ocean * forcing, second)
+            row = start + t
             for half in range(2):
-                flat[pl.ds(64 * half + row - at, 8, stride=8), :] = q[half] + ocean * new[half]
+                flat[pl.ds(64 * half + row, 8, stride=8), :] = new[half]
         store = pltpu.make_async_copy(ref, out_ref.at[:, pl.ds(at, 8), :], sems.at[1 + strip])
         store.start()
         stores.append(store)

time: 12.8 us -> 12.8 us (level)
  no operation moved by 1% of the time
where the time goes in v8:
time: 12.8 us; the launch traced here: 12.7 us
  Pallas kernels  6.39 us (50%)
  starting transfers between devices  3.54 us (28%)
  waiting for transfers between devices  2.68 us (21%)
    ppermute x1, starting transfers between devices, shards(): lax.ppermute(outer, 'lon', [(i, (i + 1 if i % 2 else i - 1) % lon) for i...  1.95 us
    pallas_call x1, Pallas kernels, strip_pass(): pl.pallas_call(strip_kernel, out_shape=[block((16, ROWS - 8, 128), F32),...  1.77 us
    pallas_call x1, Pallas kernels, main_pass(): pl.pallas_call(functools.partial(main_kernel, size), out_shape=[block(row...  1.63 us
    ppermute x1, starting transfers between devices, shards(): first = lax.ppermute(first, ('lon', 'lat'), pairs(0))  1.58 us
    ppermute x1, waiting for transfers between devices, shards(): second = lax.ppermute(second, ('lon', 'lat'), pairs(1))  1.58 us
    pallas_call x1, Pallas kernels, border_pass(): pl.pallas_call(border_kernel, out_shape=jax.ShapeDtypeStruct((16, ROWS, 1...  1.48 us
    pallas_call x1, Pallas kernels, prepare(): pl.pallas_call(prepare_kernel, out_shape=[block((ROWS, 2, 8, 128), F32),...  1.42 us
    ppermute x1, waiting for transfers between devices, shards(): lax.ppermute(outer, 'lon', [(i, (i + 1 if i % 2 else i - 1) % lon) for i...  0.58 us
  transfers between devices with their start and end apart: 4, of which 3 were waited for; matrix products, arithmetic and copies ran while one was open for 0% of the time, Pallas kernels for 27%

profile of v8, /device:TPU:16, one launch (start us, length us, event | category | flops | bytes accessed | tf_op | source)
XLA Modules:
  0.0 12.7 jit_solution(6045350300170572703)
XLA Ops:
  0.0 0.0 copy-start
  0.0 0.0 copy-start.1
  0.0 0.0 copy-start.2
  0.0 0.0 copy-start.3
  0.0 1.4 %rows_edges.1 = (f32[64,2,8,128]{3,2,1,0:T(8,128)S(1)}, f32[8,2,8,128]{3,2,1,0:T(8,128)S(1)}, f32[4,8,128]{2,1,0:T(8,128)S(1)}, f32[4,8,128]{2,1,0:T(8,128)S(1)}...) custom-call(f32[16,64,128]{2,1,0:T(8,128)} %state_ref.1, f32[1,16]{1,0:T(1,128)} %bitcast.3, ...), custom_call_target="tpu_custom_call" | custom-call | flops 400000 | bytes 1200000 | tf_op jit(solution)/shard_map/rows_edges/pallas_call | solution.py:136
  1.5 2.0 %collective-permute-start = (f32[4,8,128]{2,1,0:T(8,128)S(1)}, f32[4,8,128]{2,1,0:T(8,128)S(1)}, u32[]{:S(2)}, u32[]{:S(2)}) collective-permute-start(f32[4,8,128]{2,1,0:T(8,128)S(1)} %get-tuple-element.32), channel_id=1, source_target_pairs={{0,28},{4,8},{8,4},{12,16},{16,12},{20,24},{24,20},{28,0},{1,29},{... | collective-permute-start | bytes 49160 | tf_op jit(solution)/shard_map/ppermute | solution.py:579
  3.4 0.0 collective-permute-start.1
  3.4 0.0 copy-done
  3.4 0.0 copy-done.1
  3.4 0.0 copy-done.2
  3.4 0.0 copy-done.3
  3.4 1.6 %main_pass.1 = (f32[64,2,8,128]{3,2,1,0:T(8,128)S(1)}, f32[6,8,128]{2,1,0:T(8,128)S(1)}, f32[8,128]{1,0:T(8,128)S(1)}, bf16[128,512]{1,0:T(8,128)(2,1)S(1)}, bf1...) custom-call(f32[64,2,8,128]{3,2,1,0:T(8,128)S(1)} %get-tuple-element, ...), custom_call_target="tpu_custom_call" | custom-call | flops 150000000 | bytes 1500000 | tf_op jit(solution)/shard_map/main_pass/pallas_call | solution.py:320
  5.1 0.6 %collective-permute-done.outer_ref = f32[4,8,128]{2,1,0:T(8,128)S(1)} collective-permute-done((f32[4,8,128]{2,1,0:T(8,128)S(1)}, f32[4,8,128]{2,1,0:T(8,128)S(1)}, u32[]{:S(2)}, u32[]{:S(2)}) %collective-permute-start) | collective-permute-done | bytes 16416 | tf_op jit(solution)/shard_map/ppermute | solution.py:579
  5.7 0.0 collective-permute-done.1.inner_ref
  5.7 0.1 add_corners.1
  5.7 1.6 %collective-permute-start.2 = (f32[7,8,128]{2,1,0:T(8,128)S(1)}, f32[7,8,128]{2,1,0:T(8,128)S(1)}, u32[]{:S(2)}, u32[]{:S(2)}) collective-permute-start(f32[7,8,128]{2,1,0:T(8,128)S(1)} %get-tuple-element.38), channel_id=1, source_target_pairs={{0,1},{1,0},{2,3},{3,2},{4,5},{5,4},{6,7},{7,6},{8,9},{9,8},{10,11... | collective-permute-start | bytes 86024 | tf_op jit(solution)/shard_map/ppermute | solution.py:595
  7.3 0.0 collective-permute-start.3
  7.3 1.8 %strip_pass.1 = (f32[16,56,128]{2,1,0:T(8,128)S(1)}, f32[16,8,128]{2,1,0:T(8,128)S(1)}, f32[16,8,128]{2,1,0:T(8,128)S(1)}, f32[6,2,8,128]{3,2,1,0:T(8,128)S(1)},...) custom-call(f32[64,2,8,128]{3,2,1,0:T(8,128)S(1)} %get-tuple-element.31.rows_ref, ...), custom_call_target="tpu_custom_call" | custom-call | flops 150000000 | bytes 2000000 | tf_op jit(solution)/shard_map/strip_pass/pallas_call | solution.py:456
  9.1 0.5 %collective-permute-done.2.first_ref = f32[7,8,128]{2,1,0:T(8,128)S(1)} collective-permute-done((f32[7,8,128]{2,1,0:T(8,128)S(1)}, f32[7,8,128]{2,1,0:T(8,128)S(1)}, u32[]{:S(2)}, u32[]{:S(2)}) %collective-permute-start.2) | collective-permute-done | bytes 28704 | tf_op jit(solution)/shard_map/ppermute | solution.py:595
  9.6 1.6 %collective-permute-done.3.second_ref = f32[7,8,128]{2,1,0:T(8,128)S(1)} collective-permute-done((f32[7,8,128]{2,1,0:T(8,128)S(1)}, f32[7,8,128]{2,1,0:T(8,128)S(1)}, u32[]{:S(2)}, u32[]{:S(2)}) %collective-permute-start.3) | collective-permute-done | bytes 28704 | tf_op jit(solution)/shard_map/ppermute | solution.py:596
  11.2 1.5 %border_pass.1 = f32[16,64,128]{2,1,0:T(8,128)} custom-call(f32[64,2,8,128]{3,2,1,0:T(8,128)S(1)} %get-tuple-element.31.rows_ref, s32[64,128]{1,0:T(8,128)S(1)} %copy-done, f32[7,8,128]{2,1,0:T(8,128)S(1)} %collective-permute-done.2.first_ref, f32[7,8,128]{2,1,0:T(8,128)S(1)} %collective-permute-done.3.second_ref, ...), custom_call_target="tpu_custom_call" | custom-call | flops 60000000 | bytes 1000000 | tf_op jit(solution)/shard_map/border_pass/pallas_call | solution.py:556
Async XLA Ops:
  0.0 3.4 %copy-start = (s32[64,128]{1,0:T(8,128)S(1)}, s32[64,128]{1,0:T(8,128)}, u32[]{:S(2)}) copy-start(s32[64,128]{1,0:T(8,128)} %mask_ref.3) | copy-start | bytes 98308
  0.0 3.4 %copy-start.1 = (bf16[3,3,16,16]{3,2,1,0:T(8,128)(2,1)S(1)}, bf16[3,3,16,16]{3,2,1,0:T(8,128)(2,1)}, u32[]{:S(2)}) copy-start(bf16[3,3,16,16]{3,2,1,0:T(8,128)(2,1)} %k_one_ref.1) | copy-start | bytes 13828
  0.0 3.4 %copy-start.2 = (bf16[3,3,16,16]{3,2,1,0:T(8,128)(2,1)S(1)}, bf16[3,3,16,16]{3,2,1,0:T(8,128)(2,1)}, u32[]{:S(2)}) copy-start(bf16[3,3,16,16]{3,2,1,0:T(8,128)(2,1)} %k_two_ref.1) | copy-start | bytes 13828
  0.0 3.4 %copy-start.3 = (bf16[3,3,8,16]{3,2,1,0:T(8,128)(2,1)S(1)}, bf16[3,3,8,16]{3,2,1,0:T(8,128)(2,1)}, u32[]{:S(2)}) copy-start(bf16[3,3,8,16]{3,2,1,0:T(8,128)(2,1)} %k_three_ref.1) | copy-start | bytes 6916
  1.5 4.2 %collective-permute-start = (f32[4,8,128]{2,1,0:T(8,128)S(1)}, f32[4,8,128]{2,1,0:T(8,128)S(1)}, u32[]{:S(2)}, u32[]{:S(2)}) collective-permute-start(f32[4,8,128]{2,1,0:T(8,128)S(1)} %get-tuple-element.32), channel_id=1, source_target_pairs={{0,28},{4,8},{8,4},{12,16},{16,12},{20,24},{24,20},{28,0},{1,29},{... | collective-permute-start | bytes 49160 | tf_op jit(solution)/shard_map/ppermute | solution.py:579
  3.4 2.3 %collective-permute-start.1 = (f32[4,8,128]{2,1,0:T(8,128)S(1)}, f32[4,8,128]{2,1,0:T(8,128)S(1)}, u32[]{:S(2)}, u32[]{:S(2)}) collective-permute-start(f32[4,8,128]{2,1,0:T(8,128)S(1)} %get-tuple-element.33), channel_id=1, source_target_pairs={{0,4},{4,0},{8,12},{12,8},{16,20},{20,16},{24,28},{28,24},{1,5},{5... | collective-permute-start | bytes 49160 | tf_op jit(solution)/shard_map/ppermute | solution.py:578
  5.7 3.9 %collective-permute-start.2 = (f32[7,8,128]{2,1,0:T(8,128)S(1)}, f32[7,8,128]{2,1,0:T(8,128)S(1)}, u32[]{:S(2)}, u32[]{:S(2)}) collective-permute-start(f32[7,8,128]{2,1,0:T(8,128)S(1)} %get-tuple-element.38), channel_id=1, source_target_pairs={{0,1},{1,0},{2,3},{3,2},{4,5},{5,4},{6,7},{7,6},{8,9},{9,8},{10,11... | collective-permute-start | bytes 86024 | tf_op jit(solution)/shard_map/ppermute | solution.py:595
  7.3 3.9 %collective-permute-start.3 = (f32[7,8,128]{2,1,0:T(8,128)S(1)}, f32[7,8,128]{2,1,0:T(8,128)S(1)}, u32[]{:S(2)}, u32[]{:S(2)}) collective-permute-start(f32[7,8,128]{2,1,0:T(8,128)S(1)} %get-tuple-element.39), channel_id=1, source_target_pairs={{1,2},{2,1},{0,4},{3,31},{5,6},{6,5},{4,0},{7,27},{9,10},{10,9},{8... | collective-permute-start | bytes 86024 | tf_op jit(solution)/shard_map/ppermute | solution.py:596

commit v9 on v8

--- a/solution.py
+++ b/solution.py
@@ -471,16 +471,48 @@
     )(rows, strip, outer, inner, main, ocean, *weights, bias)
 
 
+def copy_middle(cells_ref, out_ref, sem):
+    source = cells_ref.at[:, pl.ds(0, ROWS - 16), :]
+    return pltpu.make_async_copy(source, out_ref.at[:, pl.ds(8, ROWS - 16), :], sem)
+
+
+def early_middle(lat, size):
+    return lat == size - 2
+
+
+def middle_kernel(size, cells_ref, out_ref, sem):
+    @pl.when(early_middle(lax.axis_index("lat"), size))
+    def _():
+        copy = copy_middle(cells_ref, out_ref, sem)
+        copy.start()
+        copy.wait()
+
+
+def store_middle(size, cells):
+    return pl.pallas_call(
+        functools.partial(middle_kernel, size),
+        out_shape=jax.ShapeDtypeStruct((16, ROWS, 128), F32),
+        in_specs=[VMEM],
+        out_specs=HBM,
+        scratch_shapes=[pltpu.SemaphoreType.DMA(())],
+        compiler_params=pltpu.CompilerParams(vmem_limit_bytes=LIMIT),
+        cost_estimate=pl.CostEstimate(flops=1000, bytes_accessed=800000, transcendentals=0),
+        name="store_middle",
+    )(cells)
+
+
 def border_kernel(
-    rows_ref, mask_ref, first_ref, second_ref, side_ref, pre_one_ref, pre_two_ref, pre_three_ref,
-    one_ref, two_ref, three_ref, cells_ref, low_in_ref, high_in_ref, out_ref, low_ref, high_ref, sems,
+    size, rows_ref, mask_ref, first_ref, second_ref, side_ref, pre_one_ref, pre_two_ref, pre_three_ref,
+    one_ref, two_ref, three_ref, cells_ref, low_in_ref, high_in_ref, _, out_ref, low_ref, high_ref, sems,
 ):
     lat = lax.axis_index("lat")
     even = lax.rem(lat, 2) == 0
-    span = pl.ds(8, ROWS - 16)
-    source = cells_ref.at[:, pl.ds(0, ROWS - 16), :]
-    stores = [pltpu.make_async_copy(source, out_ref.at[:, span, :], sems.at[0])]
-    stores[0].start()
+    middle = copy_middle(cells_ref, out_ref, sems.at[0])
+    late_middle = jnp.logical_not(early_middle(lat, size))
+
+    @pl.when(late_middle)
+    def _():
+        middle.start()
 
     south, north = [], []
     low, high = [], []
@@ -535,6 +567,7 @@
         total = late(weights, low, high, width)
     total = total.reshape(4, 8, 256)[0:3] + pre_three_ref[...]
 
+    stores = []
     for strip in range(2):
         ref, at, start = ((low_ref, 0, 0), (high_ref, ROWS - 8, 5))[strip]
         flat = ref.reshape(128, 128)
@@ -551,13 +584,18 @@
     for store in stores:
         store.wait()
 
-
-def border_pass(rows, mask, first, second, side, pre, late, cells, low, high):
+    @pl.when(late_middle)
+    def _():
+        middle.wait()
+
+
+def border_pass(size, rows, mask, first, second, side, pre, late, cells, low, high, out):
     return pl.pallas_call(
-        border_kernel,
+        functools.partial(border_kernel, size),
         out_shape=jax.ShapeDtypeStruct((16, ROWS, 128), F32),
-        in_specs=[VMEM] * 14,
+        in_specs=[VMEM] * 14 + [HBM],
         out_specs=HBM,
+        input_output_aliases={14: 0},
         scratch_shapes=[
             pltpu.VMEM(low.shape, F32),
             pltpu.VMEM(high.shape, F32),
@@ -566,7 +604,7 @@
         compiler_params=pltpu.CompilerParams(vmem_limit_bytes=LIMIT),
         cost_estimate=pl.CostEstimate(flops=60000000, bytes_accessed=1000000, transcendentals=60000),
         name="border_pass",
-    )(rows, mask, first, second, side, *pre, *late, cells, low, high)
+    )(rows, mask, first, second, side, *pre, *late, cells, low, high, out)
 
 
 def shards(state, land_mask, kernel_one, bias_one, kernel_two, bias_two, kernel_three, bias_three):
@@ -597,7 +635,10 @@
     cells, low, high, side, *pre = strip_pass(
         rows, strip, inner, outer, main, ocean, weights, bias
     )
-    return border_pass(rows, land_mask, first, second, side, pre, late, cells, low, high)
+    out = store_middle(lat, cells)
+    return border_pass(
+        lat, rows, land_mask, first, second, side, pre, late, cells, low, high, out
+    )
 
 
 def solution(mesh):

time: 12.8 us -> 12.8 us (level)
  waiting for transfers between devices: 2.68 us -> 1.91 us
  Pallas kernels: 6.39 us -> 7.11 us
    pallas_call x1 -> x2, Pallas kernels: 1.48 us -> 2.21 us  [the longest x1 1.45 us: border_pass(): pl.pallas_call(functools.partial(border_kernel, size), out_shape=jax.Shap...]
    ppermute x1, waiting for transfers between devices: 0.51 us -> 0.01 us  [shards(): first = lax.ppermute(first, ('lon', 'lat'), pairs(0))]
    ppermute x1, waiting for transfers between devices: 1.58 us -> 1.31 us  [shards(): second = lax.ppermute(second, ('lon', 'lat'), pairs(1))]
  transfers between devices with their start and end apart: 4 -> 4, of which waited for: 3 -> 2; matrix products, arithmetic and copies ran while one was open for 0% -> 0% of each run, Pallas kernels for 27% -> 33%
where the time goes in v9:
time: 12.8 us; the launch traced here: 12.7 us
  Pallas kernels  7.11 us (56%)
  starting transfers between devices  3.54 us (28%)
  waiting for transfers between devices  1.91 us (15%)
    ppermute x1, starting transfers between devices, shards(): lax.ppermute(outer, 'lon', [(i, (i + 1 if i % 2 else i - 1) % lon) for i...  1.95 us
    pallas_call x1, Pallas kernels, strip_pass(): pl.pallas_call(strip_kernel, out_shape=[block((16, ROWS - 8, 128), F32),...  1.77 us
    pallas_call x1, Pallas kernels, main_pass(): pl.pallas_call(functools.partial(main_kernel, size), out_shape=[block(row...  1.61 us
    ppermute x1, starting transfers between devices, shards(): first = lax.ppermute(first, ('lon', 'lat'), pairs(0))  1.58 us
    pallas_call x1, Pallas kernels, border_pass(): pl.pallas_call(functools.partial(border_kernel, size), out_shape=jax.Shap...  1.45 us
    pallas_call x1, Pallas kernels, prepare(): pl.pallas_call(prepare_kernel, out_shape=[block((ROWS, 2, 8, 128), F32),...  1.42 us
    ppermute x1, waiting for transfers between devices, shards(): second = lax.ppermute(second, ('lon', 'lat'), pairs(1))  1.31 us
    pallas_call x1, Pallas kernels, store_middle(): pl.pallas_call(functools.partial(middle_kernel, size), out_shape=jax.Shap...  0.76 us
  transfers between devices with their start and end apart: 4, of which 2 were waited for; matrix products, arithmetic and copies ran while one was open for 0% of the time, Pallas kernels for 33%

profile of v9, /device:TPU:16, one launch (start us, length us, event | category | flops | bytes accessed | tf_op | source)
XLA Modules:
  0.0 12.7 jit_solution(6655164140532876705)
XLA Ops:
  0.0 0.0 copy-start
  0.0 0.0 copy-start.1
  0.0 0.0 copy-start.2
  0.0 0.0 copy-start.3
  0.0 1.4 %rows_edges.1 = (f32[64,2,8,128]{3,2,1,0:T(8,128)S(1)}, f32[8,2,8,128]{3,2,1,0:T(8,128)S(1)}, f32[4,8,128]{2,1,0:T(8,128)S(1)}, f32[4,8,128]{2,1,0:T(8,128)S(1)}...) custom-call(f32[16,64,128]{2,1,0:T(8,128)} %state_ref.1, f32[1,16]{1,0:T(1,128)} %bitcast.3, ...), custom_call_target="tpu_custom_call" | custom-call | flops 400000 | bytes 1200000 | tf_op jit(solution)/shard_map/rows_edges/pallas_call | solution.py:136
  1.5 2.0 %collective-permute-start = (f32[4,8,128]{2,1,0:T(8,128)S(1)}, f32[4,8,128]{2,1,0:T(8,128)S(1)}, u32[]{:S(2)}, u32[]{:S(2)}) collective-permute-start(f32[4,8,128]{2,1,0:T(8,128)S(1)} %get-tuple-element.32), channel_id=1, source_target_pairs={{0,28},{4,8},{8,4},{12,16},{16,12},{20,24},{24,20},{28,0},{1,29},{... | collective-permute-start | bytes 49160 | tf_op jit(solution)/shard_map/ppermute | solution.py:617
  3.4 0.0 collective-permute-start.1
  3.4 0.0 copy-done
  3.4 0.0 copy-done.1
  3.4 0.0 copy-done.2
  3.4 0.0 copy-done.3
  3.4 1.6 %main_pass.1 = (f32[64,2,8,128]{3,2,1,0:T(8,128)S(1)}, f32[6,8,128]{2,1,0:T(8,128)S(1)}, f32[8,128]{1,0:T(8,128)S(1)}, bf16[128,512]{1,0:T(8,128)(2,1)S(1)}, bf1...) custom-call(f32[64,2,8,128]{3,2,1,0:T(8,128)S(1)} %get-tuple-element, ...), custom_call_target="tpu_custom_call" | custom-call | flops 150000000 | bytes 1500000 | tf_op jit(solution)/shard_map/main_pass/pallas_call | solution.py:320
  5.1 0.6 %collective-permute-done.outer_ref = f32[4,8,128]{2,1,0:T(8,128)S(1)} collective-permute-done((f32[4,8,128]{2,1,0:T(8,128)S(1)}, f32[4,8,128]{2,1,0:T(8,128)S(1)}, u32[]{:S(2)}, u32[]{:S(2)}) %collective-permute-start) | collective-permute-done | bytes 16416 | tf_op jit(solution)/shard_map/ppermute | solution.py:617
  5.7 0.0 collective-permute-done.1.inner_ref
  5.7 0.1 add_corners.1
  5.7 1.6 %collective-permute-start.2 = (f32[7,8,128]{2,1,0:T(8,128)S(1)}, f32[7,8,128]{2,1,0:T(8,128)S(1)}, u32[]{:S(2)}, u32[]{:S(2)}) collective-permute-start(f32[7,8,128]{2,1,0:T(8,128)S(1)} %get-tuple-element.38), channel_id=1, source_target_pairs={{0,1},{1,0},{2,3},{3,2},{4,5},{5,4},{6,7},{7,6},{8,9},{9,8},{10,11... | collective-permute-start | bytes 86024 | tf_op jit(solution)/shard_map/ppermute | solution.py:633
  7.3 0.0 collective-permute-start.3
  7.3 1.8 %strip_pass.1 = (f32[16,56,128]{2,1,0:T(8,128)S(1)}, f32[16,8,128]{2,1,0:T(8,128)S(1)}, f32[16,8,128]{2,1,0:T(8,128)S(1)}, f32[6,2,8,128]{3,2,1,0:T(8,128)S(1)},...) custom-call(f32[64,2,8,128]{3,2,1,0:T(8,128)S(1)} %get-tuple-element.31.rows_ref, ...), custom_call_target="tpu_custom_call" | custom-call | flops 150000000 | bytes 2000000 | tf_op jit(solution)/shard_map/strip_pass/pallas_call | solution.py:456
  9.1 0.8 %store_middle.1._ = f32[16,64,128]{2,1,0:T(8,128)} custom-call(f32[16,56,128]{2,1,0:T(8,128)S(1)} %get-tuple-element.54.cells_ref), custom_call_target="tpu_custom_call" | custom-call | flops 1000 | bytes 800000 | tf_op jit(solution)/shard_map/store_middle/pallas_call | solution.py:492
  9.9 0.0 collective-permute-done.2.first_ref
  9.9 1.3 %collective-permute-done.3.second_ref = f32[7,8,128]{2,1,0:T(8,128)S(1)} collective-permute-done((f32[7,8,128]{2,1,0:T(8,128)S(1)}, f32[7,8,128]{2,1,0:T(8,128)S(1)}, u32[]{:S(2)}, u32[]{:S(2)}) %collective-permute-start.3) | collective-permute-done | bytes 28704 | tf_op jit(solution)/shard_map/ppermute | solution.py:634
  11.2 1.4 %border_pass.1 = f32[16,64,128]{2,1,0:T(8,128)} custom-call(f32[64,2,8,128]{3,2,1,0:T(8,128)S(1)} %get-tuple-element.31.rows_ref, s32[64,128]{1,0:T(8,128)S(1)} %copy-done, f32[7,8,128]{2,1,0:T(8,128)S(1)} %collective-permute-done.2.first_ref, f32[7,8,128]{2,1,0:T(8,128)S(1)} %collective-permute-done.3.second_ref, ...), custom_call_target="tpu_custom_call", output_to_operand_aliasing={{}: (14, {})} | custom-call | flops 60000000 | bytes 1000000 | tf_op jit(solution)/shard_map/border_pass/pallas_call | solution.py:593
Async XLA Ops:
  0.0 3.4 %copy-start = (s32[64,128]{1,0:T(8,128)S(1)}, s32[64,128]{1,0:T(8,128)}, u32[]{:S(2)}) copy-start(s32[64,128]{1,0:T(8,128)} %mask_ref.3) | copy-start | bytes 98308
  0.0 3.4 %copy-start.1 = (bf16[3,3,16,16]{3,2,1,0:T(8,128)(2,1)S(1)}, bf16[3,3,16,16]{3,2,1,0:T(8,128)(2,1)}, u32[]{:S(2)}) copy-start(bf16[3,3,16,16]{3,2,1,0:T(8,128)(2,1)} %k_one_ref.1) | copy-start | bytes 13828
  0.0 3.4 %copy-start.2 = (bf16[3,3,16,16]{3,2,1,0:T(8,128)(2,1)S(1)}, bf16[3,3,16,16]{3,2,1,0:T(8,128)(2,1)}, u32[]{:S(2)}) copy-start(bf16[3,3,16,16]{3,2,1,0:T(8,128)(2,1)} %k_two_ref.1) | copy-start | bytes 13828
  0.0 3.4 %copy-start.3 = (bf16[3,3,8,16]{3,2,1,0:T(8,128)(2,1)S(1)}, bf16[3,3,8,16]{3,2,1,0:T(8,128)(2,1)}, u32[]{:S(2)}) copy-start(bf16[3,3,8,16]{3,2,1,0:T(8,128)(2,1)} %k_three_ref.1) | copy-start | bytes 6916
  1.5 4.2 %collective-permute-start = (f32[4,8,128]{2,1,0:T(8,128)S(1)}, f32[4,8,128]{2,1,0:T(8,128)S(1)}, u32[]{:S(2)}, u32[]{:S(2)}) collective-permute-start(f32[4,8,128]{2,1,0:T(8,128)S(1)} %get-tuple-element.32), channel_id=1, source_target_pairs={{0,28},{4,8},{8,4},{12,16},{16,12},{20,24},{24,20},{28,0},{1,29},{... | collective-permute-start | bytes 49160 | tf_op jit(solution)/shard_map/ppermute | solution.py:617
  3.4 2.3 %collective-permute-start.1 = (f32[4,8,128]{2,1,0:T(8,128)S(1)}, f32[4,8,128]{2,1,0:T(8,128)S(1)}, u32[]{:S(2)}, u32[]{:S(2)}) collective-permute-start(f32[4,8,128]{2,1,0:T(8,128)S(1)} %get-tuple-element.33), channel_id=1, source_target_pairs={{0,4},{4,0},{8,12},{12,8},{16,20},{20,16},{24,28},{28,24},{1,5},{5... | collective-permute-start | bytes 49160 | tf_op jit(solution)/shard_map/ppermute | solution.py:616
  5.7 4.1 %collective-permute-start.2 = (f32[7,8,128]{2,1,0:T(8,128)S(1)}, f32[7,8,128]{2,1,0:T(8,128)S(1)}, u32[]{:S(2)}, u32[]{:S(2)}) collective-permute-start(f32[7,8,128]{2,1,0:T(8,128)S(1)} %get-tuple-element.38), channel_id=1, source_target_pairs={{0,1},{1,0},{2,3},{3,2},{4,5},{5,4},{6,7},{7,6},{8,9},{9,8},{10,11... | collective-permute-start | bytes 86024 | tf_op jit(solution)/shard_map/ppermute | solution.py:633
  7.3 3.9 %collective-permute-start.3 = (f32[7,8,128]{2,1,0:T(8,128)S(1)}, f32[7,8,128]{2,1,0:T(8,128)S(1)}, u32[]{:S(2)}, u32[]{:S(2)}) collective-permute-start(f32[7,8,128]{2,1,0:T(8,128)S(1)} %get-tuple-element.39), channel_id=1, source_target_pairs={{1,2},{2,1},{0,4},{3,31},{5,6},{6,5},{4,0},{7,27},{9,10},{10,9},{8... | collective-permute-start | bytes 86024 | tf_op jit(solution)/shard_map/ppermute | solution.py:634

commit v10 on v8

--- a/solution.py
+++ b/solution.py
@@ -471,93 +471,152 @@
     )(rows, strip, outer, inner, main, ocean, *weights, bias)
 
 
-def border_kernel(
-    rows_ref, mask_ref, first_ref, second_ref, side_ref, pre_one_ref, pre_two_ref, pre_three_ref,
-    one_ref, two_ref, three_ref, cells_ref, low_in_ref, high_in_ref, out_ref, low_ref, high_ref, sems,
-):
-    lat = lax.axis_index("lat")
-    even = lax.rem(lat, 2) == 0
-    span = pl.ds(8, ROWS - 16)
-    source = cells_ref.at[:, pl.ds(0, ROWS - 16), :]
-    stores = [pltpu.make_async_copy(source, out_ref.at[:, span, :], sems.at[0])]
-    stores[0].start()
-
-    south, north = [], []
-    low, high = [], []
+def north_early(lat, size):
+    return (lat == size - 2) & (lat % 2 == 0)
+
+
+def join(parts):
+    return jnp.concatenate(parts, axis=-1) if len(parts) > 1 else parts[0]
+
+
+def received(strip, near_ref, far_ref, near, lat):
+    halves, wide = [], []
     for t in range(3):
-        blocks = [[], [], [], []]
+        main, side = [], []
         for half in range(2):
             at = 2 * t + half
-            corner = jnp.where(even, second_ref[6], first_ref[6])
-            x = jnp.where(even, second_ref[at], first_ref[at])
-            y = beside(corner, 32 * half + 4 + 4 * t, corner, 32 * half + 20 + 4 * t)
-            blocks[0].append(jnp.where(lat == 0, 0.0, x))
-            blocks[1].append(jnp.where(lat == 0, 0.0, y))
-            corner = jnp.where(even, first_ref[6], second_ref[6])
-            blocks[2].append(jnp.where(even, first_ref[at], second_ref[at]))
-            blocks[3].append(beside(corner, 32 * half + 4 * t, corner, 32 * half + 16 + 4 * t))
-        south.append(blocks[0])
-        north.append(blocks[2])
-        wide = [jnp.concatenate(x, axis=0) for x in blocks]
-        low.append(jnp.concatenate(wide[0:2], axis=1).astype(BF16))
-        high.append(jnp.concatenate(wide[2:4], axis=1).astype(BF16))
-
-    def late(weights, low, high, width):
-        blank = jnp.zeros((16, width), BF16)
+            x, corner = near_ref[at], near_ref[6]
+            if far_ref is not None:
+                x = jnp.where(near, x, far_ref[at])
+                corner = jnp.where(near, corner, far_ref[6])
+            y = beside(corner, 32 * half + 4 * t + 4 * (1 - strip), corner, 32 * half + 16 + 4 * t + 4 * (1 - strip))
+            if strip == 0:
+                x, y = jnp.where(lat == 0, 0.0, x), jnp.where(lat == 0, 0.0, y)
+            main.append(x)
+            side.append(y)
+        halves.append(main)
+        parts = [jnp.concatenate(main, axis=0), jnp.concatenate(side, axis=0)]
+        wide.append(jnp.concatenate(parts, axis=1).astype(BF16))
+    return halves, wide
+
+
+def complete(strips, rows, rows_ref, mask_ref, side_ref, pre, weights, blocks, out_ref, sems):
+    def late(weights, wide, width):
+        blank = [jnp.zeros((16, width), BF16)] * 2
         operand = []
         for c in range(3):
-            lows = [turn_wide(x, c)[:, 0:width] for x in low] + [blank] * 2
-            highs = [blank] * 2 + [turn_wide(x, c)[:, 0:width] for x in high]
-            operand.extend(jnp.concatenate(pair, axis=1) for pair in zip(lows, highs))
-        operand.append(jnp.zeros((16, 2 * width), BF16))
+            columns = []
+            for strip in strips:
+                x = [turn_wide(row, c)[:, 0:width] for row in wide[strip]]
+                columns.append(x + blank if strip == 0 else blank + x)
+            operand.extend(join(parts) for parts in zip(*columns))
+        operand.append(jnp.zeros((16, width * len(strips)), BF16))
         return dot(weights[...], jnp.concatenate(operand, axis=0))
 
-    total = late(one_ref, low, high, 256)
-    low_ref[...] = low_in_ref[...]
-    high_ref[...] = high_in_ref[...]
+    def shares(pre_ref, width):
+        return join([pre_ref[:, :, width * strip : width * strip + width] for strip in strips])
+
+    total = late(weights[0], {strip: rows[strip][1] for strip in strips}, 256)
+
     col = lanes()
-    own = {row: [rows_ref[row, half] for half in range(2)] for row in (0, 1, 2, 3, 60, 61, 62, 63)}
-    own[-1], own[ROWS] = south[2], north[0]
-    ready = []
-    for at, row in enumerate((0, 1, 2, ROWS - 3, ROWS - 2, ROWS - 1)):
-        q = own[row]
-        side = [side_ref[at, half] for half in range(2)]
-        e = [turn(jnp.where(col == 0, y, x), -1) for x, y in zip(q, side)]
-        w = [turn(jnp.where(col == 127, y, x), 1) for x, y in zip(q, side)]
-        new = tendency(q, own[row + 1], own[row - 1], e, w)
-        ocean = 0.1 * mask_ref[row : row + 1, :].astype(F32)
-        ready.append((q[0] + ocean * new[0], q[1] + ocean * new[1], ocean))
-
-    for pre_ref, weights, width in ((pre_one_ref, two_ref, 256), (pre_two_ref, three_ref, 128)):
-        value = silu(total.reshape(3, 16, 512) + pre_ref[...]).astype(BF16)
-        low = [value[r, :, 0:256] for r in range(3)]
-        high = [value[r, :, 256:512] for r in range(3)]
-        total = late(weights, low, high, width)
-    total = total.reshape(4, 8, 256)[0:3] + pre_three_ref[...]
-
-    for strip in range(2):
-        ref, at, start = ((low_ref, 0, 0), (high_ref, ROWS - 8, 5))[strip]
+    ready = {}
+    for strip in strips:
+        source, target = blocks[strip]
+        target[...] = source[...]
+        for t in range(3):
+            row = t if strip == 0 else ROWS - 3 + t
+            near = {i: [rows_ref[i, half] for half in range(2)] for i in (row - 1, row, row + 1) if 0 <= i < ROWS}
+            near[-1], near[ROWS] = rows[strip][0][2], rows[strip][0][0]
+            q = near[row]
+            side = [side_ref[3 * strip + t, half] for half in range(2)]
+            e = [turn(jnp.where(col == 0, y, x), -1) for x, y in zip(q, side)]
+            w = [turn(jnp.where(col == 127, y, x), 1) for x, y in zip(q, side)]
+            new = tendency(q, near[row + 1], near[row - 1], e, w)
+            ocean = 0.1 * mask_ref[row : row + 1, :].astype(F32)
+            ready[strip, t] = (q[0] + ocean * new[0], q[1] + ocean * new[1], ocean)
+
+    for layer_at, width in ((0, 256), (1, 128)):
+        value = total.reshape(3, 16, 256 * len(strips)) + shares(pre[layer_at], 256)
+        value = silu(value).astype(BF16)
+        wide = {
+            strip: [value[r, :, 256 * i : 256 * i + 256] for r in range(3)]
+            for i, strip in enumerate(strips)
+        }
+        total = late(weights[layer_at + 1], wide, width)
+    total = total.reshape(4, 8, 128 * len(strips))[0:3] + shares(pre[2], 128)
+
+    stores = []
+    for i, strip in enumerate(strips):
+        ref, at, start = (blocks[strip][1], 0, 0) if strip == 0 else (blocks[strip][1], ROWS - 8, 5)
         flat = ref.reshape(128, 128)
         for t in range(3):
-            first, second, ocean = ready[3 * strip + t]
-            forcing = total[t, :, 128 * strip : 128 * strip + 128]
-            new = (first + ocean * forcing, second)
+            first, second, ocean = ready[strip, t]
+            new = (first + ocean * total[t, :, 128 * i : 128 * i + 128], second)
             row = start + t
             for half in range(2):
                 flat[pl.ds(64 * half + row, 8, stride=8), :] = new[half]
         store = pltpu.make_async_copy(ref, out_ref.at[:, pl.ds(at, 8), :], sems.at[1 + strip])
         store.start()
         stores.append(store)
-    for store in stores:
-        store.wait()
-
-
-def border_pass(rows, mask, first, second, side, pre, late, cells, low, high):
+    return stores
+
+
+def copy_middle(cells_ref, out_ref, sem):
+    source = cells_ref.at[:, pl.ds(0, ROWS - 16), :]
+    return pltpu.make_async_copy(source, out_ref.at[:, pl.ds(8, ROWS - 16), :], sem)
+
+
+def border_kernel(size, last, *refs):
+    rows_ref, mask_ref, first_ref, *refs = refs
+    if last:
+        second_ref, *refs = refs
+    side_ref, *refs = refs
+    pre, weights, refs = refs[0:3], refs[3:6], refs[6:]
+    cells_ref, low_in_ref, high_in_ref, *refs = refs
+    out_ref, low_ref, high_ref, sems = refs[1:] if last else refs
+    lat = lax.axis_index("lat")
+    even = lat % 2 == 0
+    early = north_early(lat, size)
+    blocks = ((low_in_ref, low_ref), (high_in_ref, high_ref))
+
+    def run(strips, middle, rows):
+        stores = []
+        if middle:
+            stores.append(copy_middle(cells_ref, out_ref, sems.at[0]))
+            stores[0].start()
+        stores += complete(
+            strips, rows, rows_ref, mask_ref, side_ref, pre, weights, blocks, out_ref, sems
+        )
+        for store in stores:
+            store.wait()
+
+    if not last:
+
+        @pl.when(early)
+        def _():
+            run((1,), True, {1: received(1, first_ref, None, even, lat)})
+
+        return
+
+    @pl.when(early)
+    def _():
+        run((0,), False, {0: received(0, second_ref, None, even, lat)})
+
+    @pl.when(jnp.logical_not(early))
+    def _():
+        low = received(0, second_ref, first_ref, even, lat)
+        run((0, 1), True, {0: low, 1: received(1, first_ref, second_ref, even, lat)})
+
+
+def border_pass(size, rows, mask, messages, side, pre, late, cells, low, high, out=()):
+    last = len(out) > 0
+    operands = (rows, mask, *messages, side, *pre, *late, cells, low, high)
     return pl.pallas_call(
-        border_kernel,
+        functools.partial(border_kernel, size, last),
         out_shape=jax.ShapeDtypeStruct((16, ROWS, 128), F32),
-        in_specs=[VMEM] * 14,
+        in_specs=[VMEM] * len(operands) + [HBM] * len(out),
         out_specs=HBM,
+        input_output_aliases={len(operands): 0} if last else {},
         scratch_shapes=[
             pltpu.VMEM(low.shape, F32),
             pltpu.VMEM(high.shape, F32),
@@ -565,8 +624,8 @@
         ],
         compiler_params=pltpu.CompilerParams(vmem_limit_bytes=LIMIT),
         cost_estimate=pl.CostEstimate(flops=60000000, bytes_accessed=1000000, transcendentals=60000),
-        name="border_pass",
-    )(rows, mask, first, second, side, *pre, *late, cells, low, high)
+        name="border_pass" if last else "north_strip",
+    )(*operands, *out)
 
 
 def shards(state, land_mask, kernel_one, bias_one, kernel_two, bias_two, kernel_three, bias_three):
@@ -597,7 +656,9 @@
     cells, low, high, side, *pre = strip_pass(
         rows, strip, inner, outer, main, ocean, weights, bias
     )
-    return border_pass(rows, land_mask, first, second, side, pre, late, cells, low, high)
+    held = (side, pre, late, cells, low, high)
+    out = border_pass(lat, rows, land_mask, (first,), *held)
+    return border_pass(lat, rows, land_mask, (first, second), *held, (out,))
 
 
 def solution(mesh):

time: 12.8 us -> 12.7 us (level)
  waiting for transfers between devices: 2.68 us -> 1.27 us
  Pallas kernels: 6.39 us -> 7.71 us
    ppermute x1, waiting for transfers between devices: 1.58 us -> 0.17 us  [shards(): second = lax.ppermute(second, ('lon', 'lat'), pairs(1))]
    pallas_call x1 -> x2, Pallas kernels: 1.48 us -> 2.79 us  [border_pass(): pl.pallas_call(functools.partial(border_kernel, size, last), out_shape=ja...]
  transfers between devices with their start and end apart: 4 -> 4, of which waited for: 3 -> 3; matrix products, arithmetic and copies ran while one was open for 0% -> 0% of each run, Pallas kernels for 27% -> 38%
where the time goes in v10:
time: 12.7 us; the launch traced here: 12.6 us
  Pallas kernels  7.71 us (61%)
  starting transfers between devices  3.54 us (28%)
  waiting for transfers between devices  1.27 us (10%)
    pallas_call x2, Pallas kernels, border_pass(): pl.pallas_call(functools.partial(border_kernel, size, last), out_shape=ja...  2.79 us
    ppermute x1, starting transfers between devices, shards(): lax.ppermute(outer, 'lon', [(i, (i + 1 if i % 2 else i - 1) % lon) for i...  1.95 us
    pallas_call x1, Pallas kernels, strip_pass(): pl.pallas_call(strip_kernel, out_shape=[block((16, ROWS - 8, 128), F32),...  1.77 us
    pallas_call x1, Pallas kernels, main_pass(): pl.pallas_call(functools.partial(main_kernel, size), out_shape=[block(row...  1.63 us
    ppermute x1, starting transfers between devices, shards(): first = lax.ppermute(first, ('lon', 'lat'), pairs(0))  1.58 us
    pallas_call x1, Pallas kernels, prepare(): pl.pallas_call(prepare_kernel, out_shape=[block((ROWS, 2, 8, 128), F32),...  1.42 us
    ppermute x1, waiting for transfers between devices, shards(): lax.ppermute(outer, 'lon', [(i, (i + 1 if i % 2 else i - 1) % lon) for i...  0.58 us
    ppermute x1, waiting for transfers between devices, shards(): first = lax.ppermute(first, ('lon', 'lat'), pairs(0))  0.51 us
  transfers between devices with their start and end apart: 4, of which 3 were waited for; matrix products, arithmetic and copies ran while one was open for 0% of the time, Pallas kernels for 38%

profile of v10, /device:TPU:16, one launch (start us, length us, event | category | flops | bytes accessed | tf_op | source)
XLA Modules:
  0.0 12.6 jit_solution(3743573970926846761)
XLA Ops:
  0.0 0.0 copy-start
  0.0 0.0 copy-start.1
  0.0 0.0 copy-start.2
  0.0 0.0 copy-start.3
  0.0 1.4 %rows_edges.1 = (f32[64,2,8,128]{3,2,1,0:T(8,128)S(1)}, f32[8,2,8,128]{3,2,1,0:T(8,128)S(1)}, f32[4,8,128]{2,1,0:T(8,128)S(1)}, f32[4,8,128]{2,1,0:T(8,128)S(1)}...) custom-call(f32[16,64,128]{2,1,0:T(8,128)} %state_ref.1, f32[1,16]{1,0:T(1,128)} %bitcast.3, ...), custom_call_target="tpu_custom_call" | custom-call | flops 400000 | bytes 1200000 | tf_op jit(solution)/shard_map/rows_edges/pallas_call | solution.py:136
  1.5 2.0 %collective-permute-start = (f32[4,8,128]{2,1,0:T(8,128)S(1)}, f32[4,8,128]{2,1,0:T(8,128)S(1)}, u32[]{:S(2)}, u32[]{:S(2)}) collective-permute-start(f32[4,8,128]{2,1,0:T(8,128)S(1)} %get-tuple-element.32), channel_id=1, source_target_pairs={{0,28},{4,8},{8,4},{12,16},{16,12},{20,24},{24,20},{28,0},{1,29},{... | collective-permute-start | bytes 49160 | tf_op jit(solution)/shard_map/ppermute | solution.py:638
  3.4 0.0 collective-permute-start.1
  3.4 0.0 copy-done
  3.4 0.0 copy-done.1
  3.4 0.0 copy-done.2
  3.4 0.0 copy-done.3
  3.4 1.6 %main_pass.1 = (f32[64,2,8,128]{3,2,1,0:T(8,128)S(1)}, f32[6,8,128]{2,1,0:T(8,128)S(1)}, f32[8,128]{1,0:T(8,128)S(1)}, bf16[128,512]{1,0:T(8,128)(2,1)S(1)}, bf1...) custom-call(f32[64,2,8,128]{3,2,1,0:T(8,128)S(1)} %get-tuple-element, ...), custom_call_target="tpu_custom_call" | custom-call | flops 150000000 | bytes 1500000 | tf_op jit(solution)/shard_map/main_pass/pallas_call | solution.py:320
  5.1 0.6 %collective-permute-done.outer_ref = f32[4,8,128]{2,1,0:T(8,128)S(1)} collective-permute-done((f32[4,8,128]{2,1,0:T(8,128)S(1)}, f32[4,8,128]{2,1,0:T(8,128)S(1)}, u32[]{:S(2)}, u32[]{:S(2)}) %collective-permute-start) | collective-permute-done | bytes 16416 | tf_op jit(solution)/shard_map/ppermute | solution.py:638
  5.7 0.0 collective-permute-done.1.inner_ref
  5.7 0.1 add_corners.1
  5.7 1.6 %collective-permute-start.2 = (f32[7,8,128]{2,1,0:T(8,128)S(1)}, f32[7,8,128]{2,1,0:T(8,128)S(1)}, u32[]{:S(2)}, u32[]{:S(2)}) collective-permute-start(f32[7,8,128]{2,1,0:T(8,128)S(1)} %get-tuple-element.38), channel_id=1, source_target_pairs={{0,1},{1,0},{2,3},{3,2},{4,5},{5,4},{6,7},{7,6},{8,9},{9,8},{10,11... | collective-permute-start | bytes 86024 | tf_op jit(solution)/shard_map/ppermute | solution.py:654
  7.3 0.0 collective-permute-start.3
  7.3 1.8 %strip_pass.1 = (f32[16,56,128]{2,1,0:T(8,128)S(1)}, f32[16,8,128]{2,1,0:T(8,128)S(1)}, f32[16,8,128]{2,1,0:T(8,128)S(1)}, f32[6,2,8,128]{3,2,1,0:T(8,128)S(1)},...) custom-call(f32[64,2,8,128]{3,2,1,0:T(8,128)S(1)} %get-tuple-element.31.rows_ref.refs_0_, ...), custom_call_target="tpu_custom_call" | custom-call | flops 150000000 | bytes 2000000 | tf_op jit(solution)/shard_map/strip_pass/pallas_call | solution.py:456
  9.1 0.5 %collective-permute-done.2.refs_2_ = f32[7,8,128]{2,1,0:T(8,128)S(1)} collective-permute-done((f32[7,8,128]{2,1,0:T(8,128)S(1)}, f32[7,8,128]{2,1,0:T(8,128)S(1)}, u32[]{:S(2)}, u32[]{:S(2)}) %collective-permute-start.2) | collective-permute-done | bytes 28704 | tf_op jit(solution)/shard_map/ppermute | solution.py:654
  9.6 1.4 %north_strip.1.refs_14_ = f32[16,64,128]{2,1,0:T(8,128)} custom-call(f32[64,2,8,128]{3,2,1,0:T(8,128)S(1)} %get-tuple-element.31.rows_ref.refs_0_, s32[64,128]{1,0:T(8,128)S(1)} %copy-done, f32[7,8,128]{2,1,0:T(8,128)S(1)} %collective-permute-done.2.refs_2_, f32[6,2,8,128]{3,2,1,0:T(8,128)S(1)} %get-tuple-element.47.refs_3_.refs_4_, ...), custom_call_target="tpu_custom_call" | custom-call | flops 60000000 | bytes 1000000 | tf_op jit(solution)/shard_map/north_strip/pallas_call | solution.py:614
  11.0 0.2 %collective-permute-done.3.refs_3_ = f32[7,8,128]{2,1,0:T(8,128)S(1)} collective-permute-done((f32[7,8,128]{2,1,0:T(8,128)S(1)}, f32[7,8,128]{2,1,0:T(8,128)S(1)}, u32[]{:S(2)}, u32[]{:S(2)}) %collective-permute-start.3) | collective-permute-done | bytes 28704 | tf_op jit(solution)/shard_map/ppermute | solution.py:655
  11.2 1.4 %border_pass.1 = f32[16,64,128]{2,1,0:T(8,128)} custom-call(f32[64,2,8,128]{3,2,1,0:T(8,128)S(1)} %get-tuple-element.31.rows_ref.refs_0_, s32[64,128]{1,0:T(8,128)S(1)} %copy-done, f32[7,8,128]{2,1,0:T(8,128)S(1)} %collective-permute-done.2.refs_2_, f32[7,8,128]{2,1,0:T(8,128)S(1)} %collective-permute-done.3.refs_3_, ...), custom_call_target="tpu_custom_call", output_to_operand_aliasing={{}: (14, {})} | custom-call | flops 60000000 | bytes 1000000 | tf_op jit(solution)/shard_map/border_pass/pallas_call | solution.py:614
Async XLA Ops:
  0.0 3.4 %copy-start = (s32[64,128]{1,0:T(8,128)S(1)}, s32[64,128]{1,0:T(8,128)}, u32[]{:S(2)}) copy-start(s32[64,128]{1,0:T(8,128)} %refs_1_.3) | copy-start | bytes 98308
  0.0 3.4 %copy-start.1 = (bf16[3,3,16,16]{3,2,1,0:T(8,128)(2,1)S(1)}, bf16[3,3,16,16]{3,2,1,0:T(8,128)(2,1)}, u32[]{:S(2)}) copy-start(bf16[3,3,16,16]{3,2,1,0:T(8,128)(2,1)} %k_one_ref.1) | copy-start | bytes 13828
  0.0 3.4 %copy-start.2 = (bf16[3,3,16,16]{3,2,1,0:T(8,128)(2,1)S(1)}, bf16[3,3,16,16]{3,2,1,0:T(8,128)(2,1)}, u32[]{:S(2)}) copy-start(bf16[3,3,16,16]{3,2,1,0:T(8,128)(2,1)} %k_two_ref.1) | copy-start | bytes 13828
  0.0 3.4 %copy-start.3 = (bf16[3,3,8,16]{3,2,1,0:T(8,128)(2,1)S(1)}, bf16[3,3,8,16]{3,2,1,0:T(8,128)(2,1)}, u32[]{:S(2)}) copy-start(bf16[3,3,8,16]{3,2,1,0:T(8,128)(2,1)} %k_three_ref.1) | copy-start | bytes 6916
  1.5 4.2 %collective-permute-start = (f32[4,8,128]{2,1,0:T(8,128)S(1)}, f32[4,8,128]{2,1,0:T(8,128)S(1)}, u32[]{:S(2)}, u32[]{:S(2)}) collective-permute-start(f32[4,8,128]{2,1,0:T(8,128)S(1)} %get-tuple-element.32), channel_id=1, source_target_pairs={{0,28},{4,8},{8,4},{12,16},{16,12},{20,24},{24,20},{28,0},{1,29},{... | collective-permute-start | bytes 49160 | tf_op jit(solution)/shard_map/ppermute | solution.py:638
  3.4 2.3 %collective-permute-start.1 = (f32[4,8,128]{2,1,0:T(8,128)S(1)}, f32[4,8,128]{2,1,0:T(8,128)S(1)}, u32[]{:S(2)}, u32[]{:S(2)}) collective-permute-start(f32[4,8,128]{2,1,0:T(8,128)S(1)} %get-tuple-element.33), channel_id=1, source_target_pairs={{0,4},{4,0},{8,12},{12,8},{16,20},{20,16},{24,28},{28,24},{1,5},{5... | collective-permute-start | bytes 49160 | tf_op jit(solution)/shard_map/ppermute | solution.py:637
  5.7 3.9 %collective-permute-start.2 = (f32[7,8,128]{2,1,0:T(8,128)S(1)}, f32[7,8,128]{2,1,0:T(8,128)S(1)}, u32[]{:S(2)}, u32[]{:S(2)}) collective-permute-start(f32[7,8,128]{2,1,0:T(8,128)S(1)} %get-tuple-element.38), channel_id=1, source_target_pairs={{0,1},{1,0},{2,3},{3,2},{4,5},{5,4},{6,7},{7,6},{8,9},{9,8},{10,11... | collective-permute-start | bytes 86024 | tf_op jit(solution)/shard_map/ppermute | solution.py:654
  7.3 3.9 %collective-permute-start.3 = (f32[7,8,128]{2,1,0:T(8,128)S(1)}, f32[7,8,128]{2,1,0:T(8,128)S(1)}, u32[]{:S(2)}, u32[]{:S(2)}) collective-permute-start(f32[7,8,128]{2,1,0:T(8,128)S(1)} %get-tuple-element.39), channel_id=1, source_target_pairs={{1,2},{2,1},{0,4},{3,31},{5,6},{6,5},{4,0},{7,27},{9,10},{10,9},{8... | collective-permute-start | bytes 86024 | tf_op jit(solution)/shard_map/ppermute | solution.py:655

commit v11 on v10

--- a/solution.py
+++ b/solution.py
@@ -86,7 +86,7 @@
 
 def prepare_kernel(
     state_ref, b_one_ref, b_two_ref, b_three_ref,
-    rows_ref, strip_ref, outer_ref, inner_ref, h_one_ref, h_two_ref, h_three_ref, cells_ref, sems,
+    cells_ref, strip_ref, outer_ref, inner_ref, h_one_ref, h_two_ref, h_three_ref, sems,
 ):
     fetches = []
     for half in range(2):
@@ -114,7 +114,6 @@
         for half in range(2):
             for r in range(8):
                 x = flat[pl.ds(8 * PITCH * half + 8 * b + r, 8, stride=PITCH), :]
-                rows_ref[8 * b + r, half] = x
                 strip[half][r] = jnp.where(group == b, turn(x, 6 + 16 * b), strip[half][r])
     for target, shift in zip((outer_ref, inner_ref), shifts):
         for q in range(2):
@@ -136,7 +135,7 @@
     return pl.pallas_call(
         prepare_kernel,
         out_shape=[
-            block((ROWS, 2, 8, 128), F32),
+            block((16, PITCH, 128), F32),
             block((8, 2, 8, 128), F32),
             block((4, 8, 128), F32),
             block((4, 8, 128), F32),
@@ -144,7 +143,7 @@
         ],
         in_specs=[HBM] * 4,
         out_specs=[VMEM] * 7,
-        scratch_shapes=[pltpu.VMEM((16, PITCH, 128), F32), pltpu.SemaphoreType.DMA((5,))],
+        scratch_shapes=[pltpu.SemaphoreType.DMA((5,))],
         compiler_params=pltpu.CompilerParams(vmem_limit_bytes=LIMIT),
         cost_estimate=pl.CostEstimate(flops=400000, bytes_accessed=1200000, transcendentals=0),
         name="rows_edges",
@@ -223,18 +222,23 @@
 
 
 def main_kernel(
-    size, rows_ref, mask_ref, k_one_ref, k_two_ref, k_three_ref, b_one_ref, b_two_ref, b_three_ref,
-    out_ref, north_ref, ocean_ref, one_ref, two_ref, three_ref,
+    size, cells_ref, mask_ref, k_one_ref, k_two_ref, k_three_ref, b_one_ref, b_two_ref, b_three_ref,
+    rows_ref, out_ref, north_ref, ocean_ref, one_ref, two_ref, three_ref,
     late_one_ref, late_two_ref, late_three_ref, bias_ref,
     wide_ref, narrow_ref, first_ref, second_ref, third_ref,
 ):
+    flat = cells_ref.reshape(16 * PITCH, 128)
+
+    def load(row, half):
+        return flat[pl.ds(8 * PITCH * half + row, 8, stride=PITCH), :]
+
     top = lax.axis_index("lat") == size - 1
     col = lanes()
     for t in range(3):
         for half in range(2):
-            folded = jnp.take_along_axis(rows_ref[ROWS - 1 - t, half], 127 - col, axis=1)
+            folded = jnp.take_along_axis(load(ROWS - 1 - t, half), 127 - col, axis=1)
             folded = -folded if half == 0 else folded
-            north_ref[2 * t + half] = jnp.where(top, folded, rows_ref[ROWS - 3 + t, half])
+            north_ref[2 * t + half] = jnp.where(top, folded, load(ROWS - 3 + t, half))
     ocean = jnp.zeros((8, 128), F32)
     for b in range(8):
         x = 0.1 * mask_ref[8 * b : 8 * b + 8, :].astype(F32)
@@ -262,7 +266,10 @@
                 ref[c, row] = jnp.zeros((16, 128), BF16)
 
     for row in range(ROWS):
-        x = jnp.concatenate([rows_ref[row, 0], rows_ref[row, 1]], axis=0).astype(BF16)
+        x = [load(row, half) for half in range(2)]
+        for half in range(2):
+            rows_ref[row, half] = x[half]
+        x = jnp.concatenate(x, axis=0).astype(BF16)
         for c in range(3):
             first_ref[c, row + 1] = turn(x, 1 - c)
 
@@ -314,13 +321,13 @@
                     out_ref[row, half] = q[half] + ocean * new[half]
 
 
-def main_pass(size, rows, mask, parameters):
+def main_pass(size, cells, mask, parameters):
     taps = pltpu.VMEM((3, ROWS + 4, 16, 128), BF16)
     block = jax.ShapeDtypeStruct
     return pl.pallas_call(
         functools.partial(main_kernel, size),
         out_shape=[
-            block(rows.shape, F32),
+            *[block((ROWS, 2, 8, 128), F32)] * 2,
             block((6, 8, 128), F32),
             block((8, 128), F32),
             *[block((n, DEPTH), BF16) for n in (128, 128, 64)],
@@ -328,7 +335,7 @@
             block((40, 128), F32),
         ],
         in_specs=[VMEM] * 8,
-        out_specs=[VMEM] * 10,
+        out_specs=[VMEM] * 11,
         scratch_shapes=[
             pltpu.VMEM((2, 9, 16, 128), BF16),
             pltpu.VMEM((9, 8, 128), F32),
@@ -339,7 +346,7 @@
             flops=150000000, bytes_accessed=1500000, transcendentals=300000
         ),
         name="main_pass",
-    )(rows, mask, *parameters)
+    )(cells, mask, *parameters)
 
 
 def taps(rows, count):
@@ -631,12 +638,12 @@
 def shards(state, land_mask, kernel_one, bias_one, kernel_two, bias_two, kernel_three, bias_three):
     lon, lat = (lax.axis_size("lon"), lax.axis_size("lat"))
     biases = [x.reshape(1, x.shape[0]) for x in (bias_one, bias_two, bias_three)]
-    rows, strip, outer, inner, *biases = prepare(state, biases)
+    cells, strip, outer, inner, *biases = prepare(state, biases)
     parameters = (kernel_one, kernel_two, kernel_three, *biases)
 
     inner = lax.ppermute(inner, "lon", [(i, i + 1 - 2 * (i % 2)) for i in range(lon)])
     outer = lax.ppermute(outer, "lon", [(i, (i + 1 if i % 2 else i - 1) % lon) for i in range(lon)])
-    main, north, ocean, *weights, bias = main_pass(lat, rows, land_mask, parameters)
+    rows, main, north, ocean, *weights, bias = main_pass(lat, cells, land_mask, parameters)
     weights, late = weights[0:3], weights[3:6]
 
     def pairs(parity):

time: 12.7 us -> 12.7 us (level)
  no operation moved by 1% of the time
where the time goes in v11:
time: 12.7 us; the launch traced here: 12.6 us
  Pallas kernels  7.69 us (61%)
  starting transfers between devices  3.54 us (28%)
  waiting for transfers between devices  1.26 us (10%)
    pallas_call x2, Pallas kernels, border_pass(): pl.pallas_call(functools.partial(border_kernel, size, last), out_shape=ja...  2.79 us
    ppermute x1, starting transfers between devices, shards(): lax.ppermute(outer, 'lon', [(i, (i + 1 if i % 2 else i - 1) % lon) for i...  1.95 us
    pallas_call x1, Pallas kernels, strip_pass(): pl.pallas_call(strip_kernel, out_shape=[block((16, ROWS - 8, 128), F32),...  1.78 us
    pallas_call x1, Pallas kernels, main_pass(): pl.pallas_call(functools.partial(main_kernel, size), out_shape=[*[block((...  1.64 us
    ppermute x1, starting transfers between devices, shards(): first = lax.ppermute(first, ('lon', 'lat'), pairs(0))  1.58 us
    pallas_call x1, Pallas kernels, prepare(): pl.pallas_call(prepare_kernel, out_shape=[block((16, PITCH, 128), F32), b...  1.39 us
    ppermute x1, waiting for transfers between devices, shards(): lax.ppermute(outer, 'lon', [(i, (i + 1 if i % 2 else i - 1) % lon) for i...  0.57 us
    ppermute x1, waiting for transfers between devices, shards(): first = lax.ppermute(first, ('lon', 'lat'), pairs(0))  0.51 us
  transfers between devices with their start and end apart: 4, of which 3 were waited for; matrix products, arithmetic and copies ran while one was open for 0% of the time, Pallas kernels for 38%

profile of v11, /device:TPU:16, one launch (start us, length us, event | category | flops | bytes accessed | tf_op | source)
XLA Modules:
  0.0 12.6 jit_solution(1137800614248950436)
XLA Ops:
  0.0 0.0 copy-start
  0.0 0.0 copy-start.1
  0.0 0.0 copy-start.2
  0.0 0.0 copy-start.3
  0.0 1.4 %rows_edges.1 = (f32[16,72,128]{2,1,0:T(8,128)S(1)}, f32[8,2,8,128]{3,2,1,0:T(8,128)S(1)}, f32[4,8,128]{2,1,0:T(8,128)S(1)}, f32[4,8,128]{2,1,0:T(8,128)S(1)}, f...) custom-call(f32[16,64,128]{2,1,0:T(8,128)} %state_ref.1, f32[1,16]{1,0:T(1,128)} %bitcast.3, ...), custom_call_target="tpu_custom_call" | custom-call | flops 400000 | bytes 1200000 | tf_op jit(solution)/shard_map/rows_edges/pallas_call | solution.py:135
  1.4 2.0 %collective-permute-start = (f32[4,8,128]{2,1,0:T(8,128)S(1)}, f32[4,8,128]{2,1,0:T(8,128)S(1)}, u32[]{:S(2)}, u32[]{:S(2)}) collective-permute-start(f32[4,8,128]{2,1,0:T(8,128)S(1)} %get-tuple-element.37), channel_id=1, source_target_pairs={{0,28},{4,8},{8,4},{12,16},{16,12},{20,24},{24,20},{28,0},{1,29},{... | collective-permute-start | bytes 49160 | tf_op jit(solution)/shard_map/ppermute | solution.py:645
  3.4 0.0 collective-permute-start.1
  3.4 0.0 copy-done
  3.4 0.0 copy-done.1
  3.4 0.0 copy-done.2
  3.4 0.0 copy-done.3
  3.4 1.6 %main_pass.1 = (f32[64,2,8,128]{3,2,1,0:T(8,128)S(1)}, f32[64,2,8,128]{3,2,1,0:T(8,128)S(1)}, f32[6,8,128]{2,1,0:T(8,128)S(1)}, f32[8,128]{1,0:T(8,128)S(1)}, bf...) custom-call(f32[16,72,128]{2,1,0:T(8,128)S(1)} %get-tuple-element.32, ...), custom_call_target="tpu_custom_call" | custom-call | flops 150000000 | bytes 1500000 | tf_op jit(solution)/shard_map/main_pass/pallas_call | solution.py:327
  5.1 0.6 %collective-permute-done.outer_ref = f32[4,8,128]{2,1,0:T(8,128)S(1)} collective-permute-done((f32[4,8,128]{2,1,0:T(8,128)S(1)}, f32[4,8,128]{2,1,0:T(8,128)S(1)}, u32[]{:S(2)}, u32[]{:S(2)}) %collective-permute-start) | collective-permute-done | bytes 16416 | tf_op jit(solution)/shard_map/ppermute | solution.py:645
  5.6 0.0 collective-permute-done.1.inner_ref
  5.6 0.1 add_corners.1
  5.7 1.6 %collective-permute-start.2 = (f32[7,8,128]{2,1,0:T(8,128)S(1)}, f32[7,8,128]{2,1,0:T(8,128)S(1)}, u32[]{:S(2)}, u32[]{:S(2)}) collective-permute-start(f32[7,8,128]{2,1,0:T(8,128)S(1)} %get-tuple-element.40), channel_id=1, source_target_pairs={{0,1},{1,0},{2,3},{3,2},{4,5},{5,4},{6,7},{7,6},{8,9},{9,8},{10,11... | collective-permute-start | bytes 86024 | tf_op jit(solution)/shard_map/ppermute | solution.py:661
  7.3 0.0 collective-permute-start.3
  7.3 1.8 %strip_pass.1 = (f32[16,56,128]{2,1,0:T(8,128)S(1)}, f32[16,8,128]{2,1,0:T(8,128)S(1)}, f32[16,8,128]{2,1,0:T(8,128)S(1)}, f32[6,2,8,128]{3,2,1,0:T(8,128)S(1)},...) custom-call(f32[64,2,8,128]{3,2,1,0:T(8,128)S(1)} %get-tuple-element.36.rows_ref.refs_0_, ...), custom_call_target="tpu_custom_call" | custom-call | flops 150000000 | bytes 2000000 | tf_op jit(solution)/shard_map/strip_pass/pallas_call | solution.py:463
  9.1 0.5 %collective-permute-done.2.refs_2_ = f32[7,8,128]{2,1,0:T(8,128)S(1)} collective-permute-done((f32[7,8,128]{2,1,0:T(8,128)S(1)}, f32[7,8,128]{2,1,0:T(8,128)S(1)}, u32[]{:S(2)}, u32[]{:S(2)}) %collective-permute-start.2) | collective-permute-done | bytes 28704 | tf_op jit(solution)/shard_map/ppermute | solution.py:661
  9.6 1.4 %north_strip.1.refs_14_ = f32[16,64,128]{2,1,0:T(8,128)} custom-call(f32[64,2,8,128]{3,2,1,0:T(8,128)S(1)} %get-tuple-element.36.rows_ref.refs_0_, s32[64,128]{1,0:T(8,128)S(1)} %copy-done, f32[7,8,128]{2,1,0:T(8,128)S(1)} %collective-permute-done.2.refs_2_, f32[6,2,8,128]{3,2,1,0:T(8,128)S(1)} %get-tuple-element.49.refs_3_.refs_4_, ...), custom_call_target="tpu_custom_call" | custom-call | flops 60000000 | bytes 1000000 | tf_op jit(solution)/shard_map/north_strip/pallas_call | solution.py:621
  11.0 0.2 %collective-permute-done.3.refs_3_ = f32[7,8,128]{2,1,0:T(8,128)S(1)} collective-permute-done((f32[7,8,128]{2,1,0:T(8,128)S(1)}, f32[7,8,128]{2,1,0:T(8,128)S(1)}, u32[]{:S(2)}, u32[]{:S(2)}) %collective-permute-start.3) | collective-permute-done | bytes 28704 | tf_op jit(solution)/shard_map/ppermute | solution.py:662
  11.2 1.4 %border_pass.1 = f32[16,64,128]{2,1,0:T(8,128)} custom-call(f32[64,2,8,128]{3,2,1,0:T(8,128)S(1)} %get-tuple-element.36.rows_ref.refs_0_, s32[64,128]{1,0:T(8,128)S(1)} %copy-done, f32[7,8,128]{2,1,0:T(8,128)S(1)} %collective-permute-done.2.refs_2_, f32[7,8,128]{2,1,0:T(8,128)S(1)} %collective-permute-done.3.refs_3_, ...), custom_call_target="tpu_custom_call", output_to_operand_aliasing={{}: (14, {})} | custom-call | flops 60000000 | bytes 1000000 | tf_op jit(solution)/shard_map/border_pass/pallas_call | solution.py:621
Async XLA Ops:
  0.0 3.4 %copy-start = (s32[64,128]{1,0:T(8,128)S(1)}, s32[64,128]{1,0:T(8,128)}, u32[]{:S(2)}) copy-start(s32[64,128]{1,0:T(8,128)} %refs_1_.3) | copy-start | bytes 98308
  0.0 3.4 %copy-start.1 = (bf16[3,3,16,16]{3,2,1,0:T(8,128)(2,1)S(1)}, bf16[3,3,16,16]{3,2,1,0:T(8,128)(2,1)}, u32[]{:S(2)}) copy-start(bf16[3,3,16,16]{3,2,1,0:T(8,128)(2,1)} %k_one_ref.1) | copy-start | bytes 13828
  0.0 3.4 %copy-start.2 = (bf16[3,3,16,16]{3,2,1,0:T(8,128)(2,1)S(1)}, bf16[3,3,16,16]{3,2,1,0:T(8,128)(2,1)}, u32[]{:S(2)}) copy-start(bf16[3,3,16,16]{3,2,1,0:T(8,128)(2,1)} %k_two_ref.1) | copy-start | bytes 13828
  0.0 3.4 %copy-start.3 = (bf16[3,3,8,16]{3,2,1,0:T(8,128)(2,1)S(1)}, bf16[3,3,8,16]{3,2,1,0:T(8,128)(2,1)}, u32[]{:S(2)}) copy-start(bf16[3,3,8,16]{3,2,1,0:T(8,128)(2,1)} %k_three_ref.1) | copy-start | bytes 6916
  1.4 4.2 %collective-permute-start = (f32[4,8,128]{2,1,0:T(8,128)S(1)}, f32[4,8,128]{2,1,0:T(8,128)S(1)}, u32[]{:S(2)}, u32[]{:S(2)}) collective-permute-start(f32[4,8,128]{2,1,0:T(8,128)S(1)} %get-tuple-element.37), channel_id=1, source_target_pairs={{0,28},{4,8},{8,4},{12,16},{16,12},{20,24},{24,20},{28,0},{1,29},{... | collective-permute-start | bytes 49160 | tf_op jit(solution)/shard_map/ppermute | solution.py:645
  3.4 2.3 %collective-permute-start.1 = (f32[4,8,128]{2,1,0:T(8,128)S(1)}, f32[4,8,128]{2,1,0:T(8,128)S(1)}, u32[]{:S(2)}, u32[]{:S(2)}) collective-permute-start(f32[4,8,128]{2,1,0:T(8,128)S(1)} %get-tuple-element.38), channel_id=1, source_target_pairs={{0,4},{4,0},{8,12},{12,8},{16,20},{20,16},{24,28},{28,24},{1,5},{5... | collective-permute-start | bytes 49160 | tf_op jit(solution)/shard_map/ppermute | solution.py:644
  5.7 3.9 %collective-permute-start.2 = (f32[7,8,128]{2,1,0:T(8,128)S(1)}, f32[7,8,128]{2,1,0:T(8,128)S(1)}, u32[]{:S(2)}, u32[]{:S(2)}) collective-permute-start(f32[7,8,128]{2,1,0:T(8,128)S(1)} %get-tuple-element.40), channel_id=1, source_target_pairs={{0,1},{1,0},{2,3},{3,2},{4,5},{5,4},{6,7},{7,6},{8,9},{9,8},{10,11... | collective-permute-start | bytes 86024 | tf_op jit(solution)/shard_map/ppermute | solution.py:661
  7.3 3.9 %collective-permute-start.3 = (f32[7,8,128]{2,1,0:T(8,128)S(1)}, f32[7,8,128]{2,1,0:T(8,128)S(1)}, u32[]{:S(2)}, u32[]{:S(2)}) collective-permute-start(f32[7,8,128]{2,1,0:T(8,128)S(1)} %get-tuple-element.41), channel_id=1, source_target_pairs={{1,2},{2,1},{0,4},{3,31},{5,6},{6,5},{4,0},{7,27},{9,10},{10,9},{8... | collective-permute-start | bytes 86024 | tf_op jit(solution)/shard_map/ppermute | solution.py:662

commit v12 on v11

--- a/solution.py
+++ b/solution.py
@@ -109,22 +109,29 @@
     ]
     for fetch in fetches[0:2]:
         fetch.wait()
-    strip = [[jnp.zeros((8, 128), F32)] * 8 for half in range(2)]
-    for b in range(8):
-        for half in range(2):
-            for r in range(8):
+    def make(half, q):
+        rows = []
+        for r in range(4 * q, 4 * q + 4):
+            value = jnp.zeros((8, 128), F32)
+            for b in range(8):
                 x = flat[pl.ds(8 * PITCH * half + 8 * b + r, 8, stride=PITCH), :]
-                strip[half][r] = jnp.where(group == b, turn(x, 6 + 16 * b), strip[half][r])
-    for target, shift in zip((outer_ref, inner_ref), shifts):
-        for q in range(2):
-            for half in range(2):
-                value = jnp.zeros((8, 128), F32)
-                for s in range(4):
-                    value = jnp.where(part == s, turn(strip[half][4 * q + s], shift[s]), value)
-                target[2 * q + half] = value
-    for half in range(2):
-        for r in range(8):
-            strip_ref[r, half] = strip[half][r]
+                value = jnp.where(group == b, turn(x, 6 + 16 * b), value)
+            rows.append(value)
+        return rows
+
+    order = [(half, q) for half in range(2) for q in range(2)]
+    ahead = make(*order[0])
+    for i, (half, q) in enumerate(order):
+        strip = ahead
+        if i + 1 < len(order):
+            ahead = make(*order[i + 1])
+        for target, shift in zip((outer_ref, inner_ref), shifts):
+            value = jnp.zeros((8, 128), F32)
+            for s in range(4):
+                value = jnp.where(part == s, turn(strip[s], shift[s]), value)
+            target[2 * q + half] = value
+        for s in range(4):
+            strip_ref[4 * q + s, half] = strip[s]
     for fetch in fetches[2:]:
         fetch.wait()
 

time: 12.7 us -> 12.7 us (level)
  no operation moved by 1% of the time
where the time goes in v12:
time: 12.7 us; the launch traced here: 12.6 us
  Pallas kernels  7.72 us (61%)
  starting transfers between devices  3.54 us (28%)
  waiting for transfers between devices  1.26 us (10%)
    pallas_call x2, Pallas kernels, border_pass(): pl.pallas_call(functools.partial(border_kernel, size, last), out_shape=ja...  2.79 us
    ppermute x1, starting transfers between devices, shards(): lax.ppermute(outer, 'lon', [(i, (i + 1 if i % 2 else i - 1) % lon) for i...  1.95 us
    pallas_call x1, Pallas kernels, strip_pass(): pl.pallas_call(strip_kernel, out_shape=[block((16, ROWS - 8, 128), F32),...  1.77 us
    pallas_call x1, Pallas kernels, main_pass(): pl.pallas_call(functools.partial(main_kernel, size), out_shape=[*[block((...  1.64 us
    ppermute x1, starting transfers between devices, shards(): first = lax.ppermute(first, ('lon', 'lat'), pairs(0))  1.58 us
    pallas_call x1, Pallas kernels, prepare(): pl.pallas_call(prepare_kernel, out_shape=[block((16, PITCH, 128), F32), b...  1.43 us
    ppermute x1, waiting for transfers between devices, shards(): lax.ppermute(outer, 'lon', [(i, (i + 1 if i % 2 else i - 1) % lon) for i...  0.57 us
    ppermute x1, waiting for transfers between devices, shards(): first = lax.ppermute(first, ('lon', 'lat'), pairs(0))  0.51 us
  transfers between devices with their start and end apart: 4, of which 3 were waited for; matrix products, arithmetic and copies ran while one was open for 0% of the time, Pallas kernels for 38%

profile of v12, /device:TPU:16, one launch (start us, length us, event | category | flops | bytes accessed | tf_op | source)
XLA Modules:
  0.0 12.6 jit_solution(3378263339458857362)
XLA Ops:
  0.0 0.0 copy-start
  0.0 0.0 copy-start.1
  0.0 0.0 copy-start.2
  0.0 0.0 copy-start.3
  0.0 1.4 %rows_edges.1 = (f32[16,72,128]{2,1,0:T(8,128)S(1)}, f32[8,2,8,128]{3,2,1,0:T(8,128)S(1)}, f32[4,8,128]{2,1,0:T(8,128)S(1)}, f32[4,8,128]{2,1,0:T(8,128)S(1)}, f...) custom-call(f32[16,64,128]{2,1,0:T(8,128)} %state_ref.1, f32[1,16]{1,0:T(1,128)} %bitcast.3, ...), custom_call_target="tpu_custom_call" | custom-call | flops 400000 | bytes 1200000 | tf_op jit(solution)/shard_map/rows_edges/pallas_call | solution.py:142
  1.5 2.0 %collective-permute-start = (f32[4,8,128]{2,1,0:T(8,128)S(1)}, f32[4,8,128]{2,1,0:T(8,128)S(1)}, u32[]{:S(2)}, u32[]{:S(2)}) collective-permute-start(f32[4,8,128]{2,1,0:T(8,128)S(1)} %get-tuple-element.37), channel_id=1, source_target_pairs={{0,28},{4,8},{8,4},{12,16},{16,12},{20,24},{24,20},{28,0},{1,29},{... | collective-permute-start | bytes 49160 | tf_op jit(solution)/shard_map/ppermute | solution.py:652
  3.4 0.0 collective-permute-start.1
  3.4 0.0 copy-done
  3.4 0.0 copy-done.1
  3.4 0.0 copy-done.2
  3.4 0.0 copy-done.3
  3.4 1.6 %main_pass.1 = (f32[64,2,8,128]{3,2,1,0:T(8,128)S(1)}, f32[64,2,8,128]{3,2,1,0:T(8,128)S(1)}, f32[6,8,128]{2,1,0:T(8,128)S(1)}, f32[8,128]{1,0:T(8,128)S(1)}, bf...) custom-call(f32[16,72,128]{2,1,0:T(8,128)S(1)} %get-tuple-element.32, ...), custom_call_target="tpu_custom_call" | custom-call | flops 150000000 | bytes 1500000 | tf_op jit(solution)/shard_map/main_pass/pallas_call | solution.py:334
  5.1 0.6 %collective-permute-done.outer_ref = f32[4,8,128]{2,1,0:T(8,128)S(1)} collective-permute-done((f32[4,8,128]{2,1,0:T(8,128)S(1)}, f32[4,8,128]{2,1,0:T(8,128)S(1)}, u32[]{:S(2)}, u32[]{:S(2)}) %collective-permute-start) | collective-permute-done | bytes 16416 | tf_op jit(solution)/shard_map/ppermute | solution.py:652
  5.7 0.0 collective-permute-done.1.inner_ref
  5.7 0.1 add_corners.1
  5.8 1.6 %collective-permute-start.2 = (f32[7,8,128]{2,1,0:T(8,128)S(1)}, f32[7,8,128]{2,1,0:T(8,128)S(1)}, u32[]{:S(2)}, u32[]{:S(2)}) collective-permute-start(f32[7,8,128]{2,1,0:T(8,128)S(1)} %get-tuple-element.40), channel_id=1, source_target_pairs={{0,1},{1,0},{2,3},{3,2},{4,5},{5,4},{6,7},{7,6},{8,9},{9,8},{10,11... | collective-permute-start | bytes 86024 | tf_op jit(solution)/shard_map/ppermute | solution.py:668
  7.3 0.0 collective-permute-start.3
  7.3 1.8 %strip_pass.1 = (f32[16,56,128]{2,1,0:T(8,128)S(1)}, f32[16,8,128]{2,1,0:T(8,128)S(1)}, f32[16,8,128]{2,1,0:T(8,128)S(1)}, f32[6,2,8,128]{3,2,1,0:T(8,128)S(1)},...) custom-call(f32[64,2,8,128]{3,2,1,0:T(8,128)S(1)} %get-tuple-element.36.rows_ref.refs_0_, ...), custom_call_target="tpu_custom_call" | custom-call | flops 150000000 | bytes 2000000 | tf_op jit(solution)/shard_map/strip_pass/pallas_call | solution.py:470
  9.1 0.5 %collective-permute-done.2.refs_2_ = f32[7,8,128]{2,1,0:T(8,128)S(1)} collective-permute-done((f32[7,8,128]{2,1,0:T(8,128)S(1)}, f32[7,8,128]{2,1,0:T(8,128)S(1)}, u32[]{:S(2)}, u32[]{:S(2)}) %collective-permute-start.2) | collective-permute-done | bytes 28704 | tf_op jit(solution)/shard_map/ppermute | solution.py:668
  9.6 1.4 %north_strip.1.refs_14_ = f32[16,64,128]{2,1,0:T(8,128)} custom-call(f32[64,2,8,128]{3,2,1,0:T(8,128)S(1)} %get-tuple-element.36.rows_ref.refs_0_, s32[64,128]{1,0:T(8,128)S(1)} %copy-done, f32[7,8,128]{2,1,0:T(8,128)S(1)} %collective-permute-done.2.refs_2_, f32[6,2,8,128]{3,2,1,0:T(8,128)S(1)} %get-tuple-element.49.refs_3_.refs_4_, ...), custom_call_target="tpu_custom_call" | custom-call | flops 60000000 | bytes 1000000 | tf_op jit(solution)/shard_map/north_strip/pallas_call | solution.py:628
  11.0 0.2 %collective-permute-done.3.refs_3_ = f32[7,8,128]{2,1,0:T(8,128)S(1)} collective-permute-done((f32[7,8,128]{2,1,0:T(8,128)S(1)}, f32[7,8,128]{2,1,0:T(8,128)S(1)}, u32[]{:S(2)}, u32[]{:S(2)}) %collective-permute-start.3) | collective-permute-done | bytes 28704 | tf_op jit(solution)/shard_map/ppermute | solution.py:669
  11.2 1.4 %border_pass.1 = f32[16,64,128]{2,1,0:T(8,128)} custom-call(f32[64,2,8,128]{3,2,1,0:T(8,128)S(1)} %get-tuple-element.36.rows_ref.refs_0_, s32[64,128]{1,0:T(8,128)S(1)} %copy-done, f32[7,8,128]{2,1,0:T(8,128)S(1)} %collective-permute-done.2.refs_2_, f32[7,8,128]{2,1,0:T(8,128)S(1)} %collective-permute-done.3.refs_3_, ...), custom_call_target="tpu_custom_call", output_to_operand_aliasing={{}: (14, {})} | custom-call | flops 60000000 | bytes 1000000 | tf_op jit(solution)/shard_map/border_pass/pallas_call | solution.py:628
Async XLA Ops:
  0.0 3.4 %copy-start = (s32[64,128]{1,0:T(8,128)S(1)}, s32[64,128]{1,0:T(8,128)}, u32[]{:S(2)}) copy-start(s32[64,128]{1,0:T(8,128)} %refs_1_.3) | copy-start | bytes 98308
  0.0 3.4 %copy-start.1 = (bf16[3,3,16,16]{3,2,1,0:T(8,128)(2,1)S(1)}, bf16[3,3,16,16]{3,2,1,0:T(8,128)(2,1)}, u32[]{:S(2)}) copy-start(bf16[3,3,16,16]{3,2,1,0:T(8,128)(2,1)} %k_one_ref.1) | copy-start | bytes 13828
  0.0 3.4 %copy-start.2 = (bf16[3,3,16,16]{3,2,1,0:T(8,128)(2,1)S(1)}, bf16[3,3,16,16]{3,2,1,0:T(8,128)(2,1)}, u32[]{:S(2)}) copy-start(bf16[3,3,16,16]{3,2,1,0:T(8,128)(2,1)} %k_two_ref.1) | copy-start | bytes 13828
  0.0 3.4 %copy-start.3 = (bf16[3,3,8,16]{3,2,1,0:T(8,128)(2,1)S(1)}, bf16[3,3,8,16]{3,2,1,0:T(8,128)(2,1)}, u32[]{:S(2)}) copy-start(bf16[3,3,8,16]{3,2,1,0:T(8,128)(2,1)} %k_three_ref.1) | copy-start | bytes 6916
  1.5 4.2 %collective-permute-start = (f32[4,8,128]{2,1,0:T(8,128)S(1)}, f32[4,8,128]{2,1,0:T(8,128)S(1)}, u32[]{:S(2)}, u32[]{:S(2)}) collective-permute-start(f32[4,8,128]{2,1,0:T(8,128)S(1)} %get-tuple-element.37), channel_id=1, source_target_pairs={{0,28},{4,8},{8,4},{12,16},{16,12},{20,24},{24,20},{28,0},{1,29},{... | collective-permute-start | bytes 49160 | tf_op jit(solution)/shard_map/ppermute | solution.py:652
  3.4 2.3 %collective-permute-start.1 = (f32[4,8,128]{2,1,0:T(8,128)S(1)}, f32[4,8,128]{2,1,0:T(8,128)S(1)}, u32[]{:S(2)}, u32[]{:S(2)}) collective-permute-start(f32[4,8,128]{2,1,0:T(8,128)S(1)} %get-tuple-element.38), channel_id=1, source_target_pairs={{0,4},{4,0},{8,12},{12,8},{16,20},{20,16},{24,28},{28,24},{1,5},{5... | collective-permute-start | bytes 49160 | tf_op jit(solution)/shard_map/ppermute | solution.py:651
  5.8 3.9 %collective-permute-start.2 = (f32[7,8,128]{2,1,0:T(8,128)S(1)}, f32[7,8,128]{2,1,0:T(8,128)S(1)}, u32[]{:S(2)}, u32[]{:S(2)}) collective-permute-start(f32[7,8,128]{2,1,0:T(8,128)S(1)} %get-tuple-element.40), channel_id=1, source_target_pairs={{0,1},{1,0},{2,3},{3,2},{4,5},{5,4},{6,7},{7,6},{8,9},{9,8},{10,11... | collective-permute-start | bytes 86024 | tf_op jit(solution)/shard_map/ppermute | solution.py:668
  7.3 3.9 %collective-permute-start.3 = (f32[7,8,128]{2,1,0:T(8,128)S(1)}, f32[7,8,128]{2,1,0:T(8,128)S(1)}, u32[]{:S(2)}, u32[]{:S(2)}) collective-permute-start(f32[7,8,128]{2,1,0:T(8,128)S(1)} %get-tuple-element.41), channel_id=1, source_target_pairs={{1,2},{2,1},{0,4},{3,31},{5,6},{6,5},{4,0},{7,27},{9,10},{10,9},{8... | collective-permute-start | bytes 86024 | tf_op jit(solution)/shard_map/ppermute | solution.py:669

commit v13 on v11

--- a/solution.py
+++ b/solution.py
@@ -88,11 +88,8 @@
     state_ref, b_one_ref, b_two_ref, b_three_ref,
     cells_ref, strip_ref, outer_ref, inner_ref, h_one_ref, h_two_ref, h_three_ref, sems,
 ):
-    fetches = []
-    for half in range(2):
-        span = pl.ds(8 * half, 8)
-        target = cells_ref.at[span, pl.ds(0, ROWS), :]
-        fetches.append(pltpu.make_async_copy(state_ref.at[span], target, sems.at[half]))
+    image = cells_ref.at[:, pl.ds(0, ROWS), :]
+    fetches = [pltpu.make_async_copy(state_ref, image, sems.at[0])]
     biases = ((b_one_ref, h_one_ref), (b_two_ref, h_two_ref), (b_three_ref, h_three_ref))
     for source, target in biases:
         fetches.append(pltpu.make_async_copy(source, target, sems.at[len(fetches)]))
@@ -107,8 +104,7 @@
         [jnp.where(even, (4 * s - a) % 128, (4 * s - b) % 128) for s in range(4)]
         for a, b in ((6, 3), (3, 6))
     ]
-    for fetch in fetches[0:2]:
-        fetch.wait()
+    fetches[0].wait()
     strip = [[jnp.zeros((8, 128), F32)] * 8 for half in range(2)]
     for b in range(8):
         for half in range(2):
@@ -125,7 +121,7 @@
     for half in range(2):
         for r in range(8):
             strip_ref[r, half] = strip[half][r]
-    for fetch in fetches[2:]:
+    for fetch in fetches[1:]:
         fetch.wait()
 
 
@@ -143,7 +139,7 @@
         ],
         in_specs=[HBM] * 4,
         out_specs=[VMEM] * 7,
-        scratch_shapes=[pltpu.SemaphoreType.DMA((5,))],
+        scratch_shapes=[pltpu.SemaphoreType.DMA((4,))],
         compiler_params=pltpu.CompilerParams(vmem_limit_bytes=LIMIT),
         cost_estimate=pl.CostEstimate(flops=400000, bytes_accessed=1200000, transcendentals=0),
         name="rows_edges",

time: 12.7 us -> 12.7 us (level)
  no operation moved by 1% of the time
where the time goes in v13:
time: 12.7 us; the launch traced here: 12.6 us
  Pallas kernels  7.69 us (61%)
  starting transfers between devices  3.54 us (28%)
  waiting for transfers between devices  1.26 us (10%)
    pallas_call x2, Pallas kernels, border_pass(): pl.pallas_call(functools.partial(border_kernel, size, last), out_shape=ja...  2.79 us
    ppermute x1, starting transfers between devices, shards(): lax.ppermute(outer, 'lon', [(i, (i + 1 if i % 2 else i - 1) % lon) for i...  1.95 us
    pallas_call x1, Pallas kernels, strip_pass(): pl.pallas_call(strip_kernel, out_shape=[block((16, ROWS - 8, 128), F32),...  1.77 us
    pallas_call x1, Pallas kernels, main_pass(): pl.pallas_call(functools.partial(main_kernel, size), out_shape=[*[block((...  1.64 us
    ppermute x1, starting transfers between devices, shards(): first = lax.ppermute(first, ('lon', 'lat'), pairs(0))  1.58 us
    pallas_call x1, Pallas kernels, prepare(): pl.pallas_call(prepare_kernel, out_shape=[block((16, PITCH, 128), F32), b...  1.4 us
    ppermute x1, waiting for transfers between devices, shards(): lax.ppermute(outer, 'lon', [(i, (i + 1 if i % 2 else i - 1) % lon) for i...  0.57 us
    ppermute x1, waiting for transfers between devices, shards(): first = lax.ppermute(first, ('lon', 'lat'), pairs(0))  0.51 us
  transfers between devices with their start and end apart: 4, of which 3 were waited for; matrix products, arithmetic and copies ran while one was open for 0% of the time, Pallas kernels for 38%

profile of v13, /device:TPU:16, one launch (start us, length us, event | category | flops | bytes accessed | tf_op | source)
XLA Modules:
  0.0 12.6 jit_solution(18058896006228461542)
XLA Ops:
  0.0 0.0 copy-start
  0.0 0.0 copy-start.1
  0.0 0.0 copy-start.2
  0.0 0.0 copy-start.3
  0.0 1.4 %rows_edges.1 = (f32[16,72,128]{2,1,0:T(8,128)S(1)}, f32[8,2,8,128]{3,2,1,0:T(8,128)S(1)}, f32[4,8,128]{2,1,0:T(8,128)S(1)}, f32[4,8,128]{2,1,0:T(8,128)S(1)}, f...) custom-call(f32[16,64,128]{2,1,0:T(8,128)} %state_ref.1, f32[1,16]{1,0:T(1,128)} %bitcast.3, ...), custom_call_target="tpu_custom_call" | custom-call | flops 400000 | bytes 1200000 | tf_op jit(solution)/shard_map/rows_edges/pallas_call | solution.py:131
  1.4 2.0 %collective-permute-start = (f32[4,8,128]{2,1,0:T(8,128)S(1)}, f32[4,8,128]{2,1,0:T(8,128)S(1)}, u32[]{:S(2)}, u32[]{:S(2)}) collective-permute-start(f32[4,8,128]{2,1,0:T(8,128)S(1)} %get-tuple-element.37), channel_id=1, source_target_pairs={{0,28},{4,8},{8,4},{12,16},{16,12},{20,24},{24,20},{28,0},{1,29},{... | collective-permute-start | bytes 49160 | tf_op jit(solution)/shard_map/ppermute | solution.py:641
  3.4 0.0 collective-permute-start.1
  3.4 0.0 copy-done
  3.4 0.0 copy-done.1
  3.4 0.0 copy-done.2
  3.4 0.0 copy-done.3
  3.4 1.6 %main_pass.1 = (f32[64,2,8,128]{3,2,1,0:T(8,128)S(1)}, f32[64,2,8,128]{3,2,1,0:T(8,128)S(1)}, f32[6,8,128]{2,1,0:T(8,128)S(1)}, f32[8,128]{1,0:T(8,128)S(1)}, bf...) custom-call(f32[16,72,128]{2,1,0:T(8,128)S(1)} %get-tuple-element.32, ...), custom_call_target="tpu_custom_call" | custom-call | flops 150000000 | bytes 1500000 | tf_op jit(solution)/shard_map/main_pass/pallas_call | solution.py:323
  5.1 0.6 %collective-permute-done.outer_ref = f32[4,8,128]{2,1,0:T(8,128)S(1)} collective-permute-done((f32[4,8,128]{2,1,0:T(8,128)S(1)}, f32[4,8,128]{2,1,0:T(8,128)S(1)}, u32[]{:S(2)}, u32[]{:S(2)}) %collective-permute-start) | collective-permute-done | bytes 16416 | tf_op jit(solution)/shard_map/ppermute | solution.py:641
  5.6 0.0 collective-permute-done.1.inner_ref
  5.6 0.1 add_corners.1
  5.7 1.6 %collective-permute-start.2 = (f32[7,8,128]{2,1,0:T(8,128)S(1)}, f32[7,8,128]{2,1,0:T(8,128)S(1)}, u32[]{:S(2)}, u32[]{:S(2)}) collective-permute-start(f32[7,8,128]{2,1,0:T(8,128)S(1)} %get-tuple-element.40), channel_id=1, source_target_pairs={{0,1},{1,0},{2,3},{3,2},{4,5},{5,4},{6,7},{7,6},{8,9},{9,8},{10,11... | collective-permute-start | bytes 86024 | tf_op jit(solution)/shard_map/ppermute | solution.py:657
  7.3 0.0 collective-permute-start.3
  7.3 1.8 %strip_pass.1 = (f32[16,56,128]{2,1,0:T(8,128)S(1)}, f32[16,8,128]{2,1,0:T(8,128)S(1)}, f32[16,8,128]{2,1,0:T(8,128)S(1)}, f32[6,2,8,128]{3,2,1,0:T(8,128)S(1)},...) custom-call(f32[64,2,8,128]{3,2,1,0:T(8,128)S(1)} %get-tuple-element.36.rows_ref.refs_0_, ...), custom_call_target="tpu_custom_call" | custom-call | flops 150000000 | bytes 2000000 | tf_op jit(solution)/shard_map/strip_pass/pallas_call | solution.py:459
  9.1 0.5 %collective-permute-done.2.refs_2_ = f32[7,8,128]{2,1,0:T(8,128)S(1)} collective-permute-done((f32[7,8,128]{2,1,0:T(8,128)S(1)}, f32[7,8,128]{2,1,0:T(8,128)S(1)}, u32[]{:S(2)}, u32[]{:S(2)}) %collective-permute-start.2) | collective-permute-done | bytes 28704 | tf_op jit(solution)/shard_map/ppermute | solution.py:657
  9.6 1.4 %north_strip.1.refs_14_ = f32[16,64,128]{2,1,0:T(8,128)} custom-call(f32[64,2,8,128]{3,2,1,0:T(8,128)S(1)} %get-tuple-element.36.rows_ref.refs_0_, s32[64,128]{1,0:T(8,128)S(1)} %copy-done, f32[7,8,128]{2,1,0:T(8,128)S(1)} %collective-permute-done.2.refs_2_, f32[6,2,8,128]{3,2,1,0:T(8,128)S(1)} %get-tuple-element.49.refs_3_.refs_4_, ...), custom_call_target="tpu_custom_call" | custom-call | flops 60000000 | bytes 1000000 | tf_op jit(solution)/shard_map/north_strip/pallas_call | solution.py:617
  11.0 0.2 %collective-permute-done.3.refs_3_ = f32[7,8,128]{2,1,0:T(8,128)S(1)} collective-permute-done((f32[7,8,128]{2,1,0:T(8,128)S(1)}, f32[7,8,128]{2,1,0:T(8,128)S(1)}, u32[]{:S(2)}, u32[]{:S(2)}) %collective-permute-start.3) | collective-permute-done | bytes 28704 | tf_op jit(solution)/shard_map/ppermute | solution.py:658
  11.2 1.4 %border_pass.1 = f32[16,64,128]{2,1,0:T(8,128)} custom-call(f32[64,2,8,128]{3,2,1,0:T(8,128)S(1)} %get-tuple-element.36.rows_ref.refs_0_, s32[64,128]{1,0:T(8,128)S(1)} %copy-done, f32[7,8,128]{2,1,0:T(8,128)S(1)} %collective-permute-done.2.refs_2_, f32[7,8,128]{2,1,0:T(8,128)S(1)} %collective-permute-done.3.refs_3_, ...), custom_call_target="tpu_custom_call", output_to_operand_aliasing={{}: (14, {})} | custom-call | flops 60000000 | bytes 1000000 | tf_op jit(solution)/shard_map/border_pass/pallas_call | solution.py:617
Async XLA Ops:
  0.0 3.4 %copy-start = (s32[64,128]{1,0:T(8,128)S(1)}, s32[64,128]{1,0:T(8,128)}, u32[]{:S(2)}) copy-start(s32[64,128]{1,0:T(8,128)} %refs_1_.3) | copy-start | bytes 98308
  0.0 3.4 %copy-start.1 = (bf16[3,3,16,16]{3,2,1,0:T(8,128)(2,1)S(1)}, bf16[3,3,16,16]{3,2,1,0:T(8,128)(2,1)}, u32[]{:S(2)}) copy-start(bf16[3,3,16,16]{3,2,1,0:T(8,128)(2,1)} %k_one_ref.1) | copy-start | bytes 13828
  0.0 3.4 %copy-start.2 = (bf16[3,3,16,16]{3,2,1,0:T(8,128)(2,1)S(1)}, bf16[3,3,16,16]{3,2,1,0:T(8,128)(2,1)}, u32[]{:S(2)}) copy-start(bf16[3,3,16,16]{3,2,1,0:T(8,128)(2,1)} %k_two_ref.1) | copy-start | bytes 13828
  0.0 3.4 %copy-start.3 = (bf16[3,3,8,16]{3,2,1,0:T(8,128)(2,1)S(1)}, bf16[3,3,8,16]{3,2,1,0:T(8,128)(2,1)}, u32[]{:S(2)}) copy-start(bf16[3,3,8,16]{3,2,1,0:T(8,128)(2,1)} %k_three_ref.1) | copy-start | bytes 6916
  1.4 4.2 %collective-permute-start = (f32[4,8,128]{2,1,0:T(8,128)S(1)}, f32[4,8,128]{2,1,0:T(8,128)S(1)}, u32[]{:S(2)}, u32[]{:S(2)}) collective-permute-start(f32[4,8,128]{2,1,0:T(8,128)S(1)} %get-tuple-element.37), channel_id=1, source_target_pairs={{0,28},{4,8},{8,4},{12,16},{16,12},{20,24},{24,20},{28,0},{1,29},{... | collective-permute-start | bytes 49160 | tf_op jit(solution)/shard_map/ppermute | solution.py:641
  3.4 2.3 %collective-permute-start.1 = (f32[4,8,128]{2,1,0:T(8,128)S(1)}, f32[4,8,128]{2,1,0:T(8,128)S(1)}, u32[]{:S(2)}, u32[]{:S(2)}) collective-permute-start(f32[4,8,128]{2,1,0:T(8,128)S(1)} %get-tuple-element.38), channel_id=1, source_target_pairs={{0,4},{4,0},{8,12},{12,8},{16,20},{20,16},{24,28},{28,24},{1,5},{5... | collective-permute-start | bytes 49160 | tf_op jit(solution)/shard_map/ppermute | solution.py:640
  5.7 3.9 %collective-permute-start.2 = (f32[7,8,128]{2,1,0:T(8,128)S(1)}, f32[7,8,128]{2,1,0:T(8,128)S(1)}, u32[]{:S(2)}, u32[]{:S(2)}) collective-permute-start(f32[7,8,128]{2,1,0:T(8,128)S(1)} %get-tuple-element.40), channel_id=1, source_target_pairs={{0,1},{1,0},{2,3},{3,2},{4,5},{5,4},{6,7},{7,6},{8,9},{9,8},{10,11... | collective-permute-start | bytes 86024 | tf_op jit(solution)/shard_map/ppermute | solution.py:657
  7.3 3.9 %collective-permute-start.3 = (f32[7,8,128]{2,1,0:T(8,128)S(1)}, f32[7,8,128]{2,1,0:T(8,128)S(1)}, u32[]{:S(2)}, u32[]{:S(2)}) collective-permute-start(f32[7,8,128]{2,1,0:T(8,128)S(1)} %get-tuple-element.41), channel_id=1, source_target_pairs={{1,2},{2,1},{0,4},{3,31},{5,6},{6,5},{4,0},{7,27},{9,10},{10,9},{8... | collective-permute-start | bytes 86024 | tf_op jit(solution)/shard_map/ppermute | solution.py:658
